TPU v7x, 256 devices: a whole 4x4x8 slice. The times are simulated.
256 devices in a mesh: feed: 64 (over y, x, z_hi, core), band: 4 (over z_lo).
Axes of the slice: x: 4, y: 4, z: 8 (z_hi: 2, z_lo: 4; z = z_hi * 4 + z_lo), core: 2. Of those that a mesh axis runs over, the one named last changes fastest.
Arguments:
- voltages: bfloat16 [2, 2048, 114688], P(None, ('band', 'feed')), may hold values from -6 to 6
- filter_taps: float32 [4, 16384], replicated, may hold values from -1 to 1
- feed_gains: bfloat16 [2, 64, 2048, 256], P(None, 'feed', 'band'), may hold values from 0.5 to 1.5
- beam_weights: bfloat16 [2, 64, 1024, 2048], P(None, 'feed', None, 'band'), may hold values from -0.125 to 0.125
- beam_mask: int32 [1024, 64], replicated, may hold values 0 or 1
- band_order: int32 [64], replicated, may hold values from 0 to 63, each once
Outputs:
- visibility: bfloat16 [2, 64, 2048, 2048], P(None, 'feed', 'band')
- beam_out: bfloat16 [64, 1024, 2, 4, 256], P('feed', 'band')
Inputs may be any that keep to these rules, and one draw needn't show every extreme that they name: `band_order`: each of the 64 channel blocks goes to exactly one slot.
All inputs are finite; a program needn't handle non-finite values.
Results may differ from a plain program's by a relative error of at most 0.015.
Values may be sent and summed in bfloat16 or wider, within the bound.
No kernel may reach another device: no remote copies, remote signals or barrier semaphores. Data moves between devices by JAX's collectives and lax.ppermute only.
A program may use at most 128 MiB of HBM per device.

v0:
```python
import math

import jax
import jax.numpy as jnp
from jax import lax
from jax.sharding import PartitionSpec as P

RADIX = 128
TILE = 32


def dft_tables(radix, length):
    index_row = jnp.arange(radix, dtype=jnp.int32)
    product = index_row[:, None] * index_row[None, :] % radix
    angles = product.astype(jnp.float32) * (2.0 * math.pi / radix)
    factor = 1.0 / math.sqrt(radix)
    table_re = (jnp.cos(angles) * factor).astype(jnp.bfloat16)
    table_im = (-jnp.sin(angles) * factor).astype(jnp.bfloat16)
    twiddle = (index_row[:, None] * index_row[None, :] % length).astype(jnp.float32) * (
        2.0 * math.pi / length
    )
    return (table_re, table_im, jnp.cos(twiddle), -jnp.sin(twiddle))


def filter_frames(voltages, filter_taps):
    tap_count, length = filter_taps.shape
    frames = voltages.shape[2] // length
    spectra_count = frames - tap_count + 1
    framed = voltages.reshape(2, voltages.shape[1], frames, length)
    summed = filter_taps[0] * framed[:, :, 0:spectra_count].astype(jnp.float32)
    for tap_index in range(1, tap_count):
        summed = summed + filter_taps[tap_index] * framed[
            :, :, tap_index : tap_index + spectra_count
        ].astype(jnp.float32)
    return summed.astype(jnp.bfloat16)


def section_first(dft_table, values_in):
    return jnp.einsum("kn,...nm->...km", dft_table, values_in, preferred_element_type=jnp.float32)


def section_second(dft_table, values_in):
    return jnp.einsum("jm,...km->...jk", dft_table, values_in, preferred_element_type=jnp.float32)


def channelize(voltages, filter_taps):
    filtered = filter_frames(voltages, filter_taps)
    length = filter_taps.shape[1]
    feed_count = filtered.shape[1]
    spectra_count = filtered.shape[2]
    split_frame = filtered.reshape(2, feed_count, spectra_count, RADIX, RADIX)
    table_re, table_im, twid_re, twid_im = dft_tables(RADIX, length)
    first_re = section_first(table_re, split_frame[0]) - section_first(table_im, split_frame[1])
    first_im = section_first(table_re, split_frame[1]) + section_first(table_im, split_frame[0])
    rot_re = (first_re * twid_re - first_im * twid_im).astype(jnp.bfloat16)
    rot_im = (first_re * twid_im + first_im * twid_re).astype(jnp.bfloat16)
    out_re = section_second(table_re, rot_re) - section_second(table_im, rot_im)
    out_im = section_second(table_re, rot_im) + section_second(table_im, rot_re)
    return (
        jnp.stack([out_re, out_im])
        .astype(jnp.bfloat16)
        .reshape(2, feed_count, spectra_count, length)
    )


def pair_product(left_rows, right_rows):
    return jnp.einsum("in,jn->ij", left_rows, right_rows, preferred_element_type=jnp.float32)


def beam_product(weights, values_in):
    return jnp.einsum("bf,fn->bn", weights, values_in, preferred_element_type=jnp.float32)


def shards(voltages, filter_taps, feed_gains, beam_weights, beam_mask, band_order):
    slot_count = lax.axis_size("feed")
    band_count = lax.axis_size("band")
    band_index = lax.axis_index("band")
    spectra = channelize(voltages, filter_taps)
    local_feeds = spectra.shape[1]
    spectra_count = spectra.shape[2]
    length = spectra.shape[3]
    block_width = length // slot_count
    blocks = spectra.reshape(2, local_feeds, spectra_count, slot_count, block_width)
    blocks = jnp.take(blocks, band_order, axis=3)
    turned = lax.all_to_all(blocks, "feed", split_axis=3, concat_axis=1, tiled=True)
    own_rows = local_feeds * slot_count
    received = turned.reshape(2, own_rows, spectra_count, block_width).astype(jnp.float32)
    gain_block = feed_gains[:, 0].astype(jnp.float32)[:, :, None, :]
    calib_re = gain_block[0] * received[0] - gain_block[1] * received[1]
    calib_im = gain_block[0] * received[1] + gain_block[1] * received[0]
    calibrated = (
        jnp.stack([calib_re, calib_im])
        .astype(jnp.bfloat16)
        .reshape(2, own_rows, spectra_count * block_width)
    )
    average = 1.0 / (spectra_count * block_width)
    beam_rows = beam_weights.shape[2] // band_count
    portion = lax.all_gather(calibrated, "band", axis=1, tiled=True)
    col_re = pair_product(calibrated[0], portion[0]) + pair_product(calibrated[1], portion[1])
    col_im = pair_product(calibrated[1], portion[0]) - pair_product(calibrated[0], portion[1])
    vis_total = jnp.stack([col_re, col_im])
    own_tiles = own_rows // TILE
    mask_cols = lax.dynamic_slice_in_dim(beam_mask, band_index * own_tiles, own_tiles, 1)
    mask_wide = jnp.repeat(mask_cols, TILE, axis=1).astype(jnp.bfloat16)
    weights = beam_weights[:, 0] * mask_wide[None]
    part_re = beam_product(weights[0], calibrated[0]) - beam_product(weights[1], calibrated[1])
    part_im = beam_product(weights[0], calibrated[1]) + beam_product(weights[1], calibrated[0])
    beam_total = lax.psum_scatter(
        jnp.stack([part_re, part_im], axis=1).astype(jnp.bfloat16),
        "band",
        scatter_dimension=0,
        tiled=True,
    ).astype(jnp.float32)
    visibility = (vis_total * average).astype(jnp.bfloat16)[:, None]
    beam_out = beam_total.reshape(1, beam_rows, 2, spectra_count, block_width).astype(jnp.bfloat16)
    return (visibility, beam_out)


def solution(mesh):
    return jax.shard_map(
        shards,
        mesh=mesh,
        in_specs=(
            P(None, ("band", "feed"), None),
            P(),
            P(None, "feed", "band", None),
            P(None, "feed", None, "band"),
            P(),
            P(),
        ),
        out_specs=(P(None, "feed", "band", None), P("feed", "band", None, None, None)),
        check_vma=False,
    )
```

profile of v0, /device:TPU:2, one launch (start us, length us, event | category | flops | bytes accessed | tf_op | source)
XLA Modules:
  0.0 379.0 jit_solution(11275660440524392993)
XLA Ops:
  10.6 4.6 %add_convert_fusion.1 = bf16[2,8,4,16384]{3,1,2,0:T(8,128)(2,1)S(1)} fusion(bf16[2,8,7,16384]{3,1,2,0:T(8,128)(2,1)} %bitcast.145, f32[16384]{0:T(1024)S(1)} %bitcast.159, f32[16384]{0:T(1024)S(1)} %bitcast.160, f32[16384]{0:T(1024)S(1)} %bitcast.158, f32[16384]{0:T(1024)S(1)} %bitcast.157), kind=kLoop, calls=%fused_computation.11 | loop fusion | flops 12582912 | bytes 10747904 | tf_op jit(solution)/shard_map/convert_element_type | solution.py:35
  16.3 2.0 fusion.19
  18.4 2.0 convolution_subtract_fusion
  20.6 3.3 fusion.10
  25.3 1.7 fusion.16
  26.9 2.3 copy.61
  29.2 2.2 stack.41
  31.4 2.8 copy.63
  34.2 1.7 fusion.15
  38.9 2.1 gather_fusion
  41.0 3.2 select_bitcast_fusion
  44.2 14.8 %all-to-all-start = ((bf16[2,8,4,64,256]{4,1,2,0,3:T(8,128)(2,1)}), bf16[2,8,4,64,256]{4,1,2,0,3:T(8,128)(2,1)S(1)}, u32[]{:S(2)}, u32[]{:S(2)}) async-start(bf16[2,8,4,64,256]{4,1,2,0,3:T(8,128)(2,1)} %select_bitcast_fusion), calls=%async_computation | async-start | bytes 4194304 | tf_op jit(solution)/shard_map/all_to_all | solution.py:85
  63.6 2.4 slice_bitcast_fusion.19
  67.5 30.6 %all-to-all-done = bf16[2,8,4,64,256]{4,1,2,0,3:T(8,128)(2,1)S(1)} async-done(((bf16[2,8,4,64,256]{4,1,2,0,3:T(8,128)(2,1)}), bf16[2,8,4,64,256]{4,1,2,0,3:T(8,128)(2,1)S(1)}, u32[]{:S(2)}, u32[]{:S(2)}) %all-to-all-start) | async-done | bytes 2097184 | tf_op jit(solution)/shard_map/all_to_all | solution.py:85
  101.6 2.7 fusion.17
  108.2 2.4 pad_maximum_fusion
  112.4 89.6 %reduce-scatter.2.cloned.1.call-done = bf16[256,2,1024]{2,0,1:T(8,128)(2,1)} async-done(((bf16[1024,2,1024]{2,0,1:T(8,128)(2,1)}), bf16[256,2,1024]{2,0,1:T(8,128)(2,1)}) %reduce-scatter.2.cloned.1.call-update) | async-done | bytes 1048592 | tf_op jit(solution)/shard_map/reduce_scatter | solution.py:108
  202.0 1.9 convert_element_type.143
  205.2 152.6 %all-gather.2.cloned.1.call-done = bf16[2,2048,1024]{1,2,0:T(8,128)(2,1)} async-done(((bf16[2,512,1024]{1,2,0:T(8,128)(2,1)}), bf16[2,2048,1024]{1,2,0:T(8,128)(2,1)}) %all-gather.2.cloned.1.call-update) | async-done | bytes 8388624 | tf_op jit(solution)/shard_map/all_gather | solution.py:98
  357.7 4.7 %fusion.1 = f32[512,2048]{1,0:T(8,128)S(1)} fusion(bf16[512,1024]{0,1:T(8,128)(2,1)S(1)} %bitcast.149, bf16[2,2048,1024]{1,2,0:T(8,128)(2,1)} %all-gather.2.cloned.1.call-done), kind=kOutput, calls=%fused_computation.12 | convolution fusion | flops 2147483648 | bytes 9437184 | tf_op jit(solution)/shard_map/in,jn->ij/dot_general | solution.py:67
  362.5 2.4 fusion.2
  364.8 2.4 subtract_bitcast_fusion
  367.2 2.4 add_bitcast_fusion
  369.6 2.5 fusion
  (50 shorter events, 25.7 us)
Async XLA Ops:
  37.5 1.2 copy-start.2
  44.2 14.8 %copy-start.6 = (bf16[2,1,512,256]{3,2,1,0:T(8,128)(2,1)S(1)}, bf16[2,1,512,256]{3,2,1,0:T(8,128)(2,1)}, u32[]{:S(2)}) copy-start(bf16[2,1,512,256]{3,2,1,0:T(8,128)(2,1)} %param.8) | copy-start | bytes 1572868
  44.2 53.9 %all-to-all-start = ((bf16[2,8,4,64,256]{4,1,2,0,3:T(8,128)(2,1)}), bf16[2,8,4,64,256]{4,1,2,0,3:T(8,128)(2,1)S(1)}, u32[]{:S(2)}, u32[]{:S(2)}) async-start(bf16[2,8,4,64,256]{4,1,2,0,3:T(8,128)(2,1)} %select_bitcast_fusion), calls=%async_computation | async-start | bytes 4194304 | tf_op jit(solution)/shard_map/all_to_all | solution.py:85
  59.0 143.0 %reduce-scatter.2.cloned.1.call-start = ((), (), s32[]{:S(2)}) async-start(), calls=%async_computation.3 | async-start | bytes 5242880 | tf_op jit(solution)/shard_map/reduce_scatter | solution.py:108
  63.5 2.4 copy-start.5
  98.7 1.1 copy-start.3
  98.7 1.2 copy-start.4
  101.6 2.7 copy-start.1
  110.6 247.2 %all-gather.2.cloned.1.call-start = ((), (), s32[]{:S(2)}) async-start(), calls=%async_computation.2 | async-start | bytes 10485760 | tf_op jit(solution)/shard_map/all_gather | solution.py:98
  357.7 4.7 %copy-start = (bf16[2,2048,1024]{1,2,0:T(8,128)(2,1)S(1)}, bf16[2,2048,1024]{1,2,0:T(8,128)(2,1)}, u32[]{:S(2)}) copy-start(bf16[2,2048,1024]{1,2,0:T(8,128)(2,1)} %all-gather.2.cloned.1.call-done) | copy-start | bytes 25165828
Sparse Core Ops, SparseCore 0:
  110.7 91.2 reduce-scatter.1
  203.9 153.7 all-gather.1
where the time goes:
time: 380 us; the launch traced here: 379 us
  waiting for transfers between devices  273 us (72%)
  matrix products  31.1 us (8%)
  local copies, waits for them, and re-layouts  24.9 us (7%)
  other arithmetic  20.8 us (5%)
  starting transfers between devices  15.1 us (4%)
  between operations  14.3 us (4%)
    all_gather x1, waiting for transfers between devices, shards(): portion = lax.all_gather(calibrated, 'band', axis=1, tiled=True)  153 us
    reduce_scatter x1, waiting for transfers between devices, shards(): lax.psum_scatter(jnp.stack([part_re, part_im], axis=1).astype(jnp.bfloat1...  89.6 us
    all_to_all x1, waiting for transfers between devices, shards(): lax.all_to_all(blocks, 'feed', split_axis=3, concat_axis=1, tiled=True)  30.6 us
    all_to_all x1, starting transfers between devices, shards(): lax.all_to_all(blocks, 'feed', split_axis=3, concat_axis=1, tiled=True)  14.8 us
    dot_general x4, matrix products, pair_product(): jnp.einsum('in,jn->ij', left_rows, right_rows, preferred_element_type=jnp...  11.8 us
    dot_general x4, matrix products, section_first(): jnp.einsum('kn,...nm->...km', dft_table, values_in, preferred_element_typ...  8.05 us
  transfers between devices with their start and end apart: 3, of which 3 were waited for; matrix products, arithmetic and copies ran while one was open for 3% of the time, Pallas kernels for 0%

commit v1 on v0

v1 whole, which is shorter than its diff:
```python
import math

import jax
import jax.numpy as jnp
import numpy as np
from jax import lax
from jax.experimental import pallas as pl
from jax.experimental.pallas import tpu as pltpu
from jax.sharding import PartitionSpec as P

RADIX = 128
TILE = 32
SIDE = 4
BOTH = ("feed", "band")
F32 = jnp.float32
BF16 = jnp.bfloat16


def feed_at(y, x, half, core):
    return ((y * SIDE + x) * 2 + half) * 2 + core


PLANE_GROUPS = [
    [feed_at(y, x, half, core) for y in range(SIDE) for x in range(SIDE) for core in range(2)]
    for half in range(2)
]


def hop(step, senders):
    pairs = []
    for y in range(SIDE):
        for x in range(SIDE):
            for core in range(2):
                for z in range(8):
                    if z % 4 in senders:
                        to = (z + step) % 8
                        pairs.append(
                            (feed_at(y, x, z // 4, core) * 4 + z % 4, feed_at(y, x, to // 4, core) * 4 + to % 4)
                        )
    return pairs


def constants(length):
    row = np.arange(RADIX)
    angles = (row[:, None] * row[None, :] % RADIX) * (2.0 * math.pi / RADIX)
    factor = 1.0 / math.sqrt(RADIX)
    re = (np.cos(angles) * factor).astype(np.float32)
    im = (-np.sin(angles) * factor).astype(np.float32)
    first = np.block([[re, -im], [im, re]])
    second = np.stack([np.hstack([re, -im]), np.hstack([im, re])])
    second = second.reshape(2, RADIX // 2, 2, 2 * RADIX).transpose(0, 2, 1, 3).reshape(4, RADIX // 2, 2 * RADIX)
    twiddle = (row[:, None] * row[None, :] % length) * (2.0 * math.pi / length)
    tw = np.stack([np.cos(twiddle), -np.sin(twiddle)]).astype(np.float32)
    place = np.zeros((64, 64), np.float32)
    for yx in range(16):
        for core in range(2):
            for half in range(2):
                place[(yx * 2 + core) * 2 + half, (yx * 2 + half) * 2 + core] = 1.0
    return (jnp.asarray(first, BF16), jnp.asarray(second, BF16), jnp.asarray(tw), jnp.asarray(place, BF16))


def channel_kernel(start, order_ref, place_ref, first_ref, second_ref, tw_ref, taps_ref, volts_ref, out_ref, frame, turned, lhs):
    length = taps_ref.shape[1]
    pick = (order_ref[...] == lax.broadcasted_iota(jnp.int32, (64, 64), 1)).astype(BF16)
    pick = jnp.dot(place_ref[...], pick, preferred_element_type=F32).astype(BF16)
    for part in range(4):
        lhs[part * 64 : (part + 1) * 64, :] = jnp.dot(pick, second_ref[part], preferred_element_type=F32).astype(BF16)

    width = 16 * RADIX

    def filter_chunk(chunk, carry):
        lane = pl.multiple_of(chunk * width, width)
        taps = [jnp.broadcast_to(taps_ref[t : t + 1, pl.ds(lane, width)], (8, width)) for t in range(4)]
        for part in range(2):
            volts = [
                volts_ref[part, :, pl.ds((start + n) * length + lane, width)].astype(F32) for n in range(5)
            ]
            for s in range(2):
                total = taps[0] * volts[s]
                for t in range(1, 4):
                    total = total + taps[t] * volts[s + t]
                for a in range(16):
                    at = pl.multiple_of(chunk * width // RADIX * 8 + a * 8, 8)
                    frame[s, part, pl.ds(at, 8), :] = total[:, a * RADIX : (a + 1) * RADIX]
        return carry

    lax.fori_loop(0, length // width, filter_chunk, 0)
    tw_re, tw_im = tw_ref[0], tw_ref[1]
    for f in range(8):
        columns = []
        for s in range(2):
            parts = [frame[s, part, pl.ds(f, RADIX, stride=8), :] for part in range(2)]
            columns.append(jnp.concatenate(parts, axis=0))
        values = jnp.concatenate(columns, axis=1).astype(BF16)
        mid = jnp.dot(first_ref[...], values, preferred_element_type=F32)
        rows = []
        for s in range(2):
            re = mid[:RADIX, s * RADIX : (s + 1) * RADIX]
            im = mid[RADIX:, s * RADIX : (s + 1) * RADIX]
            rows.append(jnp.concatenate([re * tw_re - im * tw_im, re * tw_im + im * tw_re], axis=1).astype(BF16))
        rotated = jnp.concatenate(rows, axis=0)
        out = lax.dot_general(lhs[...], rotated, (((1,), (1,)), ((), ())), preferred_element_type=F32)
        for part in range(2):
            for h in range(2):
                for s in range(2):
                    at = part * RADIX + h * 64
                    turned[part * 4 + s * 2 + h, pl.ds(f, 64, stride=8), :] = out[at : at + 64, s * RADIX : (s + 1) * RADIX]
    for block in range(8):
        out_ref[:, :, block * RADIX : (block + 1) * RADIX] = turned[block].reshape(32, 16, RADIX).astype(BF16)


def channelize(start, voltages, filter_taps, band_order):
    first, second, tw, place = constants(filter_taps.shape[1])
    vmem = pl.BlockSpec(memory_space=pltpu.VMEM)
    return pl.pallas_call(
        lambda *refs: channel_kernel(start, *refs),
        out_shape=jax.ShapeDtypeStruct((32, 16, 1024), BF16),
        in_specs=[vmem] * 7,
        out_specs=vmem,
        scratch_shapes=[
            pltpu.VMEM((2, 2, 8 * RADIX, RADIX), F32),
            pltpu.VMEM((8, 512, RADIX), F32),
            pltpu.VMEM((256, 256), BF16),
        ],
        compiler_params=pltpu.CompilerParams(vmem_limit_bytes=48 * 2**20),
        name="channelize",
    )(band_order.reshape(64, 1), place, first, second, tw, filter_taps, voltages)


def calibrate_kernel(at_ref, got_ref, own_gain_ref, other_gain_ref, own_ref, other_ref):
    half = at_ref[0]
    got = got_ref[...].astype(F32)
    low, high = got[:, :8], got[:, 8:]
    gains = (own_gain_ref[:, :, half], other_gain_ref[...])
    for which, (gain, out_ref) in enumerate(zip(gains, (own_ref, other_ref))):
        take_low = half == which
        gain = gain.astype(F32).reshape(2, 32, 8, 256)
        for s in range(2):
            re_at, im_at = slice(s * 256, (s + 1) * 256), slice(512 + s * 256, 512 + (s + 1) * 256)
            re = jnp.where(take_low, low[:, :, re_at], high[:, :, re_at])
            im = jnp.where(take_low, low[:, :, im_at], high[:, :, im_at])
            out_ref[:, re_at] = (gain[0] * re - gain[1] * im).reshape(256, 256).astype(BF16)
            out_ref[:, im_at] = (gain[0] * im + gain[1] * re).reshape(256, 256).astype(BF16)


def calibrate(half, got, own_gain, other_gain):
    vmem = pl.BlockSpec(memory_space=pltpu.VMEM)
    return pl.pallas_call(
        calibrate_kernel,
        out_shape=[jax.ShapeDtypeStruct((256, 1024), BF16)] * 2,
        in_specs=[pl.BlockSpec(memory_space=pltpu.SMEM)] + [vmem] * 3,
        out_specs=[vmem] * 2,
        compiler_params=pltpu.CompilerParams(vmem_limit_bytes=48 * 2**20),
        name="calibrate",
    )(half.reshape(1), got, own_gain, other_gain)


def weights_kernel(at_ref, mask_ref, own_ref, near_ref, far_ref, end_ref, out_ref):
    band = at_ref[0]
    low = band < 2
    outer = jnp.where(low, 0, 3)
    near_group = jnp.where(low, 2, 1)
    far_group = jnp.where(low, 3, 0)
    end_group = jnp.where(low, 1 - band, 5 - band)
    own_row = pl.multiple_of(jnp.where(low, 256, 0), 256)
    outer_row = pl.multiple_of(jnp.where(low, 0, 256), 256)
    masks = []
    for rows in (band, outer):
        cols = mask_ref[pl.ds(pl.multiple_of(rows * 256, 256), 256), :].astype(F32).astype(BF16)
        masks.append(cols)

    def spread(which, group):
        tile = lax.broadcasted_iota(jnp.int32, (64, 512), 0)
        column = lax.broadcasted_iota(jnp.int32, (64, 512), 1) // TILE + group * 16
        return jnp.dot(masks[which], (tile == column).astype(BF16), preferred_element_type=F32).astype(BF16)

    for group, src_ref, rows in (
        (band, own_ref, (band * 256, outer * 256)),
        (near_group, near_ref, (own_row, outer_row)),
        (far_group, far_ref, (own_row, outer_row)),
        (end_group, end_ref, (0, None)),
    ):
        lanes = pl.ds(pl.multiple_of(group * 512, 512), 512)
        for which, row in enumerate(rows):
            for part in range(2):
                at = slice((which * 2 + part) * 256, (which * 2 + part + 1) * 256)
                if row is None:
                    out_ref[at, lanes] = jnp.zeros((256, 512), BF16)
                else:
                    taken = src_ref[part, pl.ds(pl.multiple_of(row, 256), 256), :]
                    out_ref[at, lanes] = taken * spread(which, group)


def weight_rows(band, mask, own, near, far, end):
    vmem = pl.BlockSpec(memory_space=pltpu.VMEM)
    return pl.pallas_call(
        weights_kernel,
        out_shape=jax.ShapeDtypeStruct((1024, 2048), BF16),
        in_specs=[pl.BlockSpec(memory_space=pltpu.SMEM)] + [vmem] * 5,
        out_specs=vmem,
        compiler_params=pltpu.CompilerParams(vmem_limit_bytes=48 * 2**20),
        name="weight_rows",
    )(band.reshape(1), mask, own, near, far, end)


def pair_kernel(average, at_ref, left_a, left_b, right_a, right_b, out_ref):
    re = im = None
    for left_ref, right_ref in ((left_a, right_a), (left_b, right_b)):
        left, right = left_ref[...], right_ref[...]
        half = left.shape[1] // 2
        crossed = jnp.concatenate([left[:, half:], -left[:, :half]], axis=1)
        dims = (((1,), (1,)), ((), ()))
        now_re = lax.dot_general(left, right, dims, preferred_element_type=F32)
        now_im = lax.dot_general(crossed, right, dims, preferred_element_type=F32)
        re = now_re if re is None else re + now_re
        im = now_im if im is None else im + now_im
    out_ref[0] = (re * average).astype(BF16)
    out_ref[1] = (im * average).astype(BF16)


def pairs(average, row_block, first_col, blocks, width, sections):
    rows, depth = 512, sections[0].shape[1]
    left = pl.BlockSpec((rows, depth), lambda i, at: (at[0], 0))
    right = pl.BlockSpec((width, depth), lambda i, at: (at[1] + i, 0))
    return pl.pallas_call(
        lambda *refs: pair_kernel(average, *refs),
        out_shape=jax.ShapeDtypeStruct((2, rows, blocks * width), BF16),
        grid_spec=pltpu.PrefetchScalarGridSpec(
            num_scalar_prefetch=1,
            grid=(blocks,),
            in_specs=[left, left, right, right],
            out_specs=pl.BlockSpec((2, rows, width), lambda i, at: (0, 0, i)),
        ),
        compiler_params=pltpu.CompilerParams(vmem_limit_bytes=48 * 2**20),
        cost_estimate=pl.CostEstimate(
            flops=8 * rows * blocks * width * depth, bytes_accessed=4 * depth * (rows + blocks * width), transcendentals=0
        ),
        name="pairs",
    )(jnp.stack([row_block, first_col]), sections[0], sections[1], sections[0], sections[1])


def beam_kernel(weight_ref, section_ref, out_ref):
    half = section_ref.shape[1] // 2
    total = jnp.dot(weight_ref[...], section_ref[...], preferred_element_type=F32)
    out_ref[:, :half] = (total[:256, :half] - total[256:, half:]).astype(out_ref.dtype)
    out_ref[:, half:] = (total[:256, half:] + total[256:, :half]).astype(out_ref.dtype)


def beams(which, weights, section, dtype):
    feeds, depth = section.shape
    return pl.pallas_call(
        beam_kernel,
        out_shape=jax.ShapeDtypeStruct((256, depth), dtype),
        grid=(1,),
        in_specs=[pl.BlockSpec((512, feeds), lambda i: (which, 0)), pl.BlockSpec((feeds, depth), lambda i: (0, 0))],
        out_specs=pl.BlockSpec((256, depth), lambda i: (0, 0)),
        compiler_params=pltpu.CompilerParams(vmem_limit_bytes=48 * 2**20),
        cost_estimate=pl.CostEstimate(
            flops=4 * 256 * feeds * depth, bytes_accessed=2 * feeds * (depth + 512), transcendentals=0
        ),
        name="beams",
    )(weights, section)


def shards(voltages, filter_taps, feed_gains, beam_weights, beam_mask, band_order):
    feed, band = lax.axis_index("feed"), lax.axis_index("band")
    half = (feed // 2) % 2
    low = band < 2
    everyone = (0, 1, 2, 3)

    gains = feed_gains.reshape(2, 16, 2, 16, 256)
    other_gain = lax.dynamic_index_in_dim(gains, 1 - half, 2, keepdims=False)
    other_gain = lax.ppermute(other_gain, BOTH, hop(4, everyone))
    own_weights = beam_weights[:, 0]
    away = lax.dynamic_slice_in_dim(own_weights, jnp.where(low, 512, 0), 512, 1)
    near = lax.ppermute(away, BOTH, hop(1, (1,)) + hop(-1, (2,)))
    far = lax.ppermute(away, BOTH, hop(2, (0,)) + hop(-2, (3,)))
    end = lax.dynamic_slice_in_dim(own_weights, jnp.where(low, 256, 512), 256, 1)
    end = lax.ppermute(end, BOTH, hop(1, (0,)) + hop(-1, (3,)))

    sections = []
    for start in (0, 2):
        spectra = channelize(start, voltages, filter_taps, band_order)
        got = lax.all_to_all(spectra, "feed", 0, 0, axis_index_groups=PLANE_GROUPS, tiled=True)
        own, other = calibrate(half, got, gains, other_gain)
        up = [jnp.where(low, own, other)]
        down = [jnp.where(low, other, own)]
        for senders in (everyone, everyone, (0, 1, 2), (1, 2)):
            up.append(lax.ppermute(up[-1], BOTH, hop(1, senders)))
            down.append(lax.ppermute(down[-1], BOTH, hop(-1, tuple(3 - p for p in senders))))
        same, swap = half, 1 - half
        table = (
            (own, ((0, same), (1, same), (2, same), (3, same))),
            (up[1], ((3, swap), (0, same), (1, same), (2, swap))),
            (down[1], ((1, swap), (2, same), (3, same), (0, swap))),
            (up[2], ((2, swap), (3, swap), (0, same), (1, same))),
            (down[2], ((2, same), (3, same), (0, swap), (1, swap))),
            (up[3], ((1, same), (2, swap), (3, swap), (0, same))),
            (down[3], ((3, same), (0, swap), (1, swap), (2, same))),
            (jnp.where(low, down[4], up[4]), ((0, swap), (1, swap), (2, swap), (3, swap))),
        )
        section = jnp.zeros((4, 16, 2, 16, 1024), BF16)
        for unit, places in table:
            group = jnp.stack([jnp.int32(g) for g, _ in places])[band]
            part = jnp.stack([p for _, p in places])[band]
            section = lax.dynamic_update_slice(
                section, unit.reshape(1, 16, 1, 16, 1024), (group, 0, part, 0, 0)
            )
        sections.append(section.reshape(2048, 1024))

    average = 1.0 / 1024
    outer = jnp.where(low, 0, 3)
    weights = weight_rows(band, beam_mask, own_weights, near, far, end)
    inward = hop(-1, (1,)) + hop(1, (2,))
    block = pairs(average, outer, band, 1, 512, sections)
    block = lax.ppermute(block, BOTH, inward)
    share = jnp.stack([beams(1, weights, section, BF16) for section in sections])
    share = lax.ppermute(share, BOTH, inward)

    visibility = pairs(average, band, jnp.int32(0), 4, 512, sections)
    formed = jnp.stack([beams(0, weights, section, F32) for section in sections])
    is_outer = (band == 0) | (band == 3)
    where = jnp.where(low, 1, 2) * 512
    kept = lax.dynamic_slice_in_dim(visibility, where, 512, 2)
    visibility = lax.dynamic_update_slice_in_dim(visibility, jnp.where(is_outer, block, kept), where, 2)
    formed = formed + jnp.where(is_outer, share.astype(F32), 0.0)
    formed = formed.astype(BF16).reshape(2, 256, 2, 2, 256).transpose(1, 2, 0, 3, 4)
    return (visibility[:, None], formed.reshape(1, 256, 2, 4, 256))


def solution(mesh):
    return jax.shard_map(
        shards,
        mesh=mesh,
        in_specs=(
            P(None, ("band", "feed"), None),
            P(),
            P(None, "feed", "band", None),
            P(None, "feed", None, "band"),
            P(),
            P(),
        ),
        out_specs=(P(None, "feed", "band", None), P("feed", "band", None, None, None)),
        check_vma=False,
    )
```

time: 380 us -> 256 us (0.67)
  waiting for transfers between devices: 273 us -> 69.9 us
  starting transfers between devices: 15.1 us -> 65.5 us
  Pallas kernels: 0 us -> 47.2 us
  matrix products: 31.1 us -> 0 us
  local copies, waits for them, and re-layouts: 24.9 us -> 50.1 us
  other arithmetic: 20.8 us -> 6.85 us
    all_gather x1 -> x0, waiting for transfers between devices: 153 us -> none  [shards(): portion = lax.all_gather(calibrated, 'band', axis=1, tiled=True)]
    reduce_scatter x1 -> x0, waiting for transfers between devices: 89.6 us -> none  [shards(): lax.psum_scatter(jnp.stack([part_re, part_im], axis=1).astype(jnp.bfloat1...]
    ppermute x0 -> x22, waiting for transfers between devices: none -> 62 us  [the longest x8 23.2 us: shards(): lax.ppermute(down[-1], BOTH, hop(-1, tuple((3 - p for p in senders))))]
    ppermute x0 -> x22, starting transfers between devices: none -> 52.9 us  [the longest x8 22.1 us: shards(): up.append(lax.ppermute(up[-1], BOTH, hop(1, senders)))]
    pallas_call x0 -> x11, Pallas kernels: none -> 47.2 us  [the longest x4 18 us: beams(): pl.pallas_call(beam_kernel, out_shape=jax.ShapeDtypeStruct((256, depth),...]
    dot_general x16 -> x0, matrix products: 31.1 us -> none  [the longest x4 11.8 us: pair_product(): jnp.einsum('in,jn->ij', left_rows, right_rows, preferred_element_type=jnp...]
    unnamed x16 -> x66, local copies, waits for them, and re-layouts: 2.32 us -> 28.5 us
    all_to_all x1 -> x2, waiting for transfers between devices: 30.6 us -> 7.98 us  [shards(): lax.all_to_all(spectra, 'feed', 0, 0, axis_index_groups=PLANE_GROUPS, til...]
  transfers between devices with their start and end apart: 3 -> 24, of which waited for: 3 -> 9; matrix products, arithmetic and copies ran while one was open for 3% -> 11% of each run, Pallas kernels for 0% -> 15%
where the time goes in v1:
time: 256 us; the launch traced here: 254 us
  waiting for transfers between devices  69.9 us (27%)
  starting transfers between devices  65.5 us (26%)
  local copies, waits for them, and re-layouts  50.1 us (20%)
  Pallas kernels  47.2 us (18%)
  between operations  14.1 us (6%)
  other arithmetic  6.85 us (3%)
    unnamed x66, local copies, waits for them, and re-layouts  28.5 us
    ppermute x8, waiting for transfers between devices, shards(): lax.ppermute(down[-1], BOTH, hop(-1, tuple((3 - p for p in senders))))  23.2 us
    ppermute x8, starting transfers between devices, shards(): up.append(lax.ppermute(up[-1], BOTH, hop(1, senders)))  22.1 us
    ppermute x1, waiting for transfers between devices, shards(): end = lax.ppermute(end, BOTH, hop(1, (0,)) + hop(-1, (3,)))  21.7 us
    pallas_call x4, Pallas kernels, beams(): pl.pallas_call(beam_kernel, out_shape=jax.ShapeDtypeStruct((256, depth),...  18 us
    pallas_call x2, Pallas kernels, pairs(): pl.pallas_call(lambda *refs: pair_kernel(average, *refs), out_shape=jax.S...  17.7 us
    all_to_all x2, starting transfers between devices, shards(): lax.all_to_all(spectra, 'feed', 0, 0, axis_index_groups=PLANE_GROUPS, til...  12.7 us
    ppermute x8, starting transfers between devices, shards(): lax.ppermute(down[-1], BOTH, hop(-1, tuple((3 - p for p in senders))))  11.2 us
  transfers between devices with their start and end apart: 24, of which 9 were waited for; matrix products, arithmetic and copies ran while one was open for 11% of the time, Pallas kernels for 15%

profile of v1, /device:TPU:2, one launch (start us, length us, event | category | flops | bytes accessed | tf_op | source)
XLA Modules:
  0.0 253.7 jit_solution(11728200478696770759)
XLA Ops:
  7.8 3.5 %channelize.3 = bf16[32,16,1024]{2,1,0:T(8,128)(2,1)} custom-call(s32[64,1]{1,0:T(8,128)S(1)} %copy.16.refs_0_, bf16[64,64]{1,0:T(8,128)(2,1)S(1)} %copy-done.26, bf16[256,256]{1,0:T(8,128)(2,1)S(1)} %copy-done.18, bf16[4,64,256]{2,1,0:T(8,128)(2,1)S(1)} %copy-done.20, f32[2,128,128]{2,1,0:T(8,128)S(1)} %copy-done.22, f32[4,16384]{1,0:T(4,128)S(1)} %copy-done.16, ...), custom_call_target="tpu_custom_call" | custom-call | tf_op jit(solution)/shard_map/channelize/pallas_call | solution.py:115
  11.3 7.6 %all-to-all-start.1 = ((bf16[32,16,1024]{2,1,0:T(8,128)(2,1)}), bf16[32,16,1024]{2,1,0:T(8,128)(2,1)S(1)}, u32[]{:S(2)}, u32[]{:S(2)}) async-start(bf16[32,16,1024]{2,1,0:T(8,128)(2,1)} %channelize.3), calls=%async_computation.1 | async-start | bytes 2097152 | tf_op jit(solution)/shard_map/all_to_all | solution.py:284
  27.1 8.0 %all-to-all-done.1.got_ref = bf16[32,16,1024]{2,1,0:T(8,128)(2,1)S(1)} async-done(((bf16[32,16,1024]{2,1,0:T(8,128)(2,1)}), bf16[32,16,1024]{2,1,0:T(8,128)(2,1)S(1)}, u32[]{:S(2)}, u32[]{:S(2)}) %all-to-all-start.1) | async-done | bytes 1048608 | tf_op jit(solution)/shard_map/all_to_all | solution.py:284
  36.0 5.0 %all-to-all-start = ((bf16[32,16,1024]{2,1,0:T(8,128)(2,1)}), bf16[32,16,1024]{2,1,0:T(8,128)(2,1)S(1)}, u32[]{:S(2)}, u32[]{:S(2)}) async-start(bf16[32,16,1024]{2,1,0:T(8,128)(2,1)} %copy-done.9), calls=%async_computation | async-start | bytes 2097152 | tf_op jit(solution)/shard_map/all_to_all | solution.py:284
  45.5 7.2 %collective-permute-start = (bf16[2,16,16,256]{3,2,1,0:T(8,128)(2,1)}, bf16[2,16,16,256]{3,2,1,0:T(8,128)(2,1)S(1)}, u32[]{:S(2)}, u32[]{:S(2)}) collective-permute-start(bf16[2,16,16,256]{3,2,1,0:T(8,128)(2,1)} %dynamic-slice_bitcast_fusion.2), channel_id=1, source_target_pairs={{0,8},{1,9},{2,10},{3,11},{8,0},{9,1},{10,2},{11,3},{4,12},{5,13},... | collective-permute-start | bytes 786440 | tf_op jit(solution)/shard_map/ppermute | solution.py:273
  52.7 5.6 %collective-permute-start.19 = (bf16[2,512,512]{2,1,0:T(8,128)(2,1)}, bf16[2,512,512]{2,1,0:T(8,128)(2,1)}, u32[]{:S(2)}, u32[]{:S(2)}) collective-permute-start(bf16[2,512,512]{2,1,0:T(8,128)(2,1)} %dynamic-slice_bitcast_fusion), channel_id=1, source_target_pairs={{0,2},{8,10},{4,6},{12,14},{16,18},{24,26},{20,22},{28,30},{32,34}... | collective-permute-start | bytes 3145736 | tf_op jit(solution)/shard_map/ppermute | solution.py:277
  61.4 3.8 %collective-permute-done.other_gain_ref = bf16[2,16,16,256]{3,2,1,0:T(8,128)(2,1)S(1)} collective-permute-done((bf16[2,16,16,256]{3,2,1,0:T(8,128)(2,1)}, bf16[2,16,16,256]{3,2,1,0:T(8,128)(2,1)S(1)}, u32[]{:S(2)}, u32[]{:S(2)}) %collective-permute-start) | collective-permute-done | bytes 262176 | tf_op jit(solution)/shard_map/ppermute | solution.py:273
  77.3 21.7 %collective-permute-done.20.end_ref = bf16[2,256,512]{2,1,0:T(8,128)(2,1)} collective-permute-done((bf16[2,256,512]{2,1,0:T(8,128)(2,1)}, bf16[2,256,512]{2,1,0:T(8,128)(2,1)}, u32[]{:S(2)}, u32[]{:S(2)}) %collective-permute-start.20) | collective-permute-done | bytes 524320 | tf_op jit(solution)/shard_map/ppermute | solution.py:279
  102.4 7.8 %collective-permute-done.9 = bf16[256,1024]{1,0:T(8,128)(2,1)} collective-permute-done((bf16[256,1024]{1,0:T(8,128)(2,1)}, bf16[256,1024]{1,0:T(8,128)(2,1)}, u32[]{:S(2)}, u32[]{:S(2)}) %collective-permute-start.9) | collective-permute-done | bytes 524320 | tf_op jit(solution)/shard_map/ppermute | solution.py:289
  110.2 6.5 %collective-permute-start.11 = (bf16[256,1024]{1,0:T(8,128)(2,1)}, bf16[256,1024]{1,0:T(8,128)(2,1)}, u32[]{:S(2)}, u32[]{:S(2)}) collective-permute-start(bf16[256,1024]{1,0:T(8,128)(2,1)} %collective-permute-done.9), channel_id=1, source_target_pairs={{0,1},{1,2},{2,3},{3,8},{8,9},{9,10},{10,11},{11,0},{4,5},{5,6},{6... | collective-permute-start | bytes 1572872 | tf_op jit(solution)/shard_map/ppermute | solution.py:289
  137.8 3.1 %collective-permute-start.4 = (bf16[256,1024]{1,0:T(8,128)(2,1)}, bf16[256,1024]{1,0:T(8,128)(2,1)}, u32[]{:S(2)}, u32[]{:S(2)}) collective-permute-start(bf16[256,1024]{1,0:T(8,128)(2,1)} %collective-permute-done.2), channel_id=1, source_target_pairs={{0,11},{1,0},{2,1},{3,2},{8,3},{9,8},{10,9},{11,10},{4,15},{5,4},{... | collective-permute-start | bytes 1572872 | tf_op jit(solution)/shard_map/ppermute | solution.py:290
  142.1 4.3 %weight_rows.1.weight_ref = bf16[1024,2048]{1,0:T(8,128)(2,1)} custom-call(s32[1]{0:T(128)} %bitcast.at_ref, s32[1024,64]{1,0:T(8,128)S(1)} %copy.34.mask_ref, bf16[2,1024,512]{2,1,0:T(8,128)(2,1)S(1)} %bitcast.86, bf16[2,512,512]{2,1,0:T(8,128)(2,1)} %collective-permute-done.18.near_ref, bf16[2,512,512]{2,1,0:T(8,128)(2,1)} %collective-permute-done.19.far_ref, ...), custom_call_target="tpu_custom_call" | custom-call | tf_op jit(solution)/shard_map/weight_rows/pallas_call | solution.py:196
  152.4 4.6 %collective-permute-start.5 = (bf16[256,1024]{1,0:T(8,128)(2,1)S(1)}, bf16[256,1024]{1,0:T(8,128)(2,1)S(1)}, u32[]{:S(2)}, u32[]{:S(2)}) collective-permute-start(bf16[256,1024]{1,0:T(8,128)(2,1)S(1)} %collective-permute-done.3), channel_id=1, source_target_pairs={{0,1},{1,2},{2,3},{8,9},{9,10},{10,11},{4,5},{5,6},{6,7},{12,13},{... | collective-permute-start | bytes 1572872 | tf_op jit(solution)/shard_map/ppermute | solution.py:289
  161.7 5.3 %collective-permute-done.14 = bf16[256,1024]{1,0:T(8,128)(2,1)S(1)} collective-permute-done((bf16[256,1024]{1,0:T(8,128)(2,1)}, bf16[256,1024]{1,0:T(8,128)(2,1)S(1)}, u32[]{:S(2)}, u32[]{:S(2)}) %collective-permute-start.14) | collective-permute-done | bytes 524320 | tf_op jit(solution)/shard_map/ppermute | solution.py:290
  170.0 8.1 %collective-permute-done.6 = bf16[256,1024]{1,0:T(8,128)(2,1)S(1)} collective-permute-done((bf16[256,1024]{1,0:T(8,128)(2,1)}, bf16[256,1024]{1,0:T(8,128)(2,1)S(1)}, u32[]{:S(2)}, u32[]{:S(2)}) %collective-permute-start.6) | collective-permute-done | bytes 524320 | tf_op jit(solution)/shard_map/ppermute | solution.py:290
  181.2 8.2 %collective-permute-done.15 = bf16[256,1024]{1,0:T(8,128)(2,1)S(1)} collective-permute-done((bf16[256,1024]{1,0:T(8,128)(2,1)S(1)}, bf16[256,1024]{1,0:T(8,128)(2,1)S(1)}, u32[]{:S(2)}, u32[]{:S(2)}) %collective-permute-start.15) | collective-permute-done | bytes 524320 | tf_op jit(solution)/shard_map/ppermute | solution.py:290
  191.5 4.5 %beams.7 = bf16[256,1024]{1,0:T(8,128)(2,1)S(1)} custom-call(bf16[1024,2048]{1,0:T(8,128)(2,1)S(1)} %copy-done, bf16[2048,1024]{1,0:T(8,128)(2,1)} %bitcast.96), custom_call_target="tpu_custom_call" | custom-call | flops 2147483648 | bytes 6291456 | tf_op jit(solution)/shard_map/beams/pallas_call | solution.py:251
  199.7 4.5 %beams.6 = bf16[256,1024]{1,0:T(8,128)(2,1)S(1)} custom-call(bf16[1024,2048]{1,0:T(8,128)(2,1)S(1)} %copy-done, bf16[2048,1024]{1,0:T(8,128)(2,1)} %bitcast.79), custom_call_target="tpu_custom_call" | custom-call | flops 2147483648 | bytes 6291456 | tf_op jit(solution)/shard_map/beams/pallas_call | solution.py:251
  207.8 4.6 %pairs.3 = bf16[2,512,512]{2,1,0:T(8,128)(2,1)S(1)} custom-call(s32[2]{0:T(128)S(1)} %pad_add_fusion.1.refs_0_, bf16[2048,1024]{1,0:T(8,128)(2,1)S(1)} %bitcast.83, bf16[2048,1024]{1,0:T(8,128)(2,1)} %bitcast.97, bf16[2048,1024]{1,0:T(8,128)(2,1)S(1)} %bitcast.84, bf16[2048,1024]{1,0:T(8,128)(2,1)} %bitcast.98), custom_call_target="tpu_custom_call" | custom-call | flops 2147483648 | bytes 4194304 | tf_op jit(solution)/shard_map/pairs/pallas_call | solution.py:225
  213.9 13.1 %pairs.2 = bf16[2,512,2048]{2,1,0:T(8,128)(2,1)S(1)} custom-call(s32[2]{0:T(128)S(1)} %pad_add_fusion.refs_0_, bf16[2048,1024]{1,0:T(8,128)(2,1)} %bitcast.80, bf16[2048,1024]{1,0:T(8,128)(2,1)} %bitcast.99, bf16[2048,1024]{1,0:T(8,128)(2,1)} %bitcast.81, bf16[2048,1024]{1,0:T(8,128)(2,1)} %bitcast.100), custom_call_target="tpu_custom_call" | custom-call | flops 8589934592 | bytes 10485760 | tf_op jit(solution)/shard_map/pairs/pallas_call | solution.py:225
  231.1 4.5 %beams.5 = f32[256,1024]{1,0:T(8,128)S(1)} custom-call(bf16[1024,2048]{1,0:T(8,128)(2,1)S(1)} %copy-done, bf16[2048,1024]{1,0:T(8,128)(2,1)} %bitcast.101), custom_call_target="tpu_custom_call" | custom-call | flops 2147483648 | bytes 6291456 | tf_op jit(solution)/shard_map/beams/pallas_call | solution.py:251
  235.7 4.5 %beams.4 = f32[256,1024]{1,0:T(8,128)S(1)} custom-call(bf16[1024,2048]{1,0:T(8,128)(2,1)S(1)} %copy-done, bf16[2048,1024]{1,0:T(8,128)(2,1)} %bitcast.82), custom_call_target="tpu_custom_call" | custom-call | flops 2147483648 | bytes 6291456 | tf_op jit(solution)/shard_map/beams/pallas_call | solution.py:251
  245.5 5.5 %collective-permute-done.17 = bf16[2,512,512]{2,1,0:T(8,128)(2,1)} collective-permute-done((bf16[2,512,512]{2,1,0:T(8,128)(2,1)S(1)}, bf16[2,512,512]{2,1,0:T(8,128)(2,1)}, u32[]{:S(2)}, u32[]{:S(2)}) %collective-permute-start.17) | collective-permute-done | bytes 1048608 | tf_op jit(solution)/shard_map/ppermute | solution.py:316
  250.9 2.8 %bitcast_dynamic-update-slice_fusion = bf16[2,1,512,2048]{3,2,0,1:T(8,128)(2,1)} fusion(bf16[2,1,512,2048]{3,2,0,1:T(8,128)(2,1)} %copy.53, s32[]{:T(128)S(6)} %select_n.185, bf16[2,512,512]{2,1,0:T(8,128)(2,1)} %collective-permute-done.17, bf16[2,512,2048]{2,1,0:T(8,128)(2,1)} %copy-done.5, pred[]{:T(512)S(6)} %or.3), kind=kLoop, calls=%fused_computation.3 | loop fusion | flops 524288 | bytes 3145733 | tf_op jit(solution)/shard_map/dynamic_update_slice | solution.py:325
  (144 shorter events, 85.3 us)
Async XLA Ops:
  11.3 23.7 %all-to-all-start.1 = ((bf16[32,16,1024]{2,1,0:T(8,128)(2,1)}), bf16[32,16,1024]{2,1,0:T(8,128)(2,1)S(1)}, u32[]{:S(2)}, u32[]{:S(2)}) async-start(bf16[32,16,1024]{2,1,0:T(8,128)(2,1)} %channelize.3), calls=%async_computation.1 | async-start | bytes 2097152 | tf_op jit(solution)/shard_map/all_to_all | solution.py:284
  36.0 37.8 %all-to-all-start = ((bf16[32,16,1024]{2,1,0:T(8,128)(2,1)}), bf16[32,16,1024]{2,1,0:T(8,128)(2,1)S(1)}, u32[]{:S(2)}, u32[]{:S(2)}) async-start(bf16[32,16,1024]{2,1,0:T(8,128)(2,1)} %copy-done.9), calls=%async_computation | async-start | bytes 2097152 | tf_op jit(solution)/shard_map/all_to_all | solution.py:284
  42.2 59.3 %collective-permute-start.18 = (bf16[2,512,512]{2,1,0:T(8,128)(2,1)}, bf16[2,512,512]{2,1,0:T(8,128)(2,1)}, u32[]{:S(2)}, u32[]{:S(2)}) collective-permute-start(bf16[2,512,512]{2,1,0:T(8,128)(2,1)} %dynamic-slice_bitcast_fusion), channel_id=1, source_target_pairs={{1,2},{9,10},{5,6},{13,14},{17,18},{25,26},{21,22},{29,30},{33,34}... | collective-permute-start | bytes 3145736 | tf_op jit(solution)/shard_map/ppermute | solution.py:276
  45.5 19.7 %collective-permute-start = (bf16[2,16,16,256]{3,2,1,0:T(8,128)(2,1)}, bf16[2,16,16,256]{3,2,1,0:T(8,128)(2,1)S(1)}, u32[]{:S(2)}, u32[]{:S(2)}) collective-permute-start(bf16[2,16,16,256]{3,2,1,0:T(8,128)(2,1)} %dynamic-slice_bitcast_fusion.2), channel_id=1, source_target_pairs={{0,8},{1,9},{2,10},{3,11},{8,0},{9,1},{10,2},{11,3},{4,12},{5,13},... | collective-permute-start | bytes 786440 | tf_op jit(solution)/shard_map/ppermute | solution.py:273
  52.7 89.4 %collective-permute-start.19 = (bf16[2,512,512]{2,1,0:T(8,128)(2,1)}, bf16[2,512,512]{2,1,0:T(8,128)(2,1)}, u32[]{:S(2)}, u32[]{:S(2)}) collective-permute-start(bf16[2,512,512]{2,1,0:T(8,128)(2,1)} %dynamic-slice_bitcast_fusion), channel_id=1, source_target_pairs={{0,2},{8,10},{4,6},{12,14},{16,18},{24,26},{20,22},{28,30},{32,34}... | collective-permute-start | bytes 3145736 | tf_op jit(solution)/shard_map/ppermute | solution.py:277
  59.2 39.8 %collective-permute-start.20 = (bf16[2,256,512]{2,1,0:T(8,128)(2,1)}, bf16[2,256,512]{2,1,0:T(8,128)(2,1)}, u32[]{:S(2)}, u32[]{:S(2)}) collective-permute-start(bf16[2,256,512]{2,1,0:T(8,128)(2,1)} %dynamic-slice_bitcast_fusion.1), channel_id=1, source_target_pairs={{0,1},{8,9},{4,5},{12,13},{16,17},{24,25},{20,21},{28,29},{32,33},... | collective-permute-start | bytes 1572872 | tf_op jit(solution)/shard_map/ppermute | solution.py:279
  69.2 41.0 %collective-permute-start.9 = (bf16[256,1024]{1,0:T(8,128)(2,1)}, bf16[256,1024]{1,0:T(8,128)(2,1)}, u32[]{:S(2)}, u32[]{:S(2)}) collective-permute-start(bf16[256,1024]{1,0:T(8,128)(2,1)} %get-tuple-element.13), channel_id=1, source_target_pairs={{0,1},{1,2},{2,3},{3,8},{8,9},{9,10},{10,11},{11,0},{4,5},{5,6},{6... | collective-permute-start | bytes 1572872 | tf_op jit(solution)/shard_map/ppermute | solution.py:289
  71.6 45.1 %collective-permute-start.10 = (bf16[256,1024]{1,0:T(8,128)(2,1)}, bf16[256,1024]{1,0:T(8,128)(2,1)}, u32[]{:S(2)}, u32[]{:S(2)}) collective-permute-start(bf16[256,1024]{1,0:T(8,128)(2,1)} %get-tuple-element.12), channel_id=1, source_target_pairs={{0,11},{1,0},{2,1},{3,2},{8,3},{9,8},{10,9},{11,10},{4,15},{5,4},{... | collective-permute-start | bytes 1572872 | tf_op jit(solution)/shard_map/ppermute | solution.py:290
  99.0 36.1 %collective-permute-start.1 = (bf16[256,1024]{1,0:T(8,128)(2,1)}, bf16[256,1024]{1,0:T(8,128)(2,1)}, u32[]{:S(2)}, u32[]{:S(2)}) collective-permute-start(bf16[256,1024]{1,0:T(8,128)(2,1)} %get-tuple-element.15), channel_id=1, source_target_pairs={{0,1},{1,2},{2,3},{3,8},{8,9},{9,10},{10,11},{11,0},{4,5},{5,6},{6... | collective-permute-start | bytes 1572872 | tf_op jit(solution)/shard_map/ppermute | solution.py:289
  101.4 36.3 %collective-permute-start.2 = (bf16[256,1024]{1,0:T(8,128)(2,1)}, bf16[256,1024]{1,0:T(8,128)(2,1)}, u32[]{:S(2)}, u32[]{:S(2)}) collective-permute-start(bf16[256,1024]{1,0:T(8,128)(2,1)} %get-tuple-element.14), channel_id=1, source_target_pairs={{0,11},{1,0},{2,1},{3,2},{8,3},{9,8},{10,9},{11,10},{4,15},{5,4},{... | collective-permute-start | bytes 1572872 | tf_op jit(solution)/shard_map/ppermute | solution.py:290
  110.2 38.4 %collective-permute-start.11 = (bf16[256,1024]{1,0:T(8,128)(2,1)}, bf16[256,1024]{1,0:T(8,128)(2,1)}, u32[]{:S(2)}, u32[]{:S(2)}) collective-permute-start(bf16[256,1024]{1,0:T(8,128)(2,1)} %collective-permute-done.9), channel_id=1, source_target_pairs={{0,1},{1,2},{2,3},{3,8},{8,9},{9,10},{10,11},{11,0},{4,5},{5,6},{6... | collective-permute-start | bytes 1572872 | tf_op jit(solution)/shard_map/ppermute | solution.py:289
  116.7 33.3 %collective-permute-start.12 = (bf16[256,1024]{1,0:T(8,128)(2,1)}, bf16[256,1024]{1,0:T(8,128)(2,1)}, u32[]{:S(2)}, u32[]{:S(2)}) collective-permute-start(bf16[256,1024]{1,0:T(8,128)(2,1)} %collective-permute-done.10), channel_id=1, source_target_pairs={{0,11},{1,0},{2,1},{3,2},{8,3},{9,8},{10,9},{11,10},{4,15},{5,4},{... | collective-permute-start | bytes 1572872 | tf_op jit(solution)/shard_map/ppermute | solution.py:290
  135.0 17.3 %collective-permute-start.3 = (bf16[256,1024]{1,0:T(8,128)(2,1)}, bf16[256,1024]{1,0:T(8,128)(2,1)S(1)}, u32[]{:S(2)}, u32[]{:S(2)}) collective-permute-start(bf16[256,1024]{1,0:T(8,128)(2,1)} %collective-permute-done.1), channel_id=1, source_target_pairs={{0,1},{1,2},{2,3},{3,8},{8,9},{9,10},{10,11},{11,0},{4,5},{5,6},{6... | collective-permute-start | bytes 1572872 | tf_op jit(solution)/shard_map/ppermute | solution.py:289
  137.8 19.2 %collective-permute-start.4 = (bf16[256,1024]{1,0:T(8,128)(2,1)}, bf16[256,1024]{1,0:T(8,128)(2,1)}, u32[]{:S(2)}, u32[]{:S(2)}) collective-permute-start(bf16[256,1024]{1,0:T(8,128)(2,1)} %collective-permute-done.2), channel_id=1, source_target_pairs={{0,11},{1,0},{2,1},{3,2},{8,3},{9,8},{10,9},{11,10},{4,15},{5,4},{... | collective-permute-start | bytes 1572872 | tf_op jit(solution)/shard_map/ppermute | solution.py:290
  148.6 19.6 %collective-permute-start.13 = (bf16[256,1024]{1,0:T(8,128)(2,1)}, bf16[256,1024]{1,0:T(8,128)(2,1)S(1)}, u32[]{:S(2)}, u32[]{:S(2)}) collective-permute-start(bf16[256,1024]{1,0:T(8,128)(2,1)} %collective-permute-done.11), channel_id=1, source_target_pairs={{0,1},{1,2},{2,3},{8,9},{9,10},{10,11},{4,5},{5,6},{6,7},{12,13},{... | collective-permute-start | bytes 1572872 | tf_op jit(solution)/shard_map/ppermute | solution.py:289
  150.0 17.0 %collective-permute-start.14 = (bf16[256,1024]{1,0:T(8,128)(2,1)}, bf16[256,1024]{1,0:T(8,128)(2,1)S(1)}, u32[]{:S(2)}, u32[]{:S(2)}) collective-permute-start(bf16[256,1024]{1,0:T(8,128)(2,1)} %collective-permute-done.12), channel_id=1, source_target_pairs={{1,0},{2,1},{3,2},{9,8},{10,9},{11,10},{5,4},{6,5},{7,6},{13,12},{... | collective-permute-start | bytes 1572872 | tf_op jit(solution)/shard_map/ppermute | solution.py:290
  152.4 27.1 %collective-permute-start.5 = (bf16[256,1024]{1,0:T(8,128)(2,1)S(1)}, bf16[256,1024]{1,0:T(8,128)(2,1)S(1)}, u32[]{:S(2)}, u32[]{:S(2)}) collective-permute-start(bf16[256,1024]{1,0:T(8,128)(2,1)S(1)} %collective-permute-done.3), channel_id=1, source_target_pairs={{0,1},{1,2},{2,3},{8,9},{9,10},{10,11},{4,5},{5,6},{6,7},{12,13},{... | collective-permute-start | bytes 1572872 | tf_op jit(solution)/shard_map/ppermute | solution.py:289
  157.0 21.2 %collective-permute-start.6 = (bf16[256,1024]{1,0:T(8,128)(2,1)}, bf16[256,1024]{1,0:T(8,128)(2,1)S(1)}, u32[]{:S(2)}, u32[]{:S(2)}) collective-permute-start(bf16[256,1024]{1,0:T(8,128)(2,1)} %collective-permute-done.4), channel_id=1, source_target_pairs={{1,0},{2,1},{3,2},{9,8},{10,9},{11,10},{5,4},{6,5},{7,6},{13,12},{... | collective-permute-start | bytes 1572872 | tf_op jit(solution)/shard_map/ppermute | solution.py:290
  166.9 22.5 %collective-permute-start.15 = (bf16[256,1024]{1,0:T(8,128)(2,1)S(1)}, bf16[256,1024]{1,0:T(8,128)(2,1)S(1)}, u32[]{:S(2)}, u32[]{:S(2)}) collective-permute-start(bf16[256,1024]{1,0:T(8,128)(2,1)S(1)} %collective-permute-done.14), channel_id=1, source_target_pairs={{1,0},{2,1},{9,8},{10,9},{5,4},{6,5},{13,12},{14,13},{17,16},{18,1... | collective-permute-start | bytes 1572872 | tf_op jit(solution)/shard_map/ppermute | solution.py:290
  168.2 21.2 %collective-permute-start.16 = (bf16[256,1024]{1,0:T(8,128)(2,1)S(1)}, bf16[256,1024]{1,0:T(8,128)(2,1)S(1)}, u32[]{:S(2)}, u32[]{:S(2)}) collective-permute-start(bf16[256,1024]{1,0:T(8,128)(2,1)S(1)} %collective-permute-done.13), channel_id=1, source_target_pairs={{1,2},{2,3},{9,10},{10,11},{5,6},{6,7},{13,14},{14,15},{17,18},{18... | collective-permute-start | bytes 1572872 | tf_op jit(solution)/shard_map/ppermute | solution.py:289
  178.2 19.4 %collective-permute-start.7 = (bf16[256,1024]{1,0:T(8,128)(2,1)S(1)}, bf16[256,1024]{1,0:T(8,128)(2,1)S(1)}, u32[]{:S(2)}, u32[]{:S(2)}) collective-permute-start(bf16[256,1024]{1,0:T(8,128)(2,1)S(1)} %collective-permute-done.6), channel_id=1, source_target_pairs={{1,0},{2,1},{9,8},{10,9},{5,4},{6,5},{13,12},{14,13},{17,16},{18,1... | collective-permute-start | bytes 1572872 | tf_op jit(solution)/shard_map/ppermute | solution.py:290
  179.5 18.1 %collective-permute-start.8 = (bf16[256,1024]{1,0:T(8,128)(2,1)S(1)}, bf16[256,1024]{1,0:T(8,128)(2,1)}, u32[]{:S(2)}, u32[]{:S(2)}) collective-permute-start(bf16[256,1024]{1,0:T(8,128)(2,1)S(1)} %collective-permute-done.5), channel_id=1, source_target_pairs={{1,2},{2,3},{9,10},{10,11},{5,6},{6,7},{13,14},{14,15},{17,18},{18... | collective-permute-start | bytes 1572872 | tf_op jit(solution)/shard_map/ppermute | solution.py:289
  204.4 35.8 %collective-permute-start.21 = (bf16[2,256,1024]{2,1,0:T(8,128)(2,1)S(1)}, bf16[2,256,1024]{2,1,0:T(8,128)(2,1)S(1)}, u32[]{:S(2)}, u32[]{:S(2)}) collective-permute-start(bf16[2,256,1024]{2,1,0:T(8,128)(2,1)S(1)} %pad_maximum_fusion), channel_id=1, source_target_pairs={{1,0},{9,8},{5,4},{13,12},{17,16},{25,24},{21,20},{29,28},{33,32},... | collective-permute-start | bytes 3145736 | tf_op jit(solution)/shard_map/ppermute | solution.py:318
  212.4 38.5 %collective-permute-start.17 = (bf16[2,512,512]{2,1,0:T(8,128)(2,1)S(1)}, bf16[2,512,512]{2,1,0:T(8,128)(2,1)}, u32[]{:S(2)}, u32[]{:S(2)}) collective-permute-start(bf16[2,512,512]{2,1,0:T(8,128)(2,1)S(1)} %pairs.3), channel_id=1, source_target_pairs={{1,0},{9,8},{5,4},{13,12},{17,16},{25,24},{21,20},{29,28},{33,32},... | collective-permute-start | bytes 3145736 | tf_op jit(solution)/shard_map/ppermute | solution.py:316
  (32 other events, 373.0 us)

commit v2 on v0

v2 whole, which is shorter than its diff:
```python
import math

import jax
import jax.numpy as jnp
import numpy as np
from jax import lax
from jax.experimental import pallas as pl
from jax.experimental.pallas import tpu as pltpu
from jax.sharding import PartitionSpec as P

RADIX = 128
TILE = 32
SIDE = 4
BOTH = ("feed", "band")
F32 = jnp.float32
BF16 = jnp.bfloat16


def feed_at(y, x, half, core):
    return ((y * SIDE + x) * 2 + half) * 2 + core


PLANE_GROUPS = [
    [feed_at(y, x, half, core) for y in range(SIDE) for x in range(SIDE) for core in range(2)]
    for half in range(2)
]


def hop(step, senders):
    pairs = []
    for y in range(SIDE):
        for x in range(SIDE):
            for core in range(2):
                for z in range(8):
                    if z % 4 in senders:
                        to = (z + step) % 8
                        pairs.append(
                            (feed_at(y, x, z // 4, core) * 4 + z % 4, feed_at(y, x, to // 4, core) * 4 + to % 4)
                        )
    return pairs


def constants(length):
    row = np.arange(RADIX)
    angles = (row[:, None] * row[None, :] % RADIX) * (2.0 * math.pi / RADIX)
    factor = 1.0 / math.sqrt(RADIX)
    re = (np.cos(angles) * factor).astype(np.float32)
    im = (-np.sin(angles) * factor).astype(np.float32)
    first = np.block([[re, -im], [im, re]])
    second = np.stack([np.hstack([re, -im]), np.hstack([im, re])])
    second = second.reshape(2, RADIX // 2, 2, 2 * RADIX).transpose(0, 2, 1, 3).reshape(2 * RADIX, 2 * RADIX)
    twiddle = (row[:, None] * row[None, :] % length) * (2.0 * math.pi / length)
    tw = np.stack([np.cos(twiddle), -np.sin(twiddle)]).astype(np.float32)
    place = np.zeros((64, 2 * RADIX), np.float32)
    for yx in range(16):
        for core in range(2):
            for half in range(2):
                place[(yx * 2 + core) * 2 + half, (yx * 2 + half) * 2 + core] = 1.0
    return (jnp.asarray(np.concatenate([first, second, place]), BF16), jnp.asarray(tw))


def channel_kernel(order_ref, tables_hbm, tw_hbm, taps_hbm, volts_hbm, out_ref, frame, turned, lhs, tables, tw_ref, taps_ref, volts_ref, sems):
    length = taps_ref.shape[1]
    early, late = pl.ds(0, 5 * length), pl.ds(5 * length, 2 * length)
    copies = [
        pltpu.make_async_copy(tables_hbm, tables, sems.at[0]),
        pltpu.make_async_copy(taps_hbm, taps_ref, sems.at[1]),
        pltpu.make_async_copy(volts_hbm.at[:, :, early], volts_ref.at[:, :, early], sems.at[2]),
        pltpu.make_async_copy(tw_hbm, tw_ref, sems.at[3]),
        pltpu.make_async_copy(volts_hbm.at[:, :, late], volts_ref.at[:, :, late], sems.at[4]),
    ]
    for copy in copies:
        copy.start()
    pick = (order_ref[...] == lax.broadcasted_iota(jnp.int32, (64, 64), 0)).astype(BF16)
    copies[0].wait()
    pick = lax.dot_general(tables[512:576, :64], pick, BOTH_LAST, preferred_element_type=F32).astype(BF16)
    for part in range(4):
        second = tables[256 + part * 64 : 256 + (part + 1) * 64, :]
        lhs[part * 64 : (part + 1) * 64, :] = jnp.dot(pick, second, preferred_element_type=F32).astype(BF16)
    width = 16 * RADIX
    for copy in copies[1:4]:
        copy.wait()
    for start in (0, 2):
        if start:
            copies[4].wait()

        def filter_chunk(chunk, carry):
            lane = pl.multiple_of(chunk * width, width)
            taps = [jnp.broadcast_to(taps_ref[t : t + 1, pl.ds(lane, width)], (8, width)) for t in range(4)]
            for part in range(2):
                volts = [volts_ref[part, :, pl.ds((start + n) * length + lane, width)].astype(F32) for n in range(5)]
                for s in range(2):
                    total = taps[0] * volts[s]
                    for t in range(1, 4):
                        total = total + taps[t] * volts[s + t]
                    for a in range(16):
                        at = pl.multiple_of(chunk * width // RADIX * 8 + a * 8, 8)
                        frame[s, part, pl.ds(at, 8), :] = total[:, a * RADIX : (a + 1) * RADIX]
            return carry

        lax.fori_loop(0, length // width, filter_chunk, 0)
        tw_re, tw_im = tw_ref[0], tw_ref[1]
        for f in range(8):
            columns = []
            for s in range(2):
                parts = [frame[s, part, pl.ds(f, RADIX, stride=8), :] for part in range(2)]
                columns.append(jnp.concatenate(parts, axis=0))
            values = jnp.concatenate(columns, axis=1).astype(BF16)
            mid = jnp.dot(tables[:256, :], values, preferred_element_type=F32)
            rows = []
            for s in range(2):
                re = mid[:RADIX, s * RADIX : (s + 1) * RADIX]
                im = mid[RADIX:, s * RADIX : (s + 1) * RADIX]
                rows.append(jnp.concatenate([re * tw_re - im * tw_im, re * tw_im + im * tw_re], axis=1).astype(BF16))
            rotated = jnp.concatenate(rows, axis=0)
            out = lax.dot_general(lhs[...], rotated, BOTH_LAST, preferred_element_type=F32)
            for part in range(2):
                for h in range(2):
                    for s in range(2):
                        at = part * RADIX + h * 64
                        columns = out[at : at + 64, s * RADIX : (s + 1) * RADIX]
                        turned[s * 4 + part * 2 + h, pl.ds(f, 64, stride=8), :] = columns
        for block in range(8):
            at = start * 512 + block * RADIX
            out_ref[:, :, at : at + RADIX] = turned[block].reshape(32, 16, RADIX).astype(BF16)


ANY = pl.BlockSpec(memory_space=pl.ANY)
VMEM = pl.BlockSpec(memory_space=pltpu.VMEM)
SMEM = pl.BlockSpec(memory_space=pltpu.SMEM)
GRANT = pltpu.CompilerParams(vmem_limit_bytes=56 * 2**20)
BRIEF = pl.CostEstimate(flops=1, bytes_accessed=1, transcendentals=0)


BOTH_LAST = (((1,), (1,)), ((), ()))


def channelize(voltages, filter_taps, band_order):
    tables, tw = constants(filter_taps.shape[1])
    return pl.pallas_call(
        channel_kernel,
        out_shape=jax.ShapeDtypeStruct((32, 16, 2048), BF16),
        in_specs=[VMEM] + [ANY] * 4,
        out_specs=VMEM,
        scratch_shapes=[
            pltpu.VMEM((2, 2, 8 * RADIX, RADIX), F32),
            pltpu.VMEM((8, 512, RADIX), F32),
            pltpu.VMEM((256, 256), BF16),
            pltpu.VMEM(tables.shape, BF16),
            pltpu.VMEM(tw.shape, F32),
            pltpu.VMEM(filter_taps.shape, F32),
            pltpu.VMEM(voltages.shape, BF16),
            pltpu.SemaphoreType.DMA((5,)),
        ],
        compiler_params=GRANT,
        cost_estimate=BRIEF,
        name="channelize",
    )(band_order.reshape(1, 64), tables, tw, filter_taps, voltages)


def times(gain, values):
    parts = []
    for at in range(0, values.shape[-1], 512):
        re, im = values[:, at : at + 256], values[:, at + 256 : at + 512]
        parts += [gain[0] * re - gain[1] * im, gain[0] * im + gain[1] * re]
    return jnp.concatenate(parts, axis=1)


def calibrate_kernel(at_ref, got_ref, gain_ref, up_ref, down_ref):
    half, low_band = at_ref[0], at_ref[1] < 2
    got = got_ref[...].astype(F32)
    swapped = half == 1
    own = jnp.where(swapped, got[:, 8:], got[:, :8]).reshape(256, got.shape[2])
    other = jnp.where(swapped, got[:, :8], got[:, 8:]).reshape(256, got.shape[2])
    own = times(gain_ref[:, :, half].astype(F32).reshape(2, 256, 256), own)
    up_ref[...] = jnp.where(low_band, own, other).astype(BF16)
    down_ref[...] = jnp.where(low_band, other, own).astype(BF16)


def calibrate(section, place, got, gains):
    return pl.pallas_call(
        calibrate_kernel,
        out_shape=[jax.ShapeDtypeStruct((256, 1024), BF16)] * 2,
        grid=(1,),
        in_specs=[
            SMEM,
            pl.BlockSpec((32, 16, 1024), lambda i: (0, 0, section)),
            pl.BlockSpec((2, 16, 2, 16, 256), lambda i: (0, 0, 0, 0, 0)),
        ],
        out_specs=[pl.BlockSpec((256, 1024), lambda i: (0, 0))] * 2,
        compiler_params=GRANT,
        cost_estimate=BRIEF,
        name="calibrate",
    )(place, got, gains)


def enter_kernel(at_ref, part_hbm, gain_hbm, out_hbm, part, gain, sems):
    @pl.when(at_ref[0] == 1)
    def _():
        loads = [pltpu.make_async_copy(part_hbm, part, sems.at[0]), pltpu.make_async_copy(gain_hbm, gain, sems.at[1])]
        for copy in loads:
            copy.start()
        for copy in loads:
            copy.wait()
        part[...] = times(gain[...].astype(F32).reshape(2, 256, 256), part[...].astype(F32)).astype(BF16)
        store = pltpu.make_async_copy(part, out_hbm, sems.at[2])
        store.start()
        store.wait()


def enter(is_entry, part, gain):
    return pl.pallas_call(
        enter_kernel,
        out_shape=jax.ShapeDtypeStruct(part.shape, BF16),
        in_specs=[SMEM, ANY, ANY],
        out_specs=ANY,
        scratch_shapes=[
            pltpu.VMEM(part.shape, BF16),
            pltpu.VMEM(gain.shape, BF16),
            pltpu.SemaphoreType.DMA((3,)),
        ],
        input_output_aliases={1: 0},
        compiler_params=GRANT,
        cost_estimate=BRIEF,
        name="enter",
    )(is_entry.astype(jnp.int32).reshape(1), part, gain)


def spread(mask, group):
    tile = lax.broadcasted_iota(jnp.int32, (64, 512), 0)
    column = lax.broadcasted_iota(jnp.int32, (64, 512), 1) // TILE + group * 16
    return jnp.dot(mask, (tile == column).astype(BF16), preferred_element_type=F32).astype(BF16)


def weights_kernel(at_ref, mask_ref, local_ref, near_ref, far_ref, end_ref, out_ref):
    band = at_ref[0]
    low = band < 2
    groups = (band, jnp.where(low, 2, 1), jnp.where(low, 3, 0), jnp.where(low, 1 - band, 5 - band))
    mask = mask_ref[...].astype(F32).astype(BF16)
    for group, src_ref in zip(groups, (local_ref, near_ref, far_ref, end_ref)):
        lanes = pl.ds(pl.multiple_of(group * 512, 512), 512)
        wide = spread(mask, group)
        for part in range(2):
            out_ref[part * 256 : (part + 1) * 256, lanes] = src_ref[part] * wide


def weight_rows(band, mask, local, *others):
    fixed = pl.BlockSpec((2, 256, 512), lambda i, at: (0, 0, 0))
    return pl.pallas_call(
        weights_kernel,
        out_shape=jax.ShapeDtypeStruct((512, 2048), BF16),
        grid_spec=pltpu.PrefetchScalarGridSpec(
            num_scalar_prefetch=1,
            grid=(1,),
            in_specs=[
                pl.BlockSpec((256, 64), lambda i, at: (at[0], 0)),
                pl.BlockSpec((2, 256, 512), lambda i, at: (0, at[0], 0)),
            ]
            + [fixed] * 3,
            out_specs=pl.BlockSpec((512, 2048), lambda i, at: (0, 0)),
        ),
        compiler_params=GRANT,
        cost_estimate=BRIEF,
        name="weight_rows",
    )(band.reshape(1), mask, local, *others)


def crossed(left):
    parts = []
    for at in range(0, left.shape[1], 512):
        parts += [left[:, at + 256 : at + 512], -left[:, at : at + 256]]
    return jnp.concatenate(parts, axis=1)


def fetch(low, half, sources, to, sems):
    waits = []
    for index, (below, above) in enumerate(sources):
        place = to.at[:, half if index == 0 else 1 - half]
        copies = [pltpu.make_async_copy(ref, place, sems.at[index]) for ref in (below, above)]
        pl.when(low)(copies[0].start)
        pl.when(jnp.logical_not(low))(copies[1].start)
        waits.append(copies[0])
    return waits


def weighted(mask, group, weight_ref, values):
    wide = spread(mask, group)
    both = jnp.concatenate([weight_ref[0] * wide, weight_ref[1] * wide], axis=0)
    total = jnp.dot(both, values, preferred_element_type=F32)
    parts = []
    for at in range(0, values.shape[1], 512):
        re, im = slice(at, at + 256), slice(at + 256, at + 512)
        parts += [total[:256, re] - total[256:, im], total[:256, im] + total[256:, re]]
    return jnp.concatenate(parts, axis=1)


def gather(half, band, sources, to, sems):
    low = band < 2
    same, swap = half, 1 - half
    up_0, down_0, up_1, down_1, up_2, down_2, up_3, down_3, up_4, down_4 = sources
    table = (
        (up_0, down_0, ((0, same), (1, same), (2, same), (3, same))),
        (up_1, up_1, ((3, swap), (0, same), (1, same), (2, swap))),
        (down_1, down_1, ((1, swap), (2, same), (3, same), (0, swap))),
        (up_2, up_2, ((2, swap), (3, swap), (0, same), (1, same))),
        (down_2, down_2, ((2, same), (3, same), (0, swap), (1, swap))),
        (up_3, up_3, ((1, same), (2, swap), (3, swap), (0, same))),
        (down_3, down_3, ((3, same), (0, swap), (1, swap), (2, same))),
        (down_4, up_4, ((0, swap), (1, swap), (2, swap), (3, swap))),
    )
    waits = []
    for index, (below, above, places) in enumerate(table):
        group = by_band(band, [g for g, _ in places])
        run = by_band(band, [r for _, r in places])
        copies = [pltpu.make_async_copy(ref, to.at[group, :, run], sems.at[index]) for ref in (below, above)]
        pl.when(low)(copies[0].start)
        pl.when(jnp.logical_not(low))(copies[1].start)
        waits.append(copies[0])
    return waits


def share_kernel(at_ref, mask_ref, near_weight, far_weight, *refs):
    sources, out_ref, near, far, sems = refs[:8], refs[8], refs[9], refs[10], refs[11]
    half, band = at_ref[0], at_ref[1]
    low = band < 2
    near_waits = fetch(low, half, (sources[0:2], sources[2:4]), near, sems.at[0])
    far_waits = fetch(low, half, (sources[4:6], sources[6:8]), far, sems.at[1])
    mask = mask_ref[...].astype(F32).astype(BF16)
    for copy in near_waits:
        copy.wait()
    total = weighted(mask, jnp.where(low, 2, 1), near_weight, near[...].reshape(512, 1024))
    for copy in far_waits:
        copy.wait()
    out_ref[...] = total + weighted(mask, jnp.where(low, 3, 0), far_weight, far[...].reshape(512, 1024))


def outer_rows(at):
    return jnp.where(at[1] < 2, 0, 3)


def early_share(place, mask, near_weight, far_weight, parts):
    fixed = pl.BlockSpec((2, 256, 512), lambda i, at: (0, 0, 0))
    return pl.pallas_call(
        share_kernel,
        out_shape=jax.ShapeDtypeStruct((256, 1024), F32),
        grid_spec=pltpu.PrefetchScalarGridSpec(
            num_scalar_prefetch=1,
            grid=(1,),
            in_specs=[pl.BlockSpec((256, 64), lambda i, at: (outer_rows(at), 0)), fixed, fixed] + [ANY] * 8,
            out_specs=pl.BlockSpec((256, 1024), lambda i, at: (0, 0)),
            scratch_shapes=[pltpu.VMEM((16, 2, 16, 1024), BF16)] * 2 + [pltpu.SemaphoreType.DMA((2, 2))],
        ),
        compiler_params=GRANT,
        cost_estimate=BRIEF,
        name="early_share",
    )(place, mask, near_weight, far_weight, *[part.reshape(16, 16, 1024) for part in parts])


def edge_kernel(average, summed, at_ref, mask_ref, weight_ref, early_ref, *refs):
    sources, (block_ref, share_ref, rows, cols, sems) = refs[:8], refs[-5:]
    so_far = refs[8:9] if summed else ()
    half, band = at_ref[0], at_ref[1]
    low = band < 2
    col_waits = fetch(low, half, (sources[4:6], sources[6:8]), cols, sems.at[0])
    row_waits = fetch(low, half, (sources[0:2], sources[2:4]), rows, sems.at[1])
    mask = mask_ref[...].astype(F32).astype(BF16)
    for copy in col_waits:
        copy.wait()
    right = cols[...].reshape(512, 1024)
    share_ref[...] = (early_ref[...] + weighted(mask, band, weight_ref, right)).astype(BF16)
    for copy in row_waits:
        copy.wait()
    left = rows[...].reshape(512, 1024)
    both = jnp.concatenate([left, crossed(left)], axis=0)
    total = lax.dot_general(both, right, BOTH_LAST, preferred_element_type=F32)
    if so_far:
        total = total + so_far[0][...]
        block_ref[0] = (total[:512] * average).astype(BF16)
        block_ref[1] = (total[512:] * average).astype(BF16)
    else:
        block_ref[...] = total


def edge(average, place, mask, local, early, parts, so_far, after):
    block = jax.ShapeDtypeStruct((2, 512, 512), BF16) if so_far else jax.ShapeDtypeStruct((1024, 512), F32)
    whole = lambda shape: pl.BlockSpec(shape, lambda i, at: (0,) * len(shape))
    return pl.pallas_call(
        lambda *refs: edge_kernel(average, bool(so_far), *refs),
        out_shape=[block, jax.ShapeDtypeStruct((256, 1024), BF16)],
        grid_spec=pltpu.PrefetchScalarGridSpec(
            num_scalar_prefetch=1,
            grid=(1,),
            in_specs=[
                pl.BlockSpec((256, 64), lambda i, at: (outer_rows(at), 0)),
                pl.BlockSpec((2, 256, 512), lambda i, at: (0, outer_rows(at), 0)),
                whole((256, 1024)),
            ]
            + [ANY] * 8
            + [whole((1024, 512))] * len(so_far)
            + [ANY] * len(after),
            out_specs=[whole(block.shape), whole((256, 1024))],
            scratch_shapes=[pltpu.VMEM((16, 2, 16, 1024), BF16)] * 2 + [pltpu.SemaphoreType.DMA((2, 2))],
        ),
        compiler_params=GRANT,
        cost_estimate=BRIEF,
        name="edge",
    )(place, mask, local, early, *[part.reshape(16, 16, 1024) for part in parts], *so_far, *after)


def given_group(band):
    return jnp.where(band < 2, 1, 2)


def pair_kernel(average, at_ref, *refs):
    sources, (out_ref, section_a, section_b, held, lhs, made, sems, out_sems) = refs[:20], refs[-8:]
    half, band = at_ref[0], at_ref[1]
    waits = []
    for index in range(2):
        waits += gather(half, band, sources[index * 10 : (index + 1) * 10], held.at[index], sems.at[index])
    for copy in waits:
        copy.wait()
    kept = [pltpu.make_async_copy(held.at[i], to, out_sems.at[i]) for i, to in enumerate((section_a, section_b))]
    for copy in kept:
        copy.start()
    for index in range(2):
        left = held[index, band].reshape(512, 1024)
        lhs[:512, index * 1024 : (index + 1) * 1024] = left
        lhs[512:, index * 1024 : (index + 1) * 1024] = crossed(left)
    stores = []
    for step in range(3):
        group = step + (step >= given_group(band)).astype(jnp.int32)
        total = None
        for index in range(2):
            right = held[index, group].reshape(512, 1024)
            now = lax.dot_general(
                lhs[:, index * 1024 : (index + 1) * 1024], right, BOTH_LAST, preferred_element_type=F32
            )
            total = now if total is None else total + now
        made[step, 0] = (total[:512] * average).astype(BF16)
        made[step, 1] = (total[512:] * average).astype(BF16)
        lanes = pl.ds(pl.multiple_of(group * 512, 512), 512)
        stores.append(pltpu.make_async_copy(made.at[step], out_ref.at[:, :, lanes], out_sems.at[2 + step]))
        stores[-1].start()
    for copy in kept + stores:
        copy.wait()


def pairs(average, place, ups, downs, *after):
    parts = []
    for up, down in zip(ups, downs):
        parts += [part.reshape(16, 16, 1024) for pair in zip(up, down) for part in pair]
    section = jax.ShapeDtypeStruct((4, 16, 2, 16, 1024), BF16)
    visibility, *sections = pl.pallas_call(
        lambda *refs: pair_kernel(average, *refs),
        out_shape=[jax.ShapeDtypeStruct((2, 512, 2048), BF16), section, section],
        in_specs=[SMEM] + [ANY] * (20 + len(after)),
        out_specs=[ANY] * 3,
        scratch_shapes=[
            pltpu.VMEM((2, 4, 16, 2, 16, 1024), BF16),
            pltpu.VMEM((1024, 2048), BF16),
            pltpu.VMEM((3, 2, 512, 512), BF16),
            pltpu.SemaphoreType.DMA((2, 8)),
            pltpu.SemaphoreType.DMA((5,)),
        ],
        compiler_params=GRANT,
        cost_estimate=BRIEF,
        name="pairs",
    )(place, *parts, *after)
    return visibility, [section.reshape(2048, 1024) for section in sections]


def last_kernel(average, at_ref, left_a, left_b, right_a, right_b, block_ref, whole_ref, out_ref, lhs):
    band = at_ref[0]
    is_outer = (band == 0) | (band == 3)

    @pl.when(is_outer)
    def _():
        out_ref[...] = block_ref[...]

    @pl.when(jnp.logical_not(is_outer))
    def _():
        total = None
        for left_ref, right_ref in ((left_a, right_a), (left_b, right_b)):
            lhs[:512, :] = left_ref[...]
            lhs[512:, :] = crossed(left_ref[...])
            now = lax.dot_general(lhs[...], right_ref[...], BOTH_LAST, preferred_element_type=F32)
            total = now if total is None else total + now
        out_ref[0] = (total[:512] * average).astype(BF16)
        out_ref[1] = (total[512:] * average).astype(BF16)


def last_pairs(average, band, sections, block, visibility):
    left = pl.BlockSpec((512, 1024), lambda i, at: (at[0], 0))
    right = pl.BlockSpec((512, 1024), lambda i, at: (given_group(at[0]), 0))
    return pl.pallas_call(
        lambda *refs: last_kernel(average, *refs),
        out_shape=jax.ShapeDtypeStruct((2, 512, 2048), BF16),
        grid_spec=pltpu.PrefetchScalarGridSpec(
            num_scalar_prefetch=1,
            grid=(1,),
            in_specs=[left, left, right, right, pl.BlockSpec((2, 512, 512), lambda i, at: (0, 0, 0)), ANY],
            out_specs=pl.BlockSpec((2, 512, 512), lambda i, at: (0, 0, given_group(at[0]))),
            scratch_shapes=[pltpu.VMEM((1024, 1024), BF16)],
        ),
        input_output_aliases={6: 0},
        compiler_params=GRANT,
        cost_estimate=BRIEF,
        name="last_pairs",
    )(band.reshape(1), sections[0], sections[1], sections[0], sections[1], block, visibility)


def beam_kernel(weight_ref, section_a, section_b, out_ref):
    step = pl.program_id(0)

    def form(section_ref):
        total = jnp.dot(weight_ref[...], section_ref[...], preferred_element_type=F32)
        out_ref[:, :256] = (total[:256, :256] - total[256:, 256:]).astype(out_ref.dtype)
        out_ref[:, 256:] = (total[:256, 256:] + total[256:, :256]).astype(out_ref.dtype)

    pl.when(step < 2)(lambda: form(section_a))
    pl.when(step >= 2)(lambda: form(section_b))


def beams(weights, sections, dtype):
    formed = pl.pallas_call(
        beam_kernel,
        out_shape=jax.ShapeDtypeStruct((256, 2048), dtype),
        grid=(4,),
        in_specs=[
            pl.BlockSpec((512, 2048), lambda i: (0, 0)),
            pl.BlockSpec((2048, 512), lambda i: (0, jnp.minimum(i, 1))),
            pl.BlockSpec((2048, 512), lambda i: (0, jnp.maximum(i - 2, 0))),
        ],
        out_specs=pl.BlockSpec((256, 512), lambda i: (0, i)),
        compiler_params=GRANT,
        cost_estimate=BRIEF,
        name="beams",
    )(weights, *sections)
    return formed


def finish_kernel(at_ref, formed_ref, share_a, share_b, *refs):
    out_ref, turned = refs[-2:]
    is_outer = (at_ref[1] == 0) | (at_ref[1] == 3)
    for spectrum in range(4):
        share_ref = (share_a, share_b)[spectrum // 2]
        for part in range(2):
            at = spectrum * 512 + part * 256
            total = formed_ref[:, at : at + 256]
            at = at % 1024
            total = total + jnp.where(is_outer, share_ref[:, at : at + 256].astype(F32), 0.0)
            for lane in range(2):
                turned[lane, pl.ds(part * 4 + spectrum, 256, stride=8), :] = total[:, lane * 128 : (lane + 1) * 128]
    for lane in range(2):
        out_ref[:, lane * 128 : (lane + 1) * 128] = turned[lane].astype(BF16)


def finish(place, formed, shares, *after):
    return pl.pallas_call(
        finish_kernel,
        out_shape=jax.ShapeDtypeStruct((2048, 256), BF16),
        in_specs=[SMEM] + [VMEM] * 3 + [ANY] * len(after),
        out_specs=VMEM,
        scratch_shapes=[pltpu.VMEM((2, 2048, 128), F32)],
        compiler_params=GRANT,
        cost_estimate=BRIEF,
        name="finish",
    )(place, formed, *shares, *after)


def by_band(band, values):
    first, second, third, fourth = values
    return jnp.where(band < 2, jnp.where(band == 0, first, second), jnp.where(band == 2, third, fourth))


def shards(voltages, filter_taps, feed_gains, beam_weights, beam_mask, band_order):
    feed, band = lax.axis_index("feed"), lax.axis_index("band")
    half = lax.shift_right_logical(feed, 1) & 1
    low = band < 2
    outer = jnp.where(low, 0, 3)
    is_outer = band == outer
    everyone = (0, 1, 2, 3)
    place = jnp.stack([half, band])

    gains = feed_gains.reshape(2, 16, 2, 16, 256)
    sent_gain = lax.dynamic_index_in_dim(gains, 1 - half, 2, keepdims=False)
    entry_gains = (
        lax.ppermute(sent_gain, BOTH, hop(-3, (3,)) + hop(3, (0,))),
        lax.ppermute(sent_gain, BOTH, hop(-2, (2,)) + hop(2, (1,))),
    )
    own_weights = beam_weights[:, 0]
    from_near, from_far, from_end = hop(1, (1,)) + hop(-1, (2,)), hop(2, (0,)) + hop(-2, (3,)), hop(1, (0,)) + hop(-1, (3,))
    away = lax.dynamic_slice_in_dim(own_weights, jnp.where(low, 768, 0), 256, 1)
    near_outer = lax.ppermute(away, BOTH, from_near)
    far_outer = lax.ppermute(away, BOTH, from_far)

    spectra = channelize(voltages, filter_taps, band_order)
    got = lax.all_to_all(spectra, "feed", 0, 0, axis_index_groups=PLANE_GROUPS, tiled=True)
    got, near_outer, *entry_gains = lax.optimization_barrier((got, near_outer) + entry_gains)
    entry_gains[1], far_outer = lax.optimization_barrier((entry_gains[1], far_outer))
    ups, downs = [], []
    earlies = []
    for section in range(2):
        up, down = ([part] for part in calibrate(section, place, got, gains))
        for step, senders in enumerate((everyone, everyone, (0, 1, 2), (1, 2))):
            if step == 3:
                if earlies:
                    up[3], _ = lax.optimization_barrier((up[3], earlies[0]))
                across = (down[1], up[1], up[3], down[3], down[2], up[2], up[2], down[2])
                earlies.append(early_share(place, beam_mask, near_outer, far_outer, across))
            up.append(lax.ppermute(up[-1], BOTH, hop(1, senders)))
            down.append(lax.ppermute(down[-1], BOTH, hop(-1, tuple(3 - p for p in senders))))
            if step < 2:
                up[-1] = enter(band == 0, up[-1], entry_gains[step])
                down[-1] = enter(band == 3, down[-1], entry_gains[step])
        ups.append(up)
        downs.append(down)

    average = 1.0 / 1024
    inward = hop(-1, (1,)) + hop(1, (2,))
    so_far, shares = (), []
    for up, down, early in zip(ups, downs, earlies):
        beside = (up[1], down[1], down[3], up[3], up[0], down[0], down[4], up[4])
        after = () if so_far else (earlies[1],)
        block, share = edge(average, place, beam_mask, own_weights, early, beside, so_far, after)
        so_far = (block,)
        shares.append(lax.ppermute(share, BOTH, inward))
    received = lax.ppermute(block, BOTH, inward)


    late, _, _ = lax.optimization_barrier((own_weights, block, shares[0]))
    away = lax.dynamic_slice_in_dim(late, jnp.where(low, 512, 256), 256, 1)
    near = lax.ppermute(away, BOTH, from_near)
    far = lax.ppermute(away, BOTH, from_far)
    away = lax.dynamic_slice_in_dim(late, jnp.where(low, 256, 512), 256, 1)
    end = lax.ppermute(away, BOTH, from_end)

    visibility, sections = pairs(average, place, ups, downs, block, shares[0])
    visibility = last_pairs(average, band, sections, received, visibility)
    own_rows = weight_rows(band, beam_mask, own_weights, near, far, end)
    formed = finish(place, beams(own_rows, sections, F32), shares, visibility)
    return (visibility[:, None], formed.reshape(1, 256, 2, 4, 256))


def solution(mesh):
    return jax.shard_map(
        shards,
        mesh=mesh,
        in_specs=(
            P(None, ("band", "feed"), None),
            P(),
            P(None, "feed", "band", None),
            P(None, "feed", None, "band"),
            P(),
            P(),
        ),
        out_specs=(P(None, "feed", "band", None), P("feed", "band", None, None, None)),
        check_vma=False,
    )
```

time: 380 us -> 221 us (0.58)
  waiting for transfers between devices: 273 us -> 56.7 us
  Pallas kernels: 0 us -> 79.4 us
  starting transfers between devices: 15.1 us -> 61.7 us
  matrix products: 31.1 us -> 0 us
  other arithmetic: 20.8 us -> 0.6 us
  between operations: 14.3 us -> 1.14 us
  local copies, waits for them, and re-layouts: 24.9 us -> 17.1 us
    all_gather x1 -> x0, waiting for transfers between devices: 153 us -> none  [shards(): portion = lax.all_gather(calibrated, 'band', axis=1, tiled=True)]
    reduce_scatter x1 -> x0, waiting for transfers between devices: 89.6 us -> none  [shards(): lax.psum_scatter(jnp.stack([part_re, part_im], axis=1).astype(jnp.bfloat1...]
    pallas_call x0 -> x20, Pallas kernels: none -> 79.4 us  [the longest x2 14.1 us: edge(): pl.pallas_call(lambda *refs: edge_kernel(average, bool(so_far), *refs), o...]
    ppermute x0 -> x26, waiting for transfers between devices: none -> 56.7 us  [the longest x8 24.1 us: shards(): up.append(lax.ppermute(up[-1], BOTH, hop(1, senders)))]
    ppermute x0 -> x26, starting transfers between devices: none -> 54 us  [the longest x8 20 us: shards(): lax.ppermute(down[-1], BOTH, hop(-1, tuple((3 - p for p in senders))))]
    dot_general x16 -> x0, matrix products: 31.1 us -> none  [the longest x4 11.8 us: pair_product(): jnp.einsum('in,jn->ij', left_rows, right_rows, preferred_element_type=jnp...]
    all_to_all x1, waiting for transfers between devices: 30.6 us -> 0.01 us  [shards(): lax.all_to_all(spectra, 'feed', 0, 0, axis_index_groups=PLANE_GROUPS, til...]
    unnamed x16 -> x57, local copies, waits for them, and re-layouts: 2.32 us -> 13 us
  transfers between devices with their start and end apart: 3 -> 27, of which waited for: 3 -> 13; matrix products, arithmetic and copies ran while one was open for 3% -> 2% of each run, Pallas kernels for 0% -> 30%
where the time goes in v2:
time: 221 us; the launch traced here: 217 us
  Pallas kernels  79.4 us (36%)
  starting transfers between devices  61.7 us (28%)
  waiting for transfers between devices  56.7 us (26%)
  local copies, waits for them, and re-layouts  17.1 us (8%)
    ppermute x8, waiting for transfers between devices, shards(): up.append(lax.ppermute(up[-1], BOTH, hop(1, senders)))  24.1 us
    ppermute x8, starting transfers between devices, shards(): lax.ppermute(down[-1], BOTH, hop(-1, tuple((3 - p for p in senders))))  20 us
    ppermute x1, waiting for transfers between devices, shards(): lax.ppermute(sent_gain, BOTH, hop(-2, (2,)) + hop(2, (1,)))  14.1 us
    pallas_call x2, Pallas kernels, edge(): pl.pallas_call(lambda *refs: edge_kernel(average, bool(so_far), *refs), o...  14.1 us
    unnamed x57, local copies, waits for them, and re-layouts  13 us
    pallas_call x1, Pallas kernels, pairs(): pl.pallas_call(lambda *refs: pair_kernel(average, *refs), out_shape=[jax....  11.9 us
    pallas_call x2, Pallas kernels, early_share(): pl.pallas_call(share_kernel, out_shape=jax.ShapeDtypeStruct((256, 1024),...  11.5 us
    ppermute x8, starting transfers between devices, shards(): up.append(lax.ppermute(up[-1], BOTH, hop(1, senders)))  10.1 us
  transfers between devices with their start and end apart: 27, of which 13 were waited for; matrix products, arithmetic and copies ran while one was open for 2% of the time, Pallas kernels for 30%

profile of v2, /device:TPU:2, one launch (start us, length us, event | category | flops | bytes accessed | tf_op | source)
XLA Modules:
  0.0 216.7 jit_solution(3213125817509834879)
XLA Ops:
  0.6 8.2 %channelize.1 = bf16[32,16,2048]{2,1,0:T(8,128)(2,1)} custom-call(s32[1,64]{1,0:T(1,128)} %bitcast.102, bf16[576,256]{1,0:T(8,128)(2,1)} %constant.37.clone.tables_hbm, f32[2,128,128]{2,1,0:T(8,128)} %constant.38.clone.tw_hbm, f32[4,16384]{1,0:T(4,128)} %taps_hbm.1, bf16[2,8,114688]{2,1,0:T(8,128)(2,1)} %volts_hbm.1), custom_call_target="tpu_custom_call" | custom-call | flops 1 | bytes 1 | tf_op jit(solution)/shard_map/channelize/pallas_call | solution.py:140
  8.8 7.8 %all-to-all-start = ((bf16[32,16,2048]{2,1,0:T(8,128)(2,1)}), bf16[32,16,2048]{2,1,0:T(8,128)(2,1)S(1)}, u32[]{:S(2)}, u32[]{:S(2)}) async-start(bf16[32,16,2048]{2,1,0:T(8,128)(2,1)} %channelize.1), calls=%async_computation | async-start | bytes 4194304 | tf_op jit(solution)/shard_map/all_to_all | solution.py:598
  19.9 6.5 %collective-permute-start.1 = (bf16[2,16,16,256]{3,2,1,0:T(8,128)(2,1)S(1)}, bf16[2,16,16,256]{3,2,1,0:T(8,128)(2,1)S(1)}, u32[]{:S(2)}, u32[]{:S(2)}) collective-permute-start(bf16[2,16,16,256]{3,2,1,0:T(8,128)(2,1)S(1)} %dynamic-slice_bitcast_fusion.1), channel_id=1, source_target_pairs={{3,0},{11,8},{7,4},{15,12},{19,16},{27,24},{23,20},{31,28},{35,32}... | collective-permute-start | bytes 786440 | tf_op jit(solution)/shard_map/ppermute | solution.py:588
  28.4 4.8 %collective-permute-done.1.gain_hbm = bf16[2,16,16,256]{3,2,1,0:T(8,128)(2,1)S(1)} collective-permute-done((bf16[2,16,16,256]{3,2,1,0:T(8,128)(2,1)S(1)}, bf16[2,16,16,256]{3,2,1,0:T(8,128)(2,1)S(1)}, u32[]{:S(2)}, u32[]{:S(2)}) %collective-permute-start.1) | collective-permute-done | bytes 262176 | tf_op jit(solution)/shard_map/ppermute | solution.py:588
  33.2 14.1 %collective-permute-done.2.gain_hbm = bf16[2,16,16,256]{3,2,1,0:T(8,128)(2,1)S(1)} collective-permute-done((bf16[2,16,16,256]{3,2,1,0:T(8,128)(2,1)S(1)}, bf16[2,16,16,256]{3,2,1,0:T(8,128)(2,1)S(1)}, u32[]{:S(2)}, u32[]{:S(2)}) %collective-permute-start.2) | collective-permute-done | bytes 262176 | tf_op jit(solution)/shard_map/ppermute | solution.py:589
  51.3 4.8 %collective-permute-start.4 = (bf16[256,1024]{1,0:T(8,128)(2,1)}, bf16[256,1024]{1,0:T(8,128)(2,1)S(1)}, u32[]{:S(2)}, u32[]{:S(2)}) collective-permute-start(bf16[256,1024]{1,0:T(8,128)(2,1)} %get-tuple-element.23), channel_id=1, source_target_pairs={{0,11},{1,0},{2,1},{3,2},{8,3},{9,8},{10,9},{11,10},{4,15},{5,4},{... | collective-permute-start | bytes 1572872 | tf_op jit(solution)/shard_map/ppermute | solution.py:612
  64.1 5.0 %collective-permute-done.3.part_hbm = bf16[256,1024]{1,0:T(8,128)(2,1)S(1)} collective-permute-done((bf16[256,1024]{1,0:T(8,128)(2,1)}, bf16[256,1024]{1,0:T(8,128)(2,1)S(1)}, u32[]{:S(2)}, u32[]{:S(2)}) %collective-permute-start.3) | collective-permute-done | bytes 524320 | tf_op jit(solution)/shard_map/ppermute | solution.py:611
  72.9 5.4 %collective-permute-start.7 = (bf16[256,1024]{1,0:T(8,128)(2,1)}, bf16[256,1024]{1,0:T(8,128)(2,1)S(1)}, u32[]{:S(2)}, u32[]{:S(2)}) collective-permute-start(bf16[256,1024]{1,0:T(8,128)(2,1)} %enter.9), channel_id=1, source_target_pairs={{0,11},{1,0},{2,1},{3,2},{8,3},{9,8},{10,9},{11,10},{4,15},{5,4},{... | collective-permute-start | bytes 1572872 | tf_op jit(solution)/shard_map/ppermute | solution.py:612
  83.2 4.1 %collective-permute-start.14 = (bf16[256,1024]{1,0:T(8,128)(2,1)}, bf16[256,1024]{1,0:T(8,128)(2,1)S(1)}, u32[]{:S(2)}, u32[]{:S(2)}) collective-permute-start(bf16[256,1024]{1,0:T(8,128)(2,1)} %enter.12), channel_id=1, source_target_pairs={{0,1},{1,2},{2,3},{3,8},{8,9},{9,10},{10,11},{11,0},{4,5},{5,6},{6... | collective-permute-start | bytes 1572872 | tf_op jit(solution)/shard_map/ppermute | solution.py:611
  89.6 8.2 %collective-permute-done.5.part_hbm = bf16[256,1024]{1,0:T(8,128)(2,1)S(1)} collective-permute-done((bf16[256,1024]{1,0:T(8,128)(2,1)}, bf16[256,1024]{1,0:T(8,128)(2,1)S(1)}, u32[]{:S(2)}, u32[]{:S(2)}) %collective-permute-start.5) | collective-permute-done | bytes 524320 | tf_op jit(solution)/shard_map/ppermute | solution.py:611
  105.2 3.8 %collective-permute-done.14.part_hbm = bf16[256,1024]{1,0:T(8,128)(2,1)S(1)} collective-permute-done((bf16[256,1024]{1,0:T(8,128)(2,1)}, bf16[256,1024]{1,0:T(8,128)(2,1)S(1)}, u32[]{:S(2)}, u32[]{:S(2)}) %collective-permute-start.14) | collective-permute-done | bytes 524320 | tf_op jit(solution)/shard_map/ppermute | solution.py:611
  116.3 3.9 %collective-permute-done.8 = bf16[256,1024]{1,0:T(8,128)(2,1)S(1)} collective-permute-done((bf16[256,1024]{1,0:T(8,128)(2,1)}, bf16[256,1024]{1,0:T(8,128)(2,1)S(1)}, u32[]{:S(2)}, u32[]{:S(2)}) %collective-permute-start.8) | collective-permute-done | bytes 524320 | tf_op jit(solution)/shard_map/ppermute | solution.py:611
  123.2 5.8 %early_share.2.refs_3_ = f32[256,1024]{1,0:T(8,128)} custom-call(s32[2]{0:T(128)} %pad_add_fusion.at_ref.refs_0_, s32[1024,64]{1,0:T(8,128)} %copy.19.mask_ref.refs_1_, bf16[2,256,512]{2,1,0:T(8,128)(2,1)} %collective-permute-done.near_weight, bf16[2,256,512]{2,1,0:T(8,128)(2,1)} %collective-permute-done.6.far_weight, bf16[16,16,1024]{2,1,0:T(8,128)(2,1)} %bitcast.53, ...), custom_call_target="tpu_custom_call" | custom-call | flops 1 | bytes 1 | tf_op jit(solution)/shard_map/early_share/pallas_call | solution.py:343
  133.3 5.7 %early_share.3.refs_12_.refs_3_ = f32[256,1024]{1,0:T(8,128)} custom-call(s32[2]{0:T(128)} %pad_add_fusion.at_ref.refs_0_, s32[1024,64]{1,0:T(8,128)} %copy.19.mask_ref.refs_1_, bf16[2,256,512]{2,1,0:T(8,128)(2,1)} %collective-permute-done.near_weight, bf16[2,256,512]{2,1,0:T(8,128)(2,1)} %collective-permute-done.6.far_weight, ...), custom_call_target="tpu_custom_call" | custom-call | flops 1 | bytes 1 | tf_op jit(solution)/shard_map/early_share/pallas_call | solution.py:343
  142.6 6.8 %edge.2 = (f32[1024,512]{1,0:T(8,128)}, bf16[256,1024]{1,0:T(8,128)(2,1)}) custom-call(s32[2]{0:T(128)} %pad_add_fusion.at_ref.refs_0_, s32[1024,64]{1,0:T(8,128)} %copy.19.mask_ref.refs_1_, bf16[2,1024,512]{2,1,0:T(8,128)(2,1)} %bitcast.42, f32[256,1024]{1,0:T(8,128)} %early_share.2.refs_3_, bf16[16,16,1024]{2,1,0:T(8,128)(2,1)} %bitcast.57, ...), custom_call_target="tpu_custom_call" | custom-call | flops 1 | bytes 1 | tf_op jit(solution)/shard_map/edge/pallas_call | solution.py:387
  151.8 7.3 %edge.3 = (bf16[2,512,512]{2,1,0:T(8,128)(2,1)}, bf16[256,1024]{1,0:T(8,128)(2,1)}) custom-call(s32[2]{0:T(128)} %pad_add_fusion.at_ref.refs_0_, s32[1024,64]{1,0:T(8,128)} %copy.19.mask_ref.refs_1_, bf16[2,1024,512]{2,1,0:T(8,128)(2,1)} %bitcast.43, f32[256,1024]{1,0:T(8,128)} %early_share.3.refs_12_.refs_3_, bf16[16,16,1024]{2,1,0:T(8,128)(2,1)} %bitcast.51, ...), custom_call_target="tpu_custom_call" | custom-call | flops 1 | bytes 1 | tf_op jit(solution)/shard_map/edge/pallas_call | solution.py:387
  160.4 4.4 %collective-permute-done.20.refs_22_.share_a = bf16[256,1024]{1,0:T(8,128)(2,1)} collective-permute-done((bf16[256,1024]{1,0:T(8,128)(2,1)}, bf16[256,1024]{1,0:T(8,128)(2,1)}, u32[]{:S(2)}, u32[]{:S(2)}) %collective-permute-start.20) | collective-permute-done | bytes 524320 | tf_op jit(solution)/shard_map/ppermute | solution.py:627
  165.5 6.2 %collective-permute-start.23 = (bf16[2,256,512]{2,1,0:T(8,128)(2,1)S(1)}, bf16[2,256,512]{2,1,0:T(8,128)(2,1)S(1)}, u32[]{:S(2)}, u32[]{:S(2)}) collective-permute-start(bf16[2,256,512]{2,1,0:T(8,128)(2,1)S(1)} %get-tuple-element.43), channel_id=1, source_target_pairs={{0,2},{8,10},{4,6},{12,14},{16,18},{24,26},{20,22},{28,30},{32,34}... | collective-permute-start | bytes 1572872 | tf_op jit(solution)/shard_map/ppermute | solution.py:634
  174.8 11.9 %pairs.1 = (bf16[2,512,2048]{2,1,0:T(8,128)(2,1)}, bf16[4,16,2,16,1024]{4,3,2,1,0:T(8,128)(2,1)}, bf16[4,16,2,16,1024]{4,3,2,1,0:T(8,128)(2,1)}) custom-call(s32[2]{0:T(128)} %pad_add_fusion.at_ref.refs_0_, bf16[16,16,1024]{2,1,0:T(8,128)(2,1)} %bitcast.87, bf16[16,16,1024]{2,1,0:T(8,128)(2,1)} %bitcast.89, bf16[16,16,1024]{2,1,0:T(8,128)(2,1)} %bitcast.58, ...), custom_call_target="tpu_custom_call" | custom-call | flops 1 | bytes 1 | tf_op jit(solution)/shard_map/pairs/pallas_call | solution.py:453
  186.7 5.3 %collective-permute-done.24.end_ref = bf16[2,256,512]{2,1,0:T(8,128)(2,1)S(1)} collective-permute-done((bf16[2,256,512]{2,1,0:T(8,128)(2,1)S(1)}, bf16[2,256,512]{2,1,0:T(8,128)(2,1)S(1)}, u32[]{:S(2)}, u32[]{:S(2)}) %collective-permute-start.24) | collective-permute-done | bytes 524320 | tf_op jit(solution)/shard_map/ppermute | solution.py:636
  192.8 3.4 %weight_rows.1.weight_ref = bf16[512,2048]{1,0:T(8,128)(2,1)} custom-call(s32[1]{0:T(128)} %bitcast.refs_0_.at_ref, s32[1024,64]{1,0:T(8,128)} %copy.19.mask_ref.refs_1_, bf16[2,1024,512]{2,1,0:T(8,128)(2,1)} %bitcast.44, bf16[2,256,512]{2,1,0:T(8,128)(2,1)} %copy-done.23, bf16[2,256,512]{2,1,0:T(8,128)(2,1)} %copy-done.24, bf16[2,256,512]{2,1,0:T(8,128)(2,1)} %copy-done.25), custom_call_target="tpu_custom_call" | custom-call | flops 1 | bytes 1 | tf_op jit(solution)/shard_map/weight_rows/pallas_call | solution.py:249
  196.2 9.3 %beams.1.formed_ref = f32[256,2048]{1,0:T(8,128)} custom-call(bf16[512,2048]{1,0:T(8,128)(2,1)} %weight_rows.1.weight_ref, bf16[2048,1024]{1,0:T(8,128)(2,1)} %bitcast.36, bf16[2048,1024]{1,0:T(8,128)(2,1)} %bitcast.39), custom_call_target="tpu_custom_call" | custom-call | flops 1 | bytes 1 | tf_op jit(solution)/shard_map/beams/pallas_call | solution.py:525
  206.5 3.5 %last_pairs.1.refs_0_ = bf16[2,512,2048]{2,1,0:T(8,128)(2,1)} custom-call(s32[1]{0:T(128)} %bitcast.refs_0_.at_ref, bf16[2048,1024]{1,0:T(8,128)(2,1)} %bitcast.37, bf16[2048,1024]{1,0:T(8,128)(2,1)} %bitcast.40, bf16[2048,1024]{1,0:T(8,128)(2,1)} %bitcast.38, bf16[2048,1024]{1,0:T(8,128)(2,1)} %bitcast.41, ...), custom_call_target="tpu_custom_call", output_to_operand_aliasing={{}: (6, {})} | custom-call | flops 1 | bytes 1 | tf_op jit(solution)/shard_map/last_pairs/pallas_call | solution.py:495
  210.8 3.7 %finish.1 = bf16[2048,256]{1,0:T(8,128)(2,1)} custom-call(s32[2]{0:T(128)} %pad_add_fusion.at_ref.refs_0_, f32[256,2048]{1,0:T(8,128)} %beams.1.formed_ref, bf16[256,1024]{1,0:T(8,128)(2,1)} %collective-permute-done.20.refs_22_.share_a, bf16[256,1024]{1,0:T(8,128)(2,1)} %copy-done.22, bf16[2,512,2048]{2,1,0:T(8,128)(2,1)} %last_pairs.1.refs_0_), custom_call_target="tpu_custom_call" | custom-call | flops 1 | bytes 1 | tf_op jit(solution)/shard_map/finish/pallas_call | solution.py:559
  (112 shorter events, 65.8 us)
Async XLA Ops:
  8.8 38.5 %all-to-all-start = ((bf16[32,16,2048]{2,1,0:T(8,128)(2,1)}), bf16[32,16,2048]{2,1,0:T(8,128)(2,1)S(1)}, u32[]{:S(2)}, u32[]{:S(2)}) async-start(bf16[32,16,2048]{2,1,0:T(8,128)(2,1)} %channelize.1), calls=%async_computation | async-start | bytes 4194304 | tf_op jit(solution)/shard_map/all_to_all | solution.py:598
  18.5 28.9 %collective-permute-start = (bf16[2,256,512]{2,1,0:T(8,128)(2,1)}, bf16[2,256,512]{2,1,0:T(8,128)(2,1)}, u32[]{:S(2)}, u32[]{:S(2)}) collective-permute-start(bf16[2,256,512]{2,1,0:T(8,128)(2,1)} %dynamic-slice_bitcast_fusion), channel_id=1, source_target_pairs={{1,2},{9,10},{5,6},{13,14},{17,18},{25,26},{21,22},{29,30},{33,34}... | collective-permute-start | bytes 1572872 | tf_op jit(solution)/shard_map/ppermute | solution.py:594
  26.5 20.8 %collective-permute-start.2 = (bf16[2,16,16,256]{3,2,1,0:T(8,128)(2,1)S(1)}, bf16[2,16,16,256]{3,2,1,0:T(8,128)(2,1)S(1)}, u32[]{:S(2)}, u32[]{:S(2)}) collective-permute-start(bf16[2,16,16,256]{3,2,1,0:T(8,128)(2,1)S(1)} %dynamic-slice_bitcast_fusion.1), channel_id=1, source_target_pairs={{2,0},{10,8},{6,4},{14,12},{18,16},{26,24},{22,20},{30,28},{34,32}... | collective-permute-start | bytes 786440 | tf_op jit(solution)/shard_map/ppermute | solution.py:589
  51.3 17.8 %collective-permute-start.3 = (bf16[256,1024]{1,0:T(8,128)(2,1)}, bf16[256,1024]{1,0:T(8,128)(2,1)S(1)}, u32[]{:S(2)}, u32[]{:S(2)}) collective-permute-start(bf16[256,1024]{1,0:T(8,128)(2,1)} %get-tuple-element.22), channel_id=1, source_target_pairs={{0,1},{1,2},{2,3},{3,8},{8,9},{9,10},{10,11},{11,0},{4,5},{5,6},{6... | collective-permute-start | bytes 1572872 | tf_op jit(solution)/shard_map/ppermute | solution.py:611
  51.3 20.8 %collective-permute-start.4 = (bf16[256,1024]{1,0:T(8,128)(2,1)}, bf16[256,1024]{1,0:T(8,128)(2,1)S(1)}, u32[]{:S(2)}, u32[]{:S(2)}) collective-permute-start(bf16[256,1024]{1,0:T(8,128)(2,1)} %get-tuple-element.23), channel_id=1, source_target_pairs={{0,11},{1,0},{2,1},{3,2},{8,3},{9,8},{10,9},{11,10},{4,15},{5,4},{... | collective-permute-start | bytes 1572872 | tf_op jit(solution)/shard_map/ppermute | solution.py:612
  58.8 21.5 %collective-permute-start.12 = (bf16[256,1024]{1,0:T(8,128)(2,1)}, bf16[256,1024]{1,0:T(8,128)(2,1)S(1)}, u32[]{:S(2)}, u32[]{:S(2)}) collective-permute-start(bf16[256,1024]{1,0:T(8,128)(2,1)} %get-tuple-element.27), channel_id=1, source_target_pairs={{0,1},{1,2},{2,3},{3,8},{8,9},{9,10},{10,11},{11,0},{4,5},{5,6},{6... | collective-permute-start | bytes 1572872 | tf_op jit(solution)/shard_map/ppermute | solution.py:611
  58.8 28.5 %collective-permute-start.13 = (bf16[256,1024]{1,0:T(8,128)(2,1)}, bf16[256,1024]{1,0:T(8,128)(2,1)S(1)}, u32[]{:S(2)}, u32[]{:S(2)}) collective-permute-start(bf16[256,1024]{1,0:T(8,128)(2,1)} %get-tuple-element.28), channel_id=1, source_target_pairs={{0,11},{1,0},{2,1},{3,2},{8,3},{9,8},{10,9},{11,10},{4,15},{5,4},{... | collective-permute-start | bytes 1572872 | tf_op jit(solution)/shard_map/ppermute | solution.py:612
  62.1 27.5 %collective-permute-start.6 = (bf16[2,256,512]{2,1,0:T(8,128)(2,1)}, bf16[2,256,512]{2,1,0:T(8,128)(2,1)}, u32[]{:S(2)}, u32[]{:S(2)}) collective-permute-start(bf16[2,256,512]{2,1,0:T(8,128)(2,1)} %dynamic-slice_bitcast_fusion), channel_id=1, source_target_pairs={{0,2},{8,10},{4,6},{12,14},{16,18},{24,26},{20,22},{28,30},{32,34}... | collective-permute-start | bytes 1572872 | tf_op jit(solution)/shard_map/ppermute | solution.py:595
  72.0 25.7 %collective-permute-start.5 = (bf16[256,1024]{1,0:T(8,128)(2,1)}, bf16[256,1024]{1,0:T(8,128)(2,1)S(1)}, u32[]{:S(2)}, u32[]{:S(2)}) collective-permute-start(bf16[256,1024]{1,0:T(8,128)(2,1)} %enter.8), channel_id=1, source_target_pairs={{0,1},{1,2},{2,3},{3,8},{8,9},{9,10},{10,11},{11,0},{4,5},{5,6},{6... | collective-permute-start | bytes 1572872 | tf_op jit(solution)/shard_map/ppermute | solution.py:611
  72.9 30.1 %collective-permute-start.7 = (bf16[256,1024]{1,0:T(8,128)(2,1)}, bf16[256,1024]{1,0:T(8,128)(2,1)S(1)}, u32[]{:S(2)}, u32[]{:S(2)}) collective-permute-start(bf16[256,1024]{1,0:T(8,128)(2,1)} %enter.9), channel_id=1, source_target_pairs={{0,11},{1,0},{2,1},{3,2},{8,3},{9,8},{10,9},{11,10},{4,15},{5,4},{... | collective-permute-start | bytes 1572872 | tf_op jit(solution)/shard_map/ppermute | solution.py:612
  83.2 25.7 %collective-permute-start.14 = (bf16[256,1024]{1,0:T(8,128)(2,1)}, bf16[256,1024]{1,0:T(8,128)(2,1)S(1)}, u32[]{:S(2)}, u32[]{:S(2)}) collective-permute-start(bf16[256,1024]{1,0:T(8,128)(2,1)} %enter.12), channel_id=1, source_target_pairs={{0,1},{1,2},{2,3},{3,8},{8,9},{9,10},{10,11},{11,0},{4,5},{5,6},{6... | collective-permute-start | bytes 1572872 | tf_op jit(solution)/shard_map/ppermute | solution.py:611
  88.2 26.0 %collective-permute-start.15 = (bf16[256,1024]{1,0:T(8,128)(2,1)}, bf16[256,1024]{1,0:T(8,128)(2,1)S(1)}, u32[]{:S(2)}, u32[]{:S(2)}) collective-permute-start(bf16[256,1024]{1,0:T(8,128)(2,1)} %enter.13), channel_id=1, source_target_pairs={{0,11},{1,0},{2,1},{3,2},{8,3},{9,8},{10,9},{11,10},{4,15},{5,4},{... | collective-permute-start | bytes 1572872 | tf_op jit(solution)/shard_map/ppermute | solution.py:612
  100.6 19.6 %collective-permute-start.8 = (bf16[256,1024]{1,0:T(8,128)(2,1)}, bf16[256,1024]{1,0:T(8,128)(2,1)S(1)}, u32[]{:S(2)}, u32[]{:S(2)}) collective-permute-start(bf16[256,1024]{1,0:T(8,128)(2,1)} %enter.10), channel_id=1, source_target_pairs={{0,1},{1,2},{2,3},{8,9},{9,10},{10,11},{4,5},{5,6},{6,7},{12,13},{... | collective-permute-start | bytes 1572872 | tf_op jit(solution)/shard_map/ppermute | solution.py:611
  103.9 17.0 %collective-permute-start.9 = (bf16[256,1024]{1,0:T(8,128)(2,1)}, bf16[256,1024]{1,0:T(8,128)(2,1)S(1)}, u32[]{:S(2)}, u32[]{:S(2)}) collective-permute-start(bf16[256,1024]{1,0:T(8,128)(2,1)} %enter.11), channel_id=1, source_target_pairs={{1,0},{2,1},{3,2},{9,8},{10,9},{11,10},{5,4},{6,5},{7,6},{13,12},{... | collective-permute-start | bytes 1572872 | tf_op jit(solution)/shard_map/ppermute | solution.py:612
  111.9 18.4 %collective-permute-start.16 = (bf16[256,1024]{1,0:T(8,128)(2,1)}, bf16[256,1024]{1,0:T(8,128)(2,1)S(1)}, u32[]{:S(2)}, u32[]{:S(2)}) collective-permute-start(bf16[256,1024]{1,0:T(8,128)(2,1)} %enter.14), channel_id=1, source_target_pairs={{0,1},{1,2},{2,3},{8,9},{9,10},{10,11},{4,5},{5,6},{6,7},{12,13},{... | collective-permute-start | bytes 1572872 | tf_op jit(solution)/shard_map/ppermute | solution.py:611
  120.2 18.8 %collective-permute-start.10 = (bf16[256,1024]{1,0:T(8,128)(2,1)S(1)}, bf16[256,1024]{1,0:T(8,128)(2,1)S(1)}, u32[]{:S(2)}, u32[]{:S(2)}) collective-permute-start(bf16[256,1024]{1,0:T(8,128)(2,1)S(1)} %collective-permute-done.8), channel_id=1, source_target_pairs={{1,2},{2,3},{9,10},{10,11},{5,6},{6,7},{13,14},{14,15},{17,18},{18... | collective-permute-start | bytes 1572872 | tf_op jit(solution)/shard_map/ppermute | solution.py:611
  120.9 20.8 %collective-permute-start.11 = (bf16[256,1024]{1,0:T(8,128)(2,1)S(1)}, bf16[256,1024]{1,0:T(8,128)(2,1)S(1)}, u32[]{:S(2)}, u32[]{:S(2)}) collective-permute-start(bf16[256,1024]{1,0:T(8,128)(2,1)S(1)} %collective-permute-done.9), channel_id=1, source_target_pairs={{1,0},{2,1},{9,8},{10,9},{5,4},{6,5},{13,12},{14,13},{17,16},{18,1... | collective-permute-start | bytes 1572872 | tf_op jit(solution)/shard_map/ppermute | solution.py:612
  130.3 20.4 %collective-permute-start.18 = (bf16[256,1024]{1,0:T(8,128)(2,1)S(1)}, bf16[256,1024]{1,0:T(8,128)(2,1)S(1)}, u32[]{:S(2)}, u32[]{:S(2)}) collective-permute-start(bf16[256,1024]{1,0:T(8,128)(2,1)S(1)} %collective-permute-done.16), channel_id=1, source_target_pairs={{1,2},{2,3},{9,10},{10,11},{5,6},{6,7},{13,14},{14,15},{17,18},{18... | collective-permute-start | bytes 1572872 | tf_op jit(solution)/shard_map/ppermute | solution.py:611
  132.0 19.0 %collective-permute-start.19 = (bf16[256,1024]{1,0:T(8,128)(2,1)S(1)}, bf16[256,1024]{1,0:T(8,128)(2,1)S(1)}, u32[]{:S(2)}, u32[]{:S(2)}) collective-permute-start(bf16[256,1024]{1,0:T(8,128)(2,1)S(1)} %collective-permute-done.17), channel_id=1, source_target_pairs={{1,0},{2,1},{9,8},{10,9},{5,4},{6,5},{13,12},{14,13},{17,16},{18,1... | collective-permute-start | bytes 1572872 | tf_op jit(solution)/shard_map/ppermute | solution.py:612
  159.1 46.4 %collective-permute-start.21 = (bf16[2,512,512]{2,1,0:T(8,128)(2,1)}, bf16[2,512,512]{2,1,0:T(8,128)(2,1)S(1)}, u32[]{:S(2)}, u32[]{:S(2)}) collective-permute-start(bf16[2,512,512]{2,1,0:T(8,128)(2,1)} %get-tuple-element.33.refs_21_), channel_id=1, source_target_pairs={{1,0},{9,8},{5,4},{13,12},{17,16},{25,24},{21,20},{29,28},{33,32},... | collective-permute-start | bytes 3145736 | tf_op jit(solution)/shard_map/ppermute | solution.py:628
  164.8 21.8 %collective-permute-start.22 = (bf16[2,256,512]{2,1,0:T(8,128)(2,1)S(1)}, bf16[2,256,512]{2,1,0:T(8,128)(2,1)S(1)}, u32[]{:S(2)}, u32[]{:S(2)}) collective-permute-start(bf16[2,256,512]{2,1,0:T(8,128)(2,1)S(1)} %get-tuple-element.43), channel_id=1, source_target_pairs={{1,2},{9,10},{5,6},{13,14},{17,18},{25,26},{21,22},{29,30},{33,34}... | collective-permute-start | bytes 1572872 | tf_op jit(solution)/shard_map/ppermute | solution.py:633
  165.5 21.2 %collective-permute-start.23 = (bf16[2,256,512]{2,1,0:T(8,128)(2,1)S(1)}, bf16[2,256,512]{2,1,0:T(8,128)(2,1)S(1)}, u32[]{:S(2)}, u32[]{:S(2)}) collective-permute-start(bf16[2,256,512]{2,1,0:T(8,128)(2,1)S(1)} %get-tuple-element.43), channel_id=1, source_target_pairs={{0,2},{8,10},{4,6},{12,14},{16,18},{24,26},{20,22},{28,30},{32,34}... | collective-permute-start | bytes 1572872 | tf_op jit(solution)/shard_map/ppermute | solution.py:634
  171.7 20.3 %collective-permute-start.24 = (bf16[2,256,512]{2,1,0:T(8,128)(2,1)S(1)}, bf16[2,256,512]{2,1,0:T(8,128)(2,1)S(1)}, u32[]{:S(2)}, u32[]{:S(2)}) collective-permute-start(bf16[2,256,512]{2,1,0:T(8,128)(2,1)S(1)} %get-tuple-element.42), channel_id=1, source_target_pairs={{0,1},{8,9},{4,5},{12,13},{16,17},{24,25},{20,21},{28,29},{32,33},... | collective-permute-start | bytes 1572872 | tf_op jit(solution)/shard_map/ppermute | solution.py:636
  173.2 36.8 %collective-permute-start.25 = (bf16[256,1024]{1,0:T(8,128)(2,1)S(1)}, bf16[256,1024]{1,0:T(8,128)(2,1)S(1)}, u32[]{:S(2)}, u32[]{:S(2)}) collective-permute-start(bf16[256,1024]{1,0:T(8,128)(2,1)S(1)} %copy-done.27), channel_id=1, source_target_pairs={{1,0},{9,8},{5,4},{13,12},{17,16},{25,24},{21,20},{29,28},{33,32},... | collective-permute-start | bytes 1572872 | tf_op jit(solution)/shard_map/ppermute | solution.py:627
  (31 other events, 208.5 us)

commit v3 on v2

--- a/solution.py
+++ b/solution.py
@@ -232,39 +232,6 @@
     return jnp.dot(mask, (tile == column).astype(BF16), preferred_element_type=F32).astype(BF16)
 
 
-def weights_kernel(at_ref, mask_ref, local_ref, near_ref, far_ref, end_ref, out_ref):
-    band = at_ref[0]
-    low = band < 2
-    groups = (band, jnp.where(low, 2, 1), jnp.where(low, 3, 0), jnp.where(low, 1 - band, 5 - band))
-    mask = mask_ref[...].astype(F32).astype(BF16)
-    for group, src_ref in zip(groups, (local_ref, near_ref, far_ref, end_ref)):
-        lanes = pl.ds(pl.multiple_of(group * 512, 512), 512)
-        wide = spread(mask, group)
-        for part in range(2):
-            out_ref[part * 256 : (part + 1) * 256, lanes] = src_ref[part] * wide
-
-
-def weight_rows(band, mask, local, *others):
-    fixed = pl.BlockSpec((2, 256, 512), lambda i, at: (0, 0, 0))
-    return pl.pallas_call(
-        weights_kernel,
-        out_shape=jax.ShapeDtypeStruct((512, 2048), BF16),
-        grid_spec=pltpu.PrefetchScalarGridSpec(
-            num_scalar_prefetch=1,
-            grid=(1,),
-            in_specs=[
-                pl.BlockSpec((256, 64), lambda i, at: (at[0], 0)),
-                pl.BlockSpec((2, 256, 512), lambda i, at: (0, at[0], 0)),
-            ]
-            + [fixed] * 3,
-            out_specs=pl.BlockSpec((512, 2048), lambda i, at: (0, 0)),
-        ),
-        compiler_params=GRANT,
-        cost_estimate=BRIEF,
-        name="weight_rows",
-    )(band.reshape(1), mask, local, *others)
-
-
 def crossed(left):
     parts = []
     for at in range(0, left.shape[1], 512):
@@ -308,127 +275,126 @@
         (down_3, down_3, ((3, same), (0, swap), (1, swap), (2, same))),
         (down_4, up_4, ((0, swap), (1, swap), (2, swap), (3, swap))),
     )
-    waits = []
-    for index, (below, above, places) in enumerate(table):
+    table = (table[0], table[7]) + table[1:7]
+    for below, above, places in table:
         group = by_band(band, [g for g, _ in places])
         run = by_band(band, [r for _, r in places])
-        copies = [pltpu.make_async_copy(ref, to.at[group, :, run], sems.at[index]) for ref in (below, above)]
+        sem = sems.at[group * 2 + run]
+        copies = [pltpu.make_async_copy(ref, to.at[group, :, run], sem) for ref in (below, above)]
         pl.when(low)(copies[0].start)
         pl.when(jnp.logical_not(low))(copies[1].start)
-        waits.append(copies[0])
-    return waits
-
-
-def share_kernel(at_ref, mask_ref, near_weight, far_weight, *refs):
-    sources, out_ref, near, far, sems = refs[:8], refs[8], refs[9], refs[10], refs[11]
+
+
+def outer_band(band):
+    return jnp.where(band < 2, 0, 3)
+
+
+def share_kernel(at_ref, mask_ref, near_hbm, far_hbm, local_hbm, *refs):
+    sources, (out_ref, held, weights, sems, weight_sems) = refs[:12], refs[-5:]
     half, band = at_ref[0], at_ref[1]
     low = band < 2
-    near_waits = fetch(low, half, (sources[0:2], sources[2:4]), near, sems.at[0])
-    far_waits = fetch(low, half, (sources[4:6], sources[6:8]), far, sems.at[1])
+    rows = pl.ds(pl.multiple_of(outer_band(band) * 256, 256), 256)
+    loads = [
+        pltpu.make_async_copy(ref, weights.at[index], weight_sems.at[index])
+        for index, ref in enumerate((near_hbm, far_hbm, local_hbm.at[:, rows, :]))
+    ]
+    for copy in loads:
+        copy.start()
+    for index in range(3):
+        at = index * 4
+        loads += fetch(low, half, (sources[at : at + 2], sources[at + 2 : at + 4]), held.at[index], sems.at[index])
     mask = mask_ref[...].astype(F32).astype(BF16)
-    for copy in near_waits:
-        copy.wait()
-    total = weighted(mask, jnp.where(low, 2, 1), near_weight, near[...].reshape(512, 1024))
-    for copy in far_waits:
-        copy.wait()
-    out_ref[...] = total + weighted(mask, jnp.where(low, 3, 0), far_weight, far[...].reshape(512, 1024))
-
-
-def outer_rows(at):
-    return jnp.where(at[1] < 2, 0, 3)
-
-
-def early_share(place, mask, near_weight, far_weight, parts):
-    fixed = pl.BlockSpec((2, 256, 512), lambda i, at: (0, 0, 0))
+    total = None
+    for index, group in enumerate((jnp.where(low, 2, 1), jnp.where(low, 3, 0), band)):
+        for copy in (loads[index], loads[3 + 2 * index], loads[4 + 2 * index]):
+            copy.wait()
+        now = weighted(mask, group, weights.at[index], held[index].reshape(512, 1024))
+        total = now if total is None else total + now
+    out_ref[...] = total.astype(BF16)
+
+
+def outer_share(place, mask, near, far, local, up, down):
+    sources = (down[1], up[1], up[3], down[3], down[2], up[2], up[2], down[2], up[0], down[0], down[4], up[4])
     return pl.pallas_call(
         share_kernel,
-        out_shape=jax.ShapeDtypeStruct((256, 1024), F32),
+        out_shape=jax.ShapeDtypeStruct((256, 1024), BF16),
         grid_spec=pltpu.PrefetchScalarGridSpec(
             num_scalar_prefetch=1,
             grid=(1,),
-            in_specs=[pl.BlockSpec((256, 64), lambda i, at: (outer_rows(at), 0)), fixed, fixed] + [ANY] * 8,
+            in_specs=[pl.BlockSpec((256, 64), lambda i, at: (outer_band(at[1]), 0))] + [ANY] * 15,
             out_specs=pl.BlockSpec((256, 1024), lambda i, at: (0, 0)),
-            scratch_shapes=[pltpu.VMEM((16, 2, 16, 1024), BF16)] * 2 + [pltpu.SemaphoreType.DMA((2, 2))],
+            scratch_shapes=[
+                pltpu.VMEM((3, 16, 2, 16, 1024), BF16),
+                pltpu.VMEM((3, 2, 256, 512), BF16),
+                pltpu.SemaphoreType.DMA((3, 2)),
+                pltpu.SemaphoreType.DMA((3,)),
+            ],
         ),
         compiler_params=GRANT,
         cost_estimate=BRIEF,
-        name="early_share",
-    )(place, mask, near_weight, far_weight, *[part.reshape(16, 16, 1024) for part in parts])
-
-
-def edge_kernel(average, summed, at_ref, mask_ref, weight_ref, early_ref, *refs):
-    sources, (block_ref, share_ref, rows, cols, sems) = refs[:8], refs[-5:]
-    so_far = refs[8:9] if summed else ()
+        name="outer_share",
+    )(place, mask, near, far, local, *[part.reshape(16, 16, 1024) for part in sources])
+
+
+def edge_kernel(average, at_ref, *refs):
+    sources, (block_ref, far, own, sems) = refs[:16], refs[-4:]
+    half, low = at_ref[0], at_ref[1] < 2
+    waits = []
+    for section in range(2):
+        parts = sources[section * 8 : section * 8 + 8]
+        waits.append(
+            fetch(low, half, (parts[0:2], parts[2:4]), far.at[section], sems.at[section, 0])
+            + fetch(low, half, (parts[4:6], parts[6:8]), own.at[section], sems.at[section, 1])
+        )
+    total = None
+    for section in range(2):
+        for copy in waits[section]:
+            copy.wait()
+        left, right = own[section].reshape(512, 1024), far[section].reshape(512, 1024)
+        both = jnp.concatenate([left, crossed(left)], axis=0)
+        now = lax.dot_general(both, right, BOTH_LAST, preferred_element_type=F32)
+        total = now if total is None else total + now
+    block_ref[0] = (total[:512] * average).astype(BF16)
+    block_ref[1] = (total[512:] * average).astype(BF16)
+
+
+def edge(average, place, ups, downs, *after):
+    parts = []
+    for up, down in zip(ups, downs):
+        parts += [up[1], down[1], down[3], up[3], up[0], down[0], down[4], up[4]]
+    return pl.pallas_call(
+        lambda *refs: edge_kernel(average, *refs),
+        out_shape=jax.ShapeDtypeStruct((2, 512, 512), BF16),
+        in_specs=[SMEM] + [ANY] * (16 + len(after)),
+        out_specs=VMEM,
+        scratch_shapes=[pltpu.VMEM((2, 16, 2, 16, 1024), BF16)] * 2 + [pltpu.SemaphoreType.DMA((2, 2, 2))],
+        compiler_params=GRANT,
+        cost_estimate=BRIEF,
+        name="edge",
+    )(place, *[part.reshape(16, 16, 1024) for part in parts], *after)
+
+
+def pair_kernel(average, at_ref, *refs):
+    sources, block_hbm, (out_ref, section_a, section_b, held, lhs, made, sems, out_sems) = refs[:20], refs[20], refs[-8:]
     half, band = at_ref[0], at_ref[1]
-    low = band < 2
-    col_waits = fetch(low, half, (sources[4:6], sources[6:8]), cols, sems.at[0])
-    row_waits = fetch(low, half, (sources[0:2], sources[2:4]), rows, sems.at[1])
-    mask = mask_ref[...].astype(F32).astype(BF16)
-    for copy in col_waits:
-        copy.wait()
-    right = cols[...].reshape(512, 1024)
-    share_ref[...] = (early_ref[...] + weighted(mask, band, weight_ref, right)).astype(BF16)
-    for copy in row_waits:
-        copy.wait()
-    left = rows[...].reshape(512, 1024)
-    both = jnp.concatenate([left, crossed(left)], axis=0)
-    total = lax.dot_general(both, right, BOTH_LAST, preferred_element_type=F32)
-    if so_far:
-        total = total + so_far[0][...]
-        block_ref[0] = (total[:512] * average).astype(BF16)
-        block_ref[1] = (total[512:] * average).astype(BF16)
-    else:
-        block_ref[...] = total
-
-
-def edge(average, place, mask, local, early, parts, so_far, after):
-    block = jax.ShapeDtypeStruct((2, 512, 512), BF16) if so_far else jax.ShapeDtypeStruct((1024, 512), F32)
-    whole = lambda shape: pl.BlockSpec(shape, lambda i, at: (0,) * len(shape))
-    return pl.pallas_call(
-        lambda *refs: edge_kernel(average, bool(so_far), *refs),
-        out_shape=[block, jax.ShapeDtypeStruct((256, 1024), BF16)],
-        grid_spec=pltpu.PrefetchScalarGridSpec(
-            num_scalar_prefetch=1,
-            grid=(1,),
-            in_specs=[
-                pl.BlockSpec((256, 64), lambda i, at: (outer_rows(at), 0)),
-                pl.BlockSpec((2, 256, 512), lambda i, at: (0, outer_rows(at), 0)),
-                whole((256, 1024)),
-            ]
-            + [ANY] * 8
-            + [whole((1024, 512))] * len(so_far)
-            + [ANY] * len(after),
-            out_specs=[whole(block.shape), whole((256, 1024))],
-            scratch_shapes=[pltpu.VMEM((16, 2, 16, 1024), BF16)] * 2 + [pltpu.SemaphoreType.DMA((2, 2))],
-        ),
-        compiler_params=GRANT,
-        cost_estimate=BRIEF,
-        name="edge",
-    )(place, mask, local, early, *[part.reshape(16, 16, 1024) for part in parts], *so_far, *after)
-
-
-def given_group(band):
-    return jnp.where(band < 2, 1, 2)
-
-
-def pair_kernel(average, at_ref, *refs):
-    sources, (out_ref, section_a, section_b, held, lhs, made, sems, out_sems) = refs[:20], refs[-8:]
-    half, band = at_ref[0], at_ref[1]
-    waits = []
+    partner = band ^ 1
+    inner = (band == 1) | (band == 2)
+    load = pltpu.make_async_copy(block_hbm, made.at[3], out_sems.at[5])
+    load.start()
     for index in range(2):
-        waits += gather(half, band, sources[index * 10 : (index + 1) * 10], held.at[index], sems.at[index])
-    for copy in waits:
-        copy.wait()
-    kept = [pltpu.make_async_copy(held.at[i], to, out_sems.at[i]) for i, to in enumerate((section_a, section_b))]
-    for copy in kept:
-        copy.start()
+        gather(half, band, sources[index * 10 : (index + 1) * 10], held.at[index], sems.at[index])
+
+    def arrived(index, group):
+        for run in range(2):
+            pltpu.make_async_copy(sources[0], held.at[index, group, :, run], sems.at[index, group * 2 + run]).wait()
+
     for index in range(2):
+        arrived(index, band)
         left = held[index, band].reshape(512, 1024)
         lhs[:512, index * 1024 : (index + 1) * 1024] = left
         lhs[512:, index * 1024 : (index + 1) * 1024] = crossed(left)
-    stores = []
-    for step in range(3):
-        group = step + (step >= given_group(band)).astype(jnp.int32)
+
+    def columns(step, group):
         total = None
         for index in range(2):
             right = held[index, group].reshape(512, 1024)
@@ -439,13 +405,32 @@
         made[step, 0] = (total[:512] * average).astype(BF16)
         made[step, 1] = (total[512:] * average).astype(BF16)
         lanes = pl.ds(pl.multiple_of(group * 512, 512), 512)
-        stores.append(pltpu.make_async_copy(made.at[step], out_ref.at[:, :, lanes], out_sems.at[2 + step]))
-        stores[-1].start()
+        store = pltpu.make_async_copy(made.at[step], out_ref.at[:, :, lanes], out_sems.at[2 + step])
+        store.start()
+        return store
+
+    stores = [columns(0, band)]
+    for group in (band ^ 2, band ^ 3, partner):
+        for index in range(2):
+            arrived(index, group)
+    kept = [pltpu.make_async_copy(held.at[i], to, out_sems.at[i]) for i, to in enumerate((section_a, section_b))]
+    for copy in kept:
+        copy.start()
+    stores += [columns(1, band ^ 2), columns(2, band ^ 3)]
+    load.wait()
+
+    @pl.when(inner)
+    def _():
+        lanes = pl.ds(pl.multiple_of(partner * 512, 512), 512)
+        store = pltpu.make_async_copy(made.at[3], out_ref.at[:, :, lanes], out_sems.at[5])
+        store.start()
+        store.wait()
+
     for copy in kept + stores:
         copy.wait()
 
 
-def pairs(average, place, ups, downs, *after):
+def pairs(average, place, ups, downs, block, *after):
     parts = []
     for up, down in zip(ups, downs):
         parts += [part.reshape(16, 16, 1024) for pair in zip(up, down) for part in pair]
@@ -453,90 +438,103 @@
     visibility, *sections = pl.pallas_call(
         lambda *refs: pair_kernel(average, *refs),
         out_shape=[jax.ShapeDtypeStruct((2, 512, 2048), BF16), section, section],
-        in_specs=[SMEM] + [ANY] * (20 + len(after)),
+        in_specs=[SMEM] + [ANY] * (21 + len(after)),
         out_specs=[ANY] * 3,
         scratch_shapes=[
             pltpu.VMEM((2, 4, 16, 2, 16, 1024), BF16),
             pltpu.VMEM((1024, 2048), BF16),
-            pltpu.VMEM((3, 2, 512, 512), BF16),
+            pltpu.VMEM((4, 2, 512, 512), BF16),
             pltpu.SemaphoreType.DMA((2, 8)),
-            pltpu.SemaphoreType.DMA((5,)),
+            pltpu.SemaphoreType.DMA((6,)),
         ],
         compiler_params=GRANT,
         cost_estimate=BRIEF,
         name="pairs",
-    )(place, *parts, *after)
+    )(place, *parts, block, *after)
     return visibility, [section.reshape(2048, 1024) for section in sections]
 
 
-def last_kernel(average, at_ref, left_a, left_b, right_a, right_b, block_ref, whole_ref, out_ref, lhs):
-    band = at_ref[0]
-    is_outer = (band == 0) | (band == 3)
-
-    @pl.when(is_outer)
+def last_kernel(at_ref, block_hbm, whole_hbm, out_hbm, block, turned, sem):
+    band = at_ref[1]
+
+    @pl.when((band == 0) | (band == 3))
     def _():
-        out_ref[...] = block_ref[...]
-
-    @pl.when(jnp.logical_not(is_outer))
+        lanes = pl.ds(pl.multiple_of((band ^ 1) * 512, 512), 512)
+        load = pltpu.make_async_copy(block_hbm, block, sem)
+        load.start()
+        load.wait()
+        turned[0] = block[0].astype(F32).T.astype(BF16)
+        turned[1] = (-block[1].astype(F32).T).astype(BF16)
+        store = pltpu.make_async_copy(turned, out_hbm.at[:, :, lanes], sem)
+        store.start()
+        store.wait()
+
+
+def last_pairs(place, block, visibility):
+    return pl.pallas_call(
+        last_kernel,
+        out_shape=jax.ShapeDtypeStruct((2, 512, 2048), BF16),
+        in_specs=[SMEM, ANY, ANY],
+        out_specs=ANY,
+        scratch_shapes=[pltpu.VMEM((2, 512, 512), BF16)] * 2 + [pltpu.SemaphoreType.DMA],
+        input_output_aliases={2: 0},
+        compiler_params=GRANT,
+        cost_estimate=BRIEF,
+        name="last_pairs",
+    )(place, block, visibility)
+
+
+def beam_kernel(at_ref, mask_ref, local_ref, near_ref, far_ref, end_ref, section_a, section_b, out_ref, weights):
+    step, band = pl.program_id(0), at_ref[1]
+    low = band < 2
+
+    @pl.when(step == 0)
     def _():
-        total = None
-        for left_ref, right_ref in ((left_a, right_a), (left_b, right_b)):
-            lhs[:512, :] = left_ref[...]
-            lhs[512:, :] = crossed(left_ref[...])
-            now = lax.dot_general(lhs[...], right_ref[...], BOTH_LAST, preferred_element_type=F32)
-            total = now if total is None else total + now
-        out_ref[0] = (total[:512] * average).astype(BF16)
-        out_ref[1] = (total[512:] * average).astype(BF16)
-
-
-def last_pairs(average, band, sections, block, visibility):
-    left = pl.BlockSpec((512, 1024), lambda i, at: (at[0], 0))
-    right = pl.BlockSpec((512, 1024), lambda i, at: (given_group(at[0]), 0))
-    return pl.pallas_call(
-        lambda *refs: last_kernel(average, *refs),
-        out_shape=jax.ShapeDtypeStruct((2, 512, 2048), BF16),
+        mask = mask_ref[...].astype(F32).astype(BF16)
+        pieces = (
+            (band, local_ref),
+            (jnp.where(low, 2, 1), near_ref),
+            (jnp.where(low, 3, 0), far_ref),
+            (jnp.where(low, 1 - band, 5 - band), end_ref),
+        )
+        for group, piece_ref in pieces:
+            lanes = pl.ds(pl.multiple_of(group * 512, 512), 512)
+            wide = spread(mask, group)
+            for part in range(2):
+                weights[part * 256 : (part + 1) * 256, lanes] = piece_ref[part] * wide
+
+    def form(section_ref):
+        total = jnp.dot(weights[...], section_ref[...], preferred_element_type=F32)
+        out_ref[:, :256] = total[:256, :256] - total[256:, 256:]
+        out_ref[:, 256:] = total[:256, 256:] + total[256:, :256]
+
+    pl.when(step < 2)(lambda: form(section_a))
+    pl.when(step >= 2)(lambda: form(section_b))
+
+
+def beams(place, mask, local, others, sections):
+    return pl.pallas_call(
+        beam_kernel,
+        out_shape=jax.ShapeDtypeStruct((256, 2048), F32),
         grid_spec=pltpu.PrefetchScalarGridSpec(
             num_scalar_prefetch=1,
-            grid=(1,),
-            in_specs=[left, left, right, right, pl.BlockSpec((2, 512, 512), lambda i, at: (0, 0, 0)), ANY],
-            out_specs=pl.BlockSpec((2, 512, 512), lambda i, at: (0, 0, given_group(at[0]))),
-            scratch_shapes=[pltpu.VMEM((1024, 1024), BF16)],
+            grid=(4,),
+            in_specs=[
+                pl.BlockSpec((256, 64), lambda i, at: (at[1], 0)),
+                pl.BlockSpec((2, 256, 512), lambda i, at: (0, at[1], 0)),
+            ]
+            + [pl.BlockSpec((2, 256, 512), lambda i, at: (0, 0, 0))] * 3
+            + [
+                pl.BlockSpec((2048, 512), lambda i, at: (0, jnp.minimum(i, 1))),
+                pl.BlockSpec((2048, 512), lambda i, at: (0, jnp.maximum(i - 2, 0))),
+            ],
+            out_specs=pl.BlockSpec((256, 512), lambda i, at: (0, i)),
+            scratch_shapes=[pltpu.VMEM((512, 2048), BF16)],
         ),
-        input_output_aliases={6: 0},
-        compiler_params=GRANT,
-        cost_estimate=BRIEF,
-        name="last_pairs",
-    )(band.reshape(1), sections[0], sections[1], sections[0], sections[1], block, visibility)
-
-
-def beam_kernel(weight_ref, section_a, section_b, out_ref):
-    step = pl.program_id(0)
-
-    def form(section_ref):
-        total = jnp.dot(weight_ref[...], section_ref[...], preferred_element_type=F32)
-        out_ref[:, :256] = (total[:256, :256] - total[256:, 256:]).astype(out_ref.dtype)
-        out_ref[:, 256:] = (total[:256, 256:] + total[256:, :256]).astype(out_ref.dtype)
-
-    pl.when(step < 2)(lambda: form(section_a))
-    pl.when(step >= 2)(lambda: form(section_b))
-
-
-def beams(weights, sections, dtype):
-    formed = pl.pallas_call(
-        beam_kernel,
-        out_shape=jax.ShapeDtypeStruct((256, 2048), dtype),
-        grid=(4,),
-        in_specs=[
-            pl.BlockSpec((512, 2048), lambda i: (0, 0)),
-            pl.BlockSpec((2048, 512), lambda i: (0, jnp.minimum(i, 1))),
-            pl.BlockSpec((2048, 512), lambda i: (0, jnp.maximum(i - 2, 0))),
-        ],
-        out_specs=pl.BlockSpec((256, 512), lambda i: (0, i)),
         compiler_params=GRANT,
         cost_estimate=BRIEF,
         name="beams",
-    )(weights, *sections)
-    return formed
+    )(place, mask, local, *others, *sections)
 
 
 def finish_kernel(at_ref, formed_ref, share_a, share_b, *refs):
@@ -552,13 +550,13 @@
             for lane in range(2):
                 turned[lane, pl.ds(part * 4 + spectrum, 256, stride=8), :] = total[:, lane * 128 : (lane + 1) * 128]
     for lane in range(2):
-        out_ref[:, lane * 128 : (lane + 1) * 128] = turned[lane].astype(BF16)
+        out_ref[:, :, lane * 128 : (lane + 1) * 128] = turned[lane].reshape(512, 4, 128).astype(BF16)
 
 
 def finish(place, formed, shares, *after):
     return pl.pallas_call(
         finish_kernel,
-        out_shape=jax.ShapeDtypeStruct((2048, 256), BF16),
+        out_shape=jax.ShapeDtypeStruct((512, 4, 256), BF16),
         in_specs=[SMEM] + [VMEM] * 3 + [ANY] * len(after),
         out_specs=VMEM,
         scratch_shapes=[pltpu.VMEM((2, 2048, 128), F32)],
@@ -577,8 +575,6 @@
     feed, band = lax.axis_index("feed"), lax.axis_index("band")
     half = lax.shift_right_logical(feed, 1) & 1
     low = band < 2
-    outer = jnp.where(low, 0, 3)
-    is_outer = band == outer
     everyone = (0, 1, 2, 3)
     place = jnp.stack([half, band])
 
@@ -599,15 +595,9 @@
     got, near_outer, *entry_gains = lax.optimization_barrier((got, near_outer) + entry_gains)
     entry_gains[1], far_outer = lax.optimization_barrier((entry_gains[1], far_outer))
     ups, downs = [], []
-    earlies = []
     for section in range(2):
         up, down = ([part] for part in calibrate(section, place, got, gains))
         for step, senders in enumerate((everyone, everyone, (0, 1, 2), (1, 2))):
-            if step == 3:
-                if earlies:
-                    up[3], _ = lax.optimization_barrier((up[3], earlies[0]))
-                across = (down[1], up[1], up[3], down[3], down[2], up[2], up[2], down[2])
-                earlies.append(early_share(place, beam_mask, near_outer, far_outer, across))
             up.append(lax.ppermute(up[-1], BOTH, hop(1, senders)))
             down.append(lax.ppermute(down[-1], BOTH, hop(-1, tuple(3 - p for p in senders))))
             if step < 2:
@@ -618,15 +608,14 @@
 
     average = 1.0 / 1024
     inward = hop(-1, (1,)) + hop(1, (2,))
-    so_far, shares = (), []
-    for up, down, early in zip(ups, downs, earlies):
-        beside = (up[1], down[1], down[3], up[3], up[0], down[0], down[4], up[4])
-        after = () if so_far else (earlies[1],)
-        block, share = edge(average, place, beam_mask, own_weights, early, beside, so_far, after)
-        so_far = (block,)
-        shares.append(lax.ppermute(share, BOTH, inward))
+    shares = []
+    for up, down in zip(ups, downs):
+        shares.append(outer_share(place, beam_mask, near_outer, far_outer, own_weights, up, down))
+        if len(shares) == 1:
+            block = edge(average, place, ups, downs, shares[0])
+    shares[1], _ = lax.optimization_barrier((shares[1], block))
     received = lax.ppermute(block, BOTH, inward)
-
+    shares = [lax.ppermute(share, BOTH, inward) for share in shares]
 
     late, _, _ = lax.optimization_barrier((own_weights, block, shares[0]))
     away = lax.dynamic_slice_in_dim(late, jnp.where(low, 512, 256), 256, 1)
@@ -636,9 +625,8 @@
     end = lax.ppermute(away, BOTH, from_end)
 
     visibility, sections = pairs(average, place, ups, downs, block, shares[0])
-    visibility = last_pairs(average, band, sections, received, visibility)
-    own_rows = weight_rows(band, beam_mask, own_weights, near, far, end)
-    formed = finish(place, beams(own_rows, sections, F32), shares, visibility)
+    visibility = last_pairs(place, received, visibility)
+    formed = finish(place, beams(place, beam_mask, own_weights, (near, far, end), sections), shares, visibility)
     return (visibility[:, None], formed.reshape(1, 256, 2, 4, 256))
 
 

time: 221 us -> 212 us (0.959); the launches traced: 217 us -> 211 us
  Pallas kernels: 79.4 us -> 69.9 us
  waiting for transfers between devices: 56.7 us -> 64.6 us
  local copies, waits for them, and re-layouts: 17.1 us -> 14.4 us
    pallas_call x8 -> x6, Pallas kernels: 45.6 us -> 36.4 us  [the longest x2 12.6 us: outer_share(): pl.pallas_call(share_kernel, out_shape=jax.ShapeDtypeStruct((256, 1024),...]
    ppermute x8, waiting for transfers between devices: 24.1 us -> 31 us  [shards(): up.append(lax.ppermute(up[-1], BOTH, hop(1, senders)))]
    ppermute x1, waiting for transfers between devices: 5.31 us -> 0.01 us  [shards(): end = lax.ppermute(away, BOTH, from_end)]
    ppermute x8, waiting for transfers between devices: 4.04 us -> 8.64 us  [shards(): lax.ppermute(down[-1], BOTH, hop(-1, tuple((3 - p for p in senders))))]
    unnamed x57 -> x51, local copies, waits for them, and re-layouts: 13 us -> 12.4 us
  transfers between devices with their start and end apart: 27 -> 27, of which waited for: 13 -> 12; matrix products, arithmetic and copies ran while one was open for 2% -> 2% of each run, Pallas kernels for 30% -> 26%
where the time goes in v3:
time: 212 us; the launch traced here: 211 us
  Pallas kernels  69.9 us (33%)
  waiting for transfers between devices  64.6 us (30%)
  starting transfers between devices  60.3 us (28%)
  local copies, waits for them, and re-layouts  14.4 us (7%)
    ppermute x8, waiting for transfers between devices, shards(): up.append(lax.ppermute(up[-1], BOTH, hop(1, senders)))  31 us
    ppermute x8, starting transfers between devices, shards(): lax.ppermute(down[-1], BOTH, hop(-1, tuple((3 - p for p in senders))))  20 us
    ppermute x1, waiting for transfers between devices, shards(): lax.ppermute(sent_gain, BOTH, hop(-2, (2,)) + hop(2, (1,)))  14.1 us
    pallas_call x2, Pallas kernels, outer_share(): pl.pallas_call(share_kernel, out_shape=jax.ShapeDtypeStruct((256, 1024),...  12.6 us
    unnamed x51, local copies, waits for them, and re-layouts  12.4 us
    pallas_call x1, Pallas kernels, pairs(): pl.pallas_call(lambda *refs: pair_kernel(average, *refs), out_shape=[jax....  11.5 us
    ppermute x8, starting transfers between devices, shards(): up.append(lax.ppermute(up[-1], BOTH, hop(1, senders)))  10.9 us
    pallas_call x1, Pallas kernels, beams(): pl.pallas_call(beam_kernel, out_shape=jax.ShapeDtypeStruct((256, 2048), F...  10.4 us
  transfers between devices with their start and end apart: 27, of which 12 were waited for; matrix products, arithmetic and copies ran while one was open for 2% of the time, Pallas kernels for 26%

profile of v3, /device:TPU:2, one launch (start us, length us, event | category | flops | bytes accessed | tf_op | source)
XLA Modules:
  0.0 211.0 jit_solution(2141879185327925698)
XLA Ops:
  0.6 8.2 %channelize.1 = bf16[32,16,2048]{2,1,0:T(8,128)(2,1)} custom-call(s32[1,64]{1,0:T(1,128)} %bitcast.102, bf16[576,256]{1,0:T(8,128)(2,1)} %constant.37.clone.tables_hbm, f32[2,128,128]{2,1,0:T(8,128)} %constant.38.clone.tw_hbm, f32[4,16384]{1,0:T(4,128)} %taps_hbm.1, bf16[2,8,114688]{2,1,0:T(8,128)(2,1)} %volts_hbm.1), custom_call_target="tpu_custom_call" | custom-call | flops 1 | bytes 1 | tf_op jit(solution)/shard_map/channelize/pallas_call | solution.py:140
  8.8 7.8 %all-to-all-start = ((bf16[32,16,2048]{2,1,0:T(8,128)(2,1)}), bf16[32,16,2048]{2,1,0:T(8,128)(2,1)S(1)}, u32[]{:S(2)}, u32[]{:S(2)}) async-start(bf16[32,16,2048]{2,1,0:T(8,128)(2,1)} %channelize.1), calls=%async_computation | async-start | bytes 4194304 | tf_op jit(solution)/shard_map/all_to_all | solution.py:594
  20.0 6.5 %collective-permute-start.1 = (bf16[2,16,16,256]{3,2,1,0:T(8,128)(2,1)S(1)}, bf16[2,16,16,256]{3,2,1,0:T(8,128)(2,1)S(1)}, u32[]{:S(2)}, u32[]{:S(2)}) collective-permute-start(bf16[2,16,16,256]{3,2,1,0:T(8,128)(2,1)S(1)} %dynamic-slice_bitcast_fusion.1), channel_id=1, source_target_pairs={{3,0},{11,8},{7,4},{15,12},{19,16},{27,24},{23,20},{31,28},{35,32}... | collective-permute-start | bytes 786440 | tf_op jit(solution)/shard_map/ppermute | solution.py:584
  28.4 4.9 %collective-permute-done.1.gain_hbm = bf16[2,16,16,256]{3,2,1,0:T(8,128)(2,1)S(1)} collective-permute-done((bf16[2,16,16,256]{3,2,1,0:T(8,128)(2,1)S(1)}, bf16[2,16,16,256]{3,2,1,0:T(8,128)(2,1)S(1)}, u32[]{:S(2)}, u32[]{:S(2)}) %collective-permute-start.1) | collective-permute-done | bytes 262176 | tf_op jit(solution)/shard_map/ppermute | solution.py:584
  33.2 14.1 %collective-permute-done.2.gain_hbm = bf16[2,16,16,256]{3,2,1,0:T(8,128)(2,1)S(1)} collective-permute-done((bf16[2,16,16,256]{3,2,1,0:T(8,128)(2,1)S(1)}, bf16[2,16,16,256]{3,2,1,0:T(8,128)(2,1)S(1)}, u32[]{:S(2)}, u32[]{:S(2)}) %collective-permute-start.2) | collective-permute-done | bytes 262176 | tf_op jit(solution)/shard_map/ppermute | solution.py:585
  51.3 4.8 %collective-permute-start.4 = (bf16[256,1024]{1,0:T(8,128)(2,1)}, bf16[256,1024]{1,0:T(8,128)(2,1)S(1)}, u32[]{:S(2)}, u32[]{:S(2)}) collective-permute-start(bf16[256,1024]{1,0:T(8,128)(2,1)} %get-tuple-element.20), channel_id=1, source_target_pairs={{0,11},{1,0},{2,1},{3,2},{8,3},{9,8},{10,9},{11,10},{4,15},{5,4},{... | collective-permute-start | bytes 1572872 | tf_op jit(solution)/shard_map/ppermute | solution.py:602
  58.8 3.2 %collective-permute-start.13 = (bf16[256,1024]{1,0:T(8,128)(2,1)}, bf16[256,1024]{1,0:T(8,128)(2,1)S(1)}, u32[]{:S(2)}, u32[]{:S(2)}) collective-permute-start(bf16[256,1024]{1,0:T(8,128)(2,1)} %get-tuple-element.24), channel_id=1, source_target_pairs={{0,11},{1,0},{2,1},{3,2},{8,3},{9,8},{10,9},{11,10},{4,15},{5,4},{... | collective-permute-start | bytes 1572872 | tf_op jit(solution)/shard_map/ppermute | solution.py:602
  64.1 5.0 %collective-permute-done.3.part_hbm = bf16[256,1024]{1,0:T(8,128)(2,1)S(1)} collective-permute-done((bf16[256,1024]{1,0:T(8,128)(2,1)}, bf16[256,1024]{1,0:T(8,128)(2,1)S(1)}, u32[]{:S(2)}, u32[]{:S(2)}) %collective-permute-start.3) | collective-permute-done | bytes 524320 | tf_op jit(solution)/shard_map/ppermute | solution.py:601
  72.9 5.4 %collective-permute-start.5 = (bf16[256,1024]{1,0:T(8,128)(2,1)}, bf16[256,1024]{1,0:T(8,128)(2,1)S(1)}, u32[]{:S(2)}, u32[]{:S(2)}) collective-permute-start(bf16[256,1024]{1,0:T(8,128)(2,1)} %enter.9), channel_id=1, source_target_pairs={{0,11},{1,0},{2,1},{3,2},{8,3},{9,8},{10,9},{11,10},{4,15},{5,4},{... | collective-permute-start | bytes 1572872 | tf_op jit(solution)/shard_map/ppermute | solution.py:602
  83.2 4.1 %collective-permute-start.16 = (bf16[256,1024]{1,0:T(8,128)(2,1)}, bf16[256,1024]{1,0:T(8,128)(2,1)S(1)}, u32[]{:S(2)}, u32[]{:S(2)}) collective-permute-start(bf16[256,1024]{1,0:T(8,128)(2,1)} %enter.12), channel_id=1, source_target_pairs={{0,1},{1,2},{2,3},{3,8},{8,9},{9,10},{10,11},{11,0},{4,5},{5,6},{6... | collective-permute-start | bytes 1572872 | tf_op jit(solution)/shard_map/ppermute | solution.py:601
  89.6 8.2 %collective-permute-done.8.part_hbm = bf16[256,1024]{1,0:T(8,128)(2,1)S(1)} collective-permute-done((bf16[256,1024]{1,0:T(8,128)(2,1)}, bf16[256,1024]{1,0:T(8,128)(2,1)S(1)}, u32[]{:S(2)}, u32[]{:S(2)}) %collective-permute-start.8) | collective-permute-done | bytes 524320 | tf_op jit(solution)/shard_map/ppermute | solution.py:601
  105.2 3.8 %collective-permute-done.16.part_hbm = bf16[256,1024]{1,0:T(8,128)(2,1)S(1)} collective-permute-done((bf16[256,1024]{1,0:T(8,128)(2,1)}, bf16[256,1024]{1,0:T(8,128)(2,1)S(1)}, u32[]{:S(2)}, u32[]{:S(2)}) %collective-permute-start.16) | collective-permute-done | bytes 524320 | tf_op jit(solution)/shard_map/ppermute | solution.py:601
  116.3 3.9 %collective-permute-done.9 = bf16[256,1024]{1,0:T(8,128)(2,1)S(1)} collective-permute-done((bf16[256,1024]{1,0:T(8,128)(2,1)}, bf16[256,1024]{1,0:T(8,128)(2,1)S(1)}, u32[]{:S(2)}, u32[]{:S(2)}) %collective-permute-start.9) | collective-permute-done | bytes 524320 | tf_op jit(solution)/shard_map/ppermute | solution.py:601
  122.2 8.0 %collective-permute-done.17 = bf16[256,1024]{1,0:T(8,128)(2,1)S(1)} collective-permute-done((bf16[256,1024]{1,0:T(8,128)(2,1)}, bf16[256,1024]{1,0:T(8,128)(2,1)S(1)}, u32[]{:S(2)}, u32[]{:S(2)}) %collective-permute-start.17) | collective-permute-done | bytes 524320 | tf_op jit(solution)/shard_map/ppermute | solution.py:601
  134.2 8.3 %collective-permute-done.10 = bf16[256,1024]{1,0:T(8,128)(2,1)S(1)} collective-permute-done((bf16[256,1024]{1,0:T(8,128)(2,1)S(1)}, bf16[256,1024]{1,0:T(8,128)(2,1)S(1)}, u32[]{:S(2)}, u32[]{:S(2)}) %collective-permute-start.10) | collective-permute-done | bytes 524320 | tf_op jit(solution)/shard_map/ppermute | solution.py:602
  143.3 6.3 %outer_share.2.refs_17_ = bf16[256,1024]{1,0:T(8,128)(2,1)} custom-call(s32[2]{0:T(128)} %pad_add_fusion.at_ref.refs_0_, s32[1024,64]{1,0:T(8,128)} %copy.19.mask_ref, bf16[2,256,512]{2,1,0:T(8,128)(2,1)} %collective-permute-done.near_hbm, bf16[2,256,512]{2,1,0:T(8,128)(2,1)} %collective-permute-done.6.far_hbm, bf16[2,1024,512]{2,1,0:T(8,128)(2,1)} %bitcast.37, ...), custom_call_target="tpu_custom_call" | custom-call | flops 1 | bytes 1 | tf_op jit(solution)/shard_map/outer_share/pallas_call | solution.py:318
  151.1 6.3 %edge.1.refs_21_ = bf16[2,512,512]{2,1,0:T(8,128)(2,1)} custom-call(s32[2]{0:T(128)} %pad_add_fusion.at_ref.refs_0_, bf16[16,16,1024]{2,1,0:T(8,128)(2,1)} %bitcast.52, bf16[16,16,1024]{2,1,0:T(8,128)(2,1)} %bitcast.49, bf16[16,16,1024]{2,1,0:T(8,128)(2,1)} %bitcast.82, bf16[16,16,1024]{2,1,0:T(8,128)(2,1)} %bitcast.79, bf16[16,16,1024]{2,1,0:T(8,128)(2,1)} %bitcast.67, ...), custom_call_target="tpu_custom_call" | custom-call | flops 1 | bytes 1 | tf_op jit(solution)/shard_map/edge/pallas_call | solution.py:365
  158.7 6.1 %collective-permute-done.21.refs_22_.share_a = bf16[256,1024]{1,0:T(8,128)(2,1)} collective-permute-done((bf16[256,1024]{1,0:T(8,128)(2,1)}, bf16[256,1024]{1,0:T(8,128)(2,1)}, u32[]{:S(2)}, u32[]{:S(2)}) %collective-permute-start.21) | collective-permute-done | bytes 524320 | tf_op jit(solution)/shard_map/ppermute | solution.py:618
  165.6 4.2 %collective-permute-start.23 = (bf16[2,256,512]{2,1,0:T(8,128)(2,1)S(1)}, bf16[2,256,512]{2,1,0:T(8,128)(2,1)S(1)}, u32[]{:S(2)}, u32[]{:S(2)}) collective-permute-start(bf16[2,256,512]{2,1,0:T(8,128)(2,1)S(1)} %get-tuple-element.35), channel_id=1, source_target_pairs={{0,2},{8,10},{4,6},{12,14},{16,18},{24,26},{20,22},{28,30},{32,34}... | collective-permute-start | bytes 1572872 | tf_op jit(solution)/shard_map/ppermute | solution.py:623
  171.1 6.3 %outer_share.3 = bf16[256,1024]{1,0:T(8,128)(2,1)} custom-call(s32[2]{0:T(128)} %pad_add_fusion.at_ref.refs_0_, s32[1024,64]{1,0:T(8,128)} %copy.19.mask_ref, bf16[2,256,512]{2,1,0:T(8,128)(2,1)} %collective-permute-done.near_hbm, bf16[2,256,512]{2,1,0:T(8,128)(2,1)} %collective-permute-done.6.far_hbm, bf16[2,1024,512]{2,1,0:T(8,128)(2,1)} %bitcast.38, ...), custom_call_target="tpu_custom_call" | custom-call | flops 1 | bytes 1 | tf_op jit(solution)/shard_map/outer_share/pallas_call | solution.py:318
  178.9 11.5 %pairs.1 = (bf16[2,512,2048]{2,1,0:T(8,128)(2,1)}, bf16[4,16,2,16,1024]{4,3,2,1,0:T(8,128)(2,1)}, bf16[4,16,2,16,1024]{4,3,2,1,0:T(8,128)(2,1)}) custom-call(s32[2]{0:T(128)} %pad_add_fusion.at_ref.refs_0_, bf16[16,16,1024]{2,1,0:T(8,128)(2,1)} %bitcast.68, bf16[16,16,1024]{2,1,0:T(8,128)(2,1)} %bitcast.71, bf16[16,16,1024]{2,1,0:T(8,128)(2,1)} %bitcast.53, ...), custom_call_target="tpu_custom_call" | custom-call | flops 1 | bytes 1 | tf_op jit(solution)/shard_map/pairs/pallas_call | solution.py:438
  191.6 10.4 %beams.1.formed_ref = f32[256,2048]{1,0:T(8,128)} custom-call(s32[2]{0:T(128)} %pad_add_fusion.at_ref.refs_0_, s32[1024,64]{1,0:T(8,128)} %copy.19.mask_ref, bf16[2,1024,512]{2,1,0:T(8,128)(2,1)} %bitcast.39, bf16[2,256,512]{2,1,0:T(8,128)(2,1)} %copy-done.21, bf16[2,256,512]{2,1,0:T(8,128)(2,1)} %copy-done.22, bf16[2,256,512]{2,1,0:T(8,128)(2,1)} %copy-done.23, ...), custom_call_target="tpu_custom_call" | custom-call | flops 1 | bytes 1 | tf_op jit(solution)/shard_map/beams/pallas_call | solution.py:516
  203.0 3.2 %last_pairs.1.refs_0_ = bf16[2,512,2048]{2,1,0:T(8,128)(2,1)} custom-call(s32[2]{0:T(128)} %pad_add_fusion.at_ref.refs_0_, bf16[2,512,512]{2,1,0:T(8,128)(2,1)} %copy-done.19, bf16[2,512,2048]{2,1,0:T(8,128)(2,1)} %get-tuple-element.27.whole_hbm), custom_call_target="tpu_custom_call", output_to_operand_aliasing={{}: (2, {})} | custom-call | flops 1 | bytes 1 | tf_op jit(solution)/shard_map/last_pairs/pallas_call | solution.py:474
  207.0 3.9 %finish.1 = bf16[512,4,256]{2,1,0:T(4,128)(2,1)} custom-call(s32[2]{0:T(128)} %pad_add_fusion.at_ref.refs_0_, f32[256,2048]{1,0:T(8,128)} %beams.1.formed_ref, bf16[256,1024]{1,0:T(8,128)(2,1)} %collective-permute-done.21.refs_22_.share_a, bf16[256,1024]{1,0:T(8,128)(2,1)} %copy-done.20, bf16[2,512,2048]{2,1,0:T(8,128)(2,1)} %last_pairs.1.refs_0_), custom_call_target="tpu_custom_call" | custom-call | flops 1 | bytes 1 | tf_op jit(solution)/shard_map/finish/pallas_call | solution.py:557
  (103 shorter events, 55.5 us)
Async XLA Ops:
  8.8 38.5 %all-to-all-start = ((bf16[32,16,2048]{2,1,0:T(8,128)(2,1)}), bf16[32,16,2048]{2,1,0:T(8,128)(2,1)S(1)}, u32[]{:S(2)}, u32[]{:S(2)}) async-start(bf16[32,16,2048]{2,1,0:T(8,128)(2,1)} %channelize.1), calls=%async_computation | async-start | bytes 4194304 | tf_op jit(solution)/shard_map/all_to_all | solution.py:594
  18.5 28.9 %collective-permute-start = (bf16[2,256,512]{2,1,0:T(8,128)(2,1)}, bf16[2,256,512]{2,1,0:T(8,128)(2,1)}, u32[]{:S(2)}, u32[]{:S(2)}) collective-permute-start(bf16[2,256,512]{2,1,0:T(8,128)(2,1)} %dynamic-slice_bitcast_fusion), channel_id=1, source_target_pairs={{1,2},{9,10},{5,6},{13,14},{17,18},{25,26},{21,22},{29,30},{33,34}... | collective-permute-start | bytes 1572872 | tf_op jit(solution)/shard_map/ppermute | solution.py:590
  26.5 20.8 %collective-permute-start.2 = (bf16[2,16,16,256]{3,2,1,0:T(8,128)(2,1)S(1)}, bf16[2,16,16,256]{3,2,1,0:T(8,128)(2,1)S(1)}, u32[]{:S(2)}, u32[]{:S(2)}) collective-permute-start(bf16[2,16,16,256]{3,2,1,0:T(8,128)(2,1)S(1)} %dynamic-slice_bitcast_fusion.1), channel_id=1, source_target_pairs={{2,0},{10,8},{6,4},{14,12},{18,16},{26,24},{22,20},{30,28},{34,32}... | collective-permute-start | bytes 786440 | tf_op jit(solution)/shard_map/ppermute | solution.py:585
  51.3 17.8 %collective-permute-start.3 = (bf16[256,1024]{1,0:T(8,128)(2,1)}, bf16[256,1024]{1,0:T(8,128)(2,1)S(1)}, u32[]{:S(2)}, u32[]{:S(2)}) collective-permute-start(bf16[256,1024]{1,0:T(8,128)(2,1)} %get-tuple-element.18), channel_id=1, source_target_pairs={{0,1},{1,2},{2,3},{3,8},{8,9},{9,10},{10,11},{11,0},{4,5},{5,6},{6... | collective-permute-start | bytes 1572872 | tf_op jit(solution)/shard_map/ppermute | solution.py:601
  51.3 20.8 %collective-permute-start.4 = (bf16[256,1024]{1,0:T(8,128)(2,1)}, bf16[256,1024]{1,0:T(8,128)(2,1)S(1)}, u32[]{:S(2)}, u32[]{:S(2)}) collective-permute-start(bf16[256,1024]{1,0:T(8,128)(2,1)} %get-tuple-element.20), channel_id=1, source_target_pairs={{0,11},{1,0},{2,1},{3,2},{8,3},{9,8},{10,9},{11,10},{4,15},{5,4},{... | collective-permute-start | bytes 1572872 | tf_op jit(solution)/shard_map/ppermute | solution.py:602
  58.8 21.5 %collective-permute-start.12 = (bf16[256,1024]{1,0:T(8,128)(2,1)}, bf16[256,1024]{1,0:T(8,128)(2,1)S(1)}, u32[]{:S(2)}, u32[]{:S(2)}) collective-permute-start(bf16[256,1024]{1,0:T(8,128)(2,1)} %get-tuple-element.23), channel_id=1, source_target_pairs={{0,1},{1,2},{2,3},{3,8},{8,9},{9,10},{10,11},{11,0},{4,5},{5,6},{6... | collective-permute-start | bytes 1572872 | tf_op jit(solution)/shard_map/ppermute | solution.py:601
  58.8 28.5 %collective-permute-start.13 = (bf16[256,1024]{1,0:T(8,128)(2,1)}, bf16[256,1024]{1,0:T(8,128)(2,1)S(1)}, u32[]{:S(2)}, u32[]{:S(2)}) collective-permute-start(bf16[256,1024]{1,0:T(8,128)(2,1)} %get-tuple-element.24), channel_id=1, source_target_pairs={{0,11},{1,0},{2,1},{3,2},{8,3},{9,8},{10,9},{11,10},{4,15},{5,4},{... | collective-permute-start | bytes 1572872 | tf_op jit(solution)/shard_map/ppermute | solution.py:602
  62.0 27.5 %collective-permute-start.6 = (bf16[2,256,512]{2,1,0:T(8,128)(2,1)}, bf16[2,256,512]{2,1,0:T(8,128)(2,1)}, u32[]{:S(2)}, u32[]{:S(2)}) collective-permute-start(bf16[2,256,512]{2,1,0:T(8,128)(2,1)} %dynamic-slice_bitcast_fusion), channel_id=1, source_target_pairs={{0,2},{8,10},{4,6},{12,14},{16,18},{24,26},{20,22},{28,30},{32,34}... | collective-permute-start | bytes 1572872 | tf_op jit(solution)/shard_map/ppermute | solution.py:591
  72.0 25.7 %collective-permute-start.8 = (bf16[256,1024]{1,0:T(8,128)(2,1)}, bf16[256,1024]{1,0:T(8,128)(2,1)S(1)}, u32[]{:S(2)}, u32[]{:S(2)}) collective-permute-start(bf16[256,1024]{1,0:T(8,128)(2,1)} %enter.8), channel_id=1, source_target_pairs={{0,1},{1,2},{2,3},{3,8},{8,9},{9,10},{10,11},{11,0},{4,5},{5,6},{6... | collective-permute-start | bytes 1572872 | tf_op jit(solution)/shard_map/ppermute | solution.py:601
  72.9 30.1 %collective-permute-start.5 = (bf16[256,1024]{1,0:T(8,128)(2,1)}, bf16[256,1024]{1,0:T(8,128)(2,1)S(1)}, u32[]{:S(2)}, u32[]{:S(2)}) collective-permute-start(bf16[256,1024]{1,0:T(8,128)(2,1)} %enter.9), channel_id=1, source_target_pairs={{0,11},{1,0},{2,1},{3,2},{8,3},{9,8},{10,9},{11,10},{4,15},{5,4},{... | collective-permute-start | bytes 1572872 | tf_op jit(solution)/shard_map/ppermute | solution.py:602
  83.2 25.7 %collective-permute-start.16 = (bf16[256,1024]{1,0:T(8,128)(2,1)}, bf16[256,1024]{1,0:T(8,128)(2,1)S(1)}, u32[]{:S(2)}, u32[]{:S(2)}) collective-permute-start(bf16[256,1024]{1,0:T(8,128)(2,1)} %enter.12), channel_id=1, source_target_pairs={{0,1},{1,2},{2,3},{3,8},{8,9},{9,10},{10,11},{11,0},{4,5},{5,6},{6... | collective-permute-start | bytes 1572872 | tf_op jit(solution)/shard_map/ppermute | solution.py:601
  88.1 26.0 %collective-permute-start.14 = (bf16[256,1024]{1,0:T(8,128)(2,1)}, bf16[256,1024]{1,0:T(8,128)(2,1)S(1)}, u32[]{:S(2)}, u32[]{:S(2)}) collective-permute-start(bf16[256,1024]{1,0:T(8,128)(2,1)} %enter.13), channel_id=1, source_target_pairs={{0,11},{1,0},{2,1},{3,2},{8,3},{9,8},{10,9},{11,10},{4,15},{5,4},{... | collective-permute-start | bytes 1572872 | tf_op jit(solution)/shard_map/ppermute | solution.py:602
  100.6 19.5 %collective-permute-start.9 = (bf16[256,1024]{1,0:T(8,128)(2,1)}, bf16[256,1024]{1,0:T(8,128)(2,1)S(1)}, u32[]{:S(2)}, u32[]{:S(2)}) collective-permute-start(bf16[256,1024]{1,0:T(8,128)(2,1)} %enter.11), channel_id=1, source_target_pairs={{0,1},{1,2},{2,3},{8,9},{9,10},{10,11},{4,5},{5,6},{6,7},{12,13},{... | collective-permute-start | bytes 1572872 | tf_op jit(solution)/shard_map/ppermute | solution.py:601
  103.9 17.0 %collective-permute-start.7 = (bf16[256,1024]{1,0:T(8,128)(2,1)}, bf16[256,1024]{1,0:T(8,128)(2,1)S(1)}, u32[]{:S(2)}, u32[]{:S(2)}) collective-permute-start(bf16[256,1024]{1,0:T(8,128)(2,1)} %enter.10), channel_id=1, source_target_pairs={{1,0},{2,1},{3,2},{9,8},{10,9},{11,10},{5,4},{6,5},{7,6},{13,12},{... | collective-permute-start | bytes 1572872 | tf_op jit(solution)/shard_map/ppermute | solution.py:602
  111.8 18.4 %collective-permute-start.17 = (bf16[256,1024]{1,0:T(8,128)(2,1)}, bf16[256,1024]{1,0:T(8,128)(2,1)S(1)}, u32[]{:S(2)}, u32[]{:S(2)}) collective-permute-start(bf16[256,1024]{1,0:T(8,128)(2,1)} %enter.15), channel_id=1, source_target_pairs={{0,1},{1,2},{2,3},{8,9},{9,10},{10,11},{4,5},{5,6},{6,7},{12,13},{... | collective-permute-start | bytes 1572872 | tf_op jit(solution)/shard_map/ppermute | solution.py:601
  115.0 17.0 %collective-permute-start.15 = (bf16[256,1024]{1,0:T(8,128)(2,1)}, bf16[256,1024]{1,0:T(8,128)(2,1)S(1)}, u32[]{:S(2)}, u32[]{:S(2)}) collective-permute-start(bf16[256,1024]{1,0:T(8,128)(2,1)} %enter.14), channel_id=1, source_target_pairs={{1,0},{2,1},{3,2},{9,8},{10,9},{11,10},{5,4},{6,5},{7,6},{13,12},{... | collective-permute-start | bytes 1572872 | tf_op jit(solution)/shard_map/ppermute | solution.py:602
  120.9 21.6 %collective-permute-start.10 = (bf16[256,1024]{1,0:T(8,128)(2,1)S(1)}, bf16[256,1024]{1,0:T(8,128)(2,1)S(1)}, u32[]{:S(2)}, u32[]{:S(2)}) collective-permute-start(bf16[256,1024]{1,0:T(8,128)(2,1)S(1)} %collective-permute-done.7), channel_id=1, source_target_pairs={{1,0},{2,1},{9,8},{10,9},{5,4},{6,5},{13,12},{14,13},{17,16},{18,1... | collective-permute-start | bytes 1572872 | tf_op jit(solution)/shard_map/ppermute | solution.py:602
  130.2 20.7 %collective-permute-start.19 = (bf16[256,1024]{1,0:T(8,128)(2,1)S(1)}, bf16[256,1024]{1,0:T(8,128)(2,1)}, u32[]{:S(2)}, u32[]{:S(2)}) collective-permute-start(bf16[256,1024]{1,0:T(8,128)(2,1)S(1)} %collective-permute-done.17), channel_id=1, source_target_pairs={{1,2},{2,3},{9,10},{10,11},{5,6},{6,7},{13,14},{14,15},{17,18},{18... | collective-permute-start | bytes 1572872 | tf_op jit(solution)/shard_map/ppermute | solution.py:601
  131.9 19.2 %collective-permute-start.18 = (bf16[256,1024]{1,0:T(8,128)(2,1)S(1)}, bf16[256,1024]{1,0:T(8,128)(2,1)}, u32[]{:S(2)}, u32[]{:S(2)}) collective-permute-start(bf16[256,1024]{1,0:T(8,128)(2,1)S(1)} %collective-permute-done.15), channel_id=1, source_target_pairs={{1,0},{2,1},{9,8},{10,9},{5,4},{6,5},{13,12},{14,13},{17,16},{18,1... | collective-permute-start | bytes 1572872 | tf_op jit(solution)/shard_map/ppermute | solution.py:602
  157.4 44.6 %collective-permute-start.20 = (bf16[2,512,512]{2,1,0:T(8,128)(2,1)}, bf16[2,512,512]{2,1,0:T(8,128)(2,1)S(1)}, u32[]{:S(2)}, u32[]{:S(2)}) collective-permute-start(bf16[2,512,512]{2,1,0:T(8,128)(2,1)} %edge.1.refs_21_), channel_id=1, source_target_pairs={{1,0},{9,8},{5,4},{13,12},{17,16},{25,24},{21,20},{29,28},{33,32},... | collective-permute-start | bytes 3145736 | tf_op jit(solution)/shard_map/ppermute | solution.py:617
  164.9 25.6 %collective-permute-start.22 = (bf16[2,256,512]{2,1,0:T(8,128)(2,1)S(1)}, bf16[2,256,512]{2,1,0:T(8,128)(2,1)S(1)}, u32[]{:S(2)}, u32[]{:S(2)}) collective-permute-start(bf16[2,256,512]{2,1,0:T(8,128)(2,1)S(1)} %get-tuple-element.35), channel_id=1, source_target_pairs={{1,2},{9,10},{5,6},{13,14},{17,18},{25,26},{21,22},{29,30},{33,34}... | collective-permute-start | bytes 1572872 | tf_op jit(solution)/shard_map/ppermute | solution.py:622
  165.6 24.9 %collective-permute-start.23 = (bf16[2,256,512]{2,1,0:T(8,128)(2,1)S(1)}, bf16[2,256,512]{2,1,0:T(8,128)(2,1)S(1)}, u32[]{:S(2)}, u32[]{:S(2)}) collective-permute-start(bf16[2,256,512]{2,1,0:T(8,128)(2,1)S(1)} %get-tuple-element.35), channel_id=1, source_target_pairs={{0,2},{8,10},{4,6},{12,14},{16,18},{24,26},{20,22},{28,30},{32,34}... | collective-permute-start | bytes 1572872 | tf_op jit(solution)/shard_map/ppermute | solution.py:623
  169.7 20.7 %collective-permute-start.24 = (bf16[2,256,512]{2,1,0:T(8,128)(2,1)S(1)}, bf16[2,256,512]{2,1,0:T(8,128)(2,1)S(1)}, u32[]{:S(2)}, u32[]{:S(2)}) collective-permute-start(bf16[2,256,512]{2,1,0:T(8,128)(2,1)S(1)} %get-tuple-element.34), channel_id=1, source_target_pairs={{0,1},{8,9},{4,5},{12,13},{16,17},{24,25},{20,21},{28,29},{32,33},... | collective-permute-start | bytes 1572872 | tf_op jit(solution)/shard_map/ppermute | solution.py:625
  177.4 28.8 %collective-permute-start.25 = (bf16[256,1024]{1,0:T(8,128)(2,1)}, bf16[256,1024]{1,0:T(8,128)(2,1)S(1)}, u32[]{:S(2)}, u32[]{:S(2)}) collective-permute-start(bf16[256,1024]{1,0:T(8,128)(2,1)} %outer_share.3), channel_id=1, source_target_pairs={{1,0},{9,8},{5,4},{13,12},{17,16},{25,24},{21,20},{29,28},{33,32},... | collective-permute-start | bytes 1572872 | tf_op jit(solution)/shard_map/ppermute | solution.py:618
  (28 other events, 271.2 us)

commit v4 on v3

--- a/solution.py
+++ b/solution.py
@@ -125,10 +125,10 @@
             out_ref[:, :, at : at + RADIX] = turned[block].reshape(32, 16, RADIX).astype(BF16)
 
 
-ANY = pl.BlockSpec(memory_space=pl.ANY)
+ANY = pl.BlockSpec(memory_space=pltpu.HBM)
 VMEM = pl.BlockSpec(memory_space=pltpu.VMEM)
 SMEM = pl.BlockSpec(memory_space=pltpu.SMEM)
-GRANT = pltpu.CompilerParams(vmem_limit_bytes=56 * 2**20)
+GRANT = pltpu.CompilerParams(vmem_limit_bytes=63 * 2**20 + 2**19)
 BRIEF = pl.CostEstimate(flops=1, bytes_accessed=1, transcendentals=0)
 
 
@@ -166,28 +166,36 @@
     return jnp.concatenate(parts, axis=1)
 
 
-def calibrate_kernel(at_ref, got_ref, gain_ref, up_ref, down_ref):
+def calibrate_kernel(section, at_ref, got_hbm, gain_hbm, up_ref, down_ref, got_ref, gain_ref, sems):
     half, low_band = at_ref[0], at_ref[1] < 2
+    loads = [
+        pltpu.make_async_copy(got_hbm.at[:, :, pl.ds(section * 1024, 1024)], got_ref, sems.at[0]),
+        pltpu.make_async_copy(gain_hbm.at[:, :, half], gain_ref, sems.at[1]),
+    ]
+    for copy in loads:
+        copy.start()
+    for copy in loads:
+        copy.wait()
     got = got_ref[...].astype(F32)
     swapped = half == 1
     own = jnp.where(swapped, got[:, 8:], got[:, :8]).reshape(256, got.shape[2])
     other = jnp.where(swapped, got[:, :8], got[:, 8:]).reshape(256, got.shape[2])
-    own = times(gain_ref[:, :, half].astype(F32).reshape(2, 256, 256), own)
+    own = times(gain_ref[...].astype(F32).reshape(2, 256, 256), own)
     up_ref[...] = jnp.where(low_band, own, other).astype(BF16)
     down_ref[...] = jnp.where(low_band, other, own).astype(BF16)
 
 
 def calibrate(section, place, got, gains):
     return pl.pallas_call(
-        calibrate_kernel,
+        lambda *refs: calibrate_kernel(section, *refs),
         out_shape=[jax.ShapeDtypeStruct((256, 1024), BF16)] * 2,
-        grid=(1,),
-        in_specs=[
-            SMEM,
-            pl.BlockSpec((32, 16, 1024), lambda i: (0, 0, section)),
-            pl.BlockSpec((2, 16, 2, 16, 256), lambda i: (0, 0, 0, 0, 0)),
+        in_specs=[SMEM, ANY, ANY],
+        out_specs=[VMEM] * 2,
+        scratch_shapes=[
+            pltpu.VMEM((32, 16, 1024), BF16),
+            pltpu.VMEM((2, 16, 16, 256), BF16),
+            pltpu.SemaphoreType.DMA((2,)),
         ],
-        out_specs=[pl.BlockSpec((256, 1024), lambda i: (0, 0))] * 2,
         compiler_params=GRANT,
         cost_estimate=BRIEF,
         name="calibrate",
@@ -289,34 +297,52 @@
     return jnp.where(band < 2, 0, 3)
 
 
-def share_kernel(at_ref, mask_ref, near_hbm, far_hbm, local_hbm, *refs):
+def share_kernel(give, at_ref, mask_ref, near_hbm, far_hbm, local_hbm, *refs):
     sources, (out_ref, held, weights, sems, weight_sems) = refs[:12], refs[-5:]
     half, band = at_ref[0], at_ref[1]
     low = band < 2
-    rows = pl.ds(pl.multiple_of(outer_band(band) * 256, 256), 256)
-    loads = [
-        pltpu.make_async_copy(ref, weights.at[index], weight_sems.at[index])
-        for index, ref in enumerate((near_hbm, far_hbm, local_hbm.at[:, rows, :]))
-    ]
-    for copy in loads:
-        copy.start()
-    for index in range(3):
-        at = index * 4
-        loads += fetch(low, half, (sources[at : at + 2], sources[at + 2 : at + 4]), held.at[index], sems.at[index])
-    mask = mask_ref[...].astype(F32).astype(BF16)
-    total = None
-    for index, group in enumerate((jnp.where(low, 2, 1), jnp.where(low, 3, 0), band)):
-        for copy in (loads[index], loads[3 + 2 * index], loads[4 + 2 * index]):
-            copy.wait()
-        now = weighted(mask, group, weights.at[index], held[index].reshape(512, 1024))
-        total = now if total is None else total + now
-    out_ref[...] = total.astype(BF16)
-
-
-def outer_share(place, mask, near, far, local, up, down):
+    inner = (band == 1) | (band == 2)
+
+    def local(row):
+        rows = pl.ds(pl.multiple_of(row, 256), 256)
+        return pltpu.make_async_copy(local_hbm.at[:, rows, :], weights.at[2], weight_sems.at[2])
+
+    @pl.when(inner)
+    def _():
+        loads = [
+            pltpu.make_async_copy(near_hbm, weights.at[0], weight_sems.at[0]),
+            pltpu.make_async_copy(far_hbm, weights.at[1], weight_sems.at[1]),
+            local(outer_band(band) * 256),
+        ]
+        for copy in loads:
+            copy.start()
+        for index in range(3):
+            at = index * 4
+            loads += fetch(low, half, (sources[at : at + 2], sources[at + 2 : at + 4]), held.at[index], sems.at[index])
+        mask = mask_ref[...].astype(F32).astype(BF16)
+        total = None
+        for index, group in enumerate((jnp.where(low, 2, 1), jnp.where(low, 3, 0), band)):
+            for copy in (loads[index], loads[3 + 2 * index], loads[4 + 2 * index]):
+                copy.wait()
+            now = weighted(mask, group, weights.at[index], held[index].reshape(512, 1024))
+            total = now if total is None else total + now
+        out_ref[...] = total.astype(BF16)
+
+    if give:
+
+        @pl.when(jnp.logical_not(inner))
+        def _():
+            load = local(jnp.where(low, 256, 512))
+            load.start()
+            load.wait()
+            for part in range(2):
+                out_ref[:, part * 512 : (part + 1) * 512] = weights[2, part]
+
+
+def outer_share(give, place, mask, near, far, local, up, down):
     sources = (down[1], up[1], up[3], down[3], down[2], up[2], up[2], down[2], up[0], down[0], down[4], up[4])
     return pl.pallas_call(
-        share_kernel,
+        lambda *refs: share_kernel(give, *refs),
         out_shape=jax.ShapeDtypeStruct((256, 1024), BF16),
         grid_spec=pltpu.PrefetchScalarGridSpec(
             num_scalar_prefetch=1,
@@ -338,24 +364,28 @@
 
 def edge_kernel(average, at_ref, *refs):
     sources, (block_ref, far, own, sems) = refs[:16], refs[-4:]
-    half, low = at_ref[0], at_ref[1] < 2
-    waits = []
-    for section in range(2):
-        parts = sources[section * 8 : section * 8 + 8]
-        waits.append(
-            fetch(low, half, (parts[0:2], parts[2:4]), far.at[section], sems.at[section, 0])
-            + fetch(low, half, (parts[4:6], parts[6:8]), own.at[section], sems.at[section, 1])
-        )
-    total = None
-    for section in range(2):
-        for copy in waits[section]:
-            copy.wait()
-        left, right = own[section].reshape(512, 1024), far[section].reshape(512, 1024)
-        both = jnp.concatenate([left, crossed(left)], axis=0)
-        now = lax.dot_general(both, right, BOTH_LAST, preferred_element_type=F32)
-        total = now if total is None else total + now
-    block_ref[0] = (total[:512] * average).astype(BF16)
-    block_ref[1] = (total[512:] * average).astype(BF16)
+    half, band = at_ref[0], at_ref[1]
+    low = band < 2
+
+    @pl.when((band == 1) | (band == 2))
+    def _():
+        waits = []
+        for section in range(2):
+            parts = sources[section * 8 : section * 8 + 8]
+            waits.append(
+                fetch(low, half, (parts[0:2], parts[2:4]), far.at[section], sems.at[section, 0])
+                + fetch(low, half, (parts[4:6], parts[6:8]), own.at[section], sems.at[section, 1])
+            )
+        total = None
+        for section in range(2):
+            for copy in waits[section]:
+                copy.wait()
+            left, right = own[section].reshape(512, 1024), far[section].reshape(512, 1024)
+            both = jnp.concatenate([left, crossed(left)], axis=0)
+            now = lax.dot_general(both, right, BOTH_LAST, preferred_element_type=F32)
+            total = now if total is None else total + now
+        block_ref[0] = (total[:512] * average).astype(BF16)
+        block_ref[1] = (total[512:] * average).astype(BF16)
 
 
 def edge(average, place, ups, downs, *after):
@@ -495,13 +525,19 @@
             (band, local_ref),
             (jnp.where(low, 2, 1), near_ref),
             (jnp.where(low, 3, 0), far_ref),
-            (jnp.where(low, 1 - band, 5 - band), end_ref),
         )
         for group, piece_ref in pieces:
             lanes = pl.ds(pl.multiple_of(group * 512, 512), 512)
             wide = spread(mask, group)
             for part in range(2):
                 weights[part * 256 : (part + 1) * 256, lanes] = piece_ref[part] * wide
+        group = jnp.where(low, 1 - band, 5 - band)
+        lanes = pl.ds(pl.multiple_of(group * 512, 512), 512)
+        wide = spread(mask, group)
+        inner = (band == 1) | (band == 2)
+        for part in range(2):
+            given = jnp.where(inner, end_ref[:, part * 512 : (part + 1) * 512] * wide, jnp.zeros((512,), BF16))
+            weights[part * 256 : (part + 1) * 256, lanes] = given
 
     def form(section_ref):
         total = jnp.dot(weights[...], section_ref[...], preferred_element_type=F32)
@@ -523,8 +559,9 @@
                 pl.BlockSpec((256, 64), lambda i, at: (at[1], 0)),
                 pl.BlockSpec((2, 256, 512), lambda i, at: (0, at[1], 0)),
             ]
-            + [pl.BlockSpec((2, 256, 512), lambda i, at: (0, 0, 0))] * 3
+            + [pl.BlockSpec((2, 256, 512), lambda i, at: (0, 0, 0))] * 2
             + [
+                pl.BlockSpec((256, 1024), lambda i, at: (0, 0)),
                 pl.BlockSpec((2048, 512), lambda i, at: (0, jnp.minimum(i, 1))),
                 pl.BlockSpec((2048, 512), lambda i, at: (0, jnp.maximum(i - 2, 0))),
             ],
@@ -610,23 +647,24 @@
     inward = hop(-1, (1,)) + hop(1, (2,))
     shares = []
     for up, down in zip(ups, downs):
-        shares.append(outer_share(place, beam_mask, near_outer, far_outer, own_weights, up, down))
+        shares.append(outer_share(not shares, place, beam_mask, near_outer, far_outer, own_weights, up, down))
         if len(shares) == 1:
             block = edge(average, place, ups, downs, shares[0])
     shares[1], _ = lax.optimization_barrier((shares[1], block))
     received = lax.ppermute(block, BOTH, inward)
-    shares = [lax.ppermute(share, BOTH, inward) for share in shares]
-
-    late, _, _ = lax.optimization_barrier((own_weights, block, shares[0]))
-    away = lax.dynamic_slice_in_dim(late, jnp.where(low, 512, 256), 256, 1)
+    shares = [
+        lax.ppermute(shares[0], BOTH, inward + from_end),
+        lax.ppermute(shares[1], BOTH, inward),
+    ]
+
+    away = lax.dynamic_slice_in_dim(own_weights, jnp.where(low, 512, 256), 256, 1)
+    away, *_ = lax.optimization_barrier((away, block, shares[0]))
     near = lax.ppermute(away, BOTH, from_near)
     far = lax.ppermute(away, BOTH, from_far)
-    away = lax.dynamic_slice_in_dim(late, jnp.where(low, 256, 512), 256, 1)
-    end = lax.ppermute(away, BOTH, from_end)
 
     visibility, sections = pairs(average, place, ups, downs, block, shares[0])
     visibility = last_pairs(place, received, visibility)
-    formed = finish(place, beams(place, beam_mask, own_weights, (near, far, end), sections), shares, visibility)
+    formed = finish(place, beams(place, beam_mask, own_weights, (near, far, shares[0]), sections), shares, visibility)
     return (visibility[:, None], formed.reshape(1, 256, 2, 4, 256))
 
 

time: 212 us -> 204 us (0.962)
  starting transfers between devices: 60.3 us -> 72.2 us
  local copies, waits for them, and re-layouts: 14.4 us -> 2.93 us
  Pallas kernels: 69.9 us -> 59.9 us
  waiting for transfers between devices: 64.6 us -> 66.9 us
    unnamed x51 -> x13, local copies, waits for them, and re-layouts: 12.4 us -> 1.86 us
    ppermute x3 -> x2, starting transfers between devices: 4.13 us -> 11.2 us  [the longest x1 9.7 us: shards(): lax.ppermute(shares[0], BOTH, inward + from_end)]
    pallas_call x4, Pallas kernels: 17.9 us -> 12.4 us  [the longest x2 6.45 us: calibrate(): pl.pallas_call(lambda *refs: calibrate_kernel(section, *refs), out_shape=...]
    pallas_call x1, Pallas kernels: 6.34 us -> 1.72 us  [edge(): pl.pallas_call(lambda *refs: edge_kernel(average, *refs), out_shape=jax.S...]
    ppermute x8, waiting for transfers between devices: 31 us -> 34.3 us  [shards(): up.append(lax.ppermute(up[-1], BOTH, hop(1, senders)))]
    ppermute x8, starting transfers between devices: 10.9 us -> 13.4 us  [shards(): up.append(lax.ppermute(up[-1], BOTH, hop(1, senders)))]
    ppermute x1, starting transfers between devices: 4.16 us -> 6.48 us  [shards(): far = lax.ppermute(away, BOTH, from_far)]
    ppermute x3 -> x2, waiting for transfers between devices: 6.06 us -> 6.27 us  [the longest x1 6.27 us: shards(): lax.ppermute(shares[0], BOTH, inward + from_end)]
  transfers between devices with their start and end apart: 27 -> 26, of which waited for: 12 -> 10; matrix products, arithmetic and copies ran while one was open for 2% -> 1% of each run, Pallas kernels for 26% -> 22%
where the time goes in v4:
time: 204 us
  starting transfers between devices  72.2 us (35%)
  waiting for transfers between devices  66.9 us (33%)
  Pallas kernels  59.9 us (29%)
  local copies, waits for them, and re-layouts  2.93 us (1%)
    ppermute x8, waiting for transfers between devices, shards(): up.append(lax.ppermute(up[-1], BOTH, hop(1, senders)))  34.3 us
    ppermute x8, starting transfers between devices, shards(): lax.ppermute(down[-1], BOTH, hop(-1, tuple((3 - p for p in senders))))  20 us
    ppermute x1, waiting for transfers between devices, shards(): lax.ppermute(sent_gain, BOTH, hop(-2, (2,)) + hop(2, (1,)))  14.9 us
    ppermute x8, starting transfers between devices, shards(): up.append(lax.ppermute(up[-1], BOTH, hop(1, senders)))  13.4 us
    pallas_call x1, Pallas kernels, pairs(): pl.pallas_call(lambda *refs: pair_kernel(average, *refs), out_shape=[jax....  11.5 us
    pallas_call x1, Pallas kernels, beams(): pl.pallas_call(beam_kernel, out_shape=jax.ShapeDtypeStruct((256, 2048), F...  10.4 us
    ppermute x1, starting transfers between devices, shards(): lax.ppermute(shares[0], BOTH, inward + from_end)  9.7 us
    pallas_call x8, Pallas kernels, enter(): pl.pallas_call(enter_kernel, out_shape=jax.ShapeDtypeStruct(part.shape, B...  8.56 us
  transfers between devices with their start and end apart: 26, of which 10 were waited for; matrix products, arithmetic and copies ran while one was open for 1% of the time, Pallas kernels for 22%

profile of v4, /device:TPU:2, one launch (start us, length us, event | category | flops | bytes accessed | tf_op | source)
XLA Modules:
  0.0 203.6 jit_solution(17202809899081835513)
XLA Ops:
  0.6 8.2 %channelize.1 = bf16[32,16,2048]{2,1,0:T(8,128)(2,1)} custom-call(s32[1,64]{1,0:T(1,128)} %bitcast.61, bf16[576,256]{1,0:T(8,128)(2,1)} %constant.37.clone.tables_hbm, f32[2,128,128]{2,1,0:T(8,128)} %constant.38.clone.tw_hbm, f32[4,16384]{1,0:T(4,128)} %taps_hbm.1, bf16[2,8,114688]{2,1,0:T(8,128)(2,1)} %volts_hbm.1), custom_call_target="tpu_custom_call" | custom-call | flops 1 | bytes 1 | tf_op jit(solution)/shard_map/channelize/pallas_call | solution.py:140
  8.8 7.8 %all-to-all-start = ((bf16[32,16,2048]{2,1,0:T(8,128)(2,1)}), bf16[32,16,2048]{2,1,0:T(8,128)(2,1)}, u32[]{:S(2)}, u32[]{:S(2)}) async-start(bf16[32,16,2048]{2,1,0:T(8,128)(2,1)} %channelize.1), calls=%async_computation | async-start | bytes 4194304 | tf_op jit(solution)/shard_map/all_to_all | solution.py:631
  18.4 6.5 %collective-permute-start.1 = (bf16[2,16,16,256]{3,2,1,0:T(8,128)(2,1)S(1)}, bf16[2,16,16,256]{3,2,1,0:T(8,128)(2,1)S(1)}, u32[]{:S(2)}, u32[]{:S(2)}) collective-permute-start(bf16[2,16,16,256]{3,2,1,0:T(8,128)(2,1)S(1)} %dynamic-slice_bitcast_fusion.2), channel_id=1, source_target_pairs={{3,0},{11,8},{7,4},{15,12},{19,16},{27,24},{23,20},{31,28},{35,32}... | collective-permute-start | bytes 786440 | tf_op jit(solution)/shard_map/ppermute | solution.py:621
  26.9 4.8 %collective-permute-done.1.gain_hbm = bf16[2,16,16,256]{3,2,1,0:T(8,128)(2,1)S(1)} collective-permute-done((bf16[2,16,16,256]{3,2,1,0:T(8,128)(2,1)S(1)}, bf16[2,16,16,256]{3,2,1,0:T(8,128)(2,1)S(1)}, u32[]{:S(2)}, u32[]{:S(2)}) %collective-permute-start.1) | collective-permute-done | bytes 262176 | tf_op jit(solution)/shard_map/ppermute | solution.py:621
  31.7 14.9 %collective-permute-done.2.gain_hbm = bf16[2,16,16,256]{3,2,1,0:T(8,128)(2,1)S(1)} collective-permute-done((bf16[2,16,16,256]{3,2,1,0:T(8,128)(2,1)S(1)}, bf16[2,16,16,256]{3,2,1,0:T(8,128)(2,1)S(1)}, u32[]{:S(2)}, u32[]{:S(2)}) %collective-permute-start.2) | collective-permute-done | bytes 262176 | tf_op jit(solution)/shard_map/ppermute | solution.py:622
  50.7 4.8 %collective-permute-start.4 = (bf16[256,1024]{1,0:T(8,128)(2,1)}, bf16[256,1024]{1,0:T(8,128)(2,1)}, u32[]{:S(2)}, u32[]{:S(2)}) collective-permute-start(bf16[256,1024]{1,0:T(8,128)(2,1)} %get-tuple-element.20), channel_id=1, source_target_pairs={{0,11},{1,0},{2,1},{3,2},{8,3},{9,8},{10,9},{11,10},{4,15},{5,4},{... | collective-permute-start | bytes 1572872 | tf_op jit(solution)/shard_map/ppermute | solution.py:639
  55.6 3.2 %calibrate.3 = (bf16[256,1024]{1,0:T(8,128)(2,1)}, bf16[256,1024]{1,0:T(8,128)(2,1)}) custom-call(s32[2]{0:T(128)} %pad_add_fusion.refs_0_.at_ref, bf16[32,16,2048]{2,1,0:T(8,128)(2,1)} %all-to-all-done.refs_1_, bf16[2,16,2,16,256]{4,3,2,1,0:T(8,128)(2,1)} %bitcast.58), custom_call_target="tpu_custom_call" | custom-call | flops 1 | bytes 1 | tf_op jit(solution)/shard_map/calibrate/pallas_call | solution.py:189
  58.9 3.2 %collective-permute-start.13 = (bf16[256,1024]{1,0:T(8,128)(2,1)}, bf16[256,1024]{1,0:T(8,128)(2,1)}, u32[]{:S(2)}, u32[]{:S(2)}) collective-permute-start(bf16[256,1024]{1,0:T(8,128)(2,1)} %get-tuple-element.24), channel_id=1, source_target_pairs={{0,11},{1,0},{2,1},{3,2},{8,3},{9,8},{10,9},{11,10},{4,15},{5,4},{... | collective-permute-start | bytes 1572872 | tf_op jit(solution)/shard_map/ppermute | solution.py:639
  64.2 4.4 %collective-permute-done.3.part_hbm = bf16[256,1024]{1,0:T(8,128)(2,1)} collective-permute-done((bf16[256,1024]{1,0:T(8,128)(2,1)}, bf16[256,1024]{1,0:T(8,128)(2,1)}, u32[]{:S(2)}, u32[]{:S(2)}) %collective-permute-start.3) | collective-permute-done | bytes 524320 | tf_op jit(solution)/shard_map/ppermute | solution.py:638
  70.9 5.3 %collective-permute-start.5 = (bf16[256,1024]{1,0:T(8,128)(2,1)}, bf16[256,1024]{1,0:T(8,128)(2,1)}, u32[]{:S(2)}, u32[]{:S(2)}) collective-permute-start(bf16[256,1024]{1,0:T(8,128)(2,1)} %enter.9), channel_id=1, source_target_pairs={{0,11},{1,0},{2,1},{3,2},{8,3},{9,8},{10,9},{11,10},{4,15},{5,4},{... | collective-permute-start | bytes 1572872 | tf_op jit(solution)/shard_map/ppermute | solution.py:639
  76.2 3.6 %collective-permute-done.12.part_hbm = bf16[256,1024]{1,0:T(8,128)(2,1)} collective-permute-done((bf16[256,1024]{1,0:T(8,128)(2,1)}, bf16[256,1024]{1,0:T(8,128)(2,1)}, u32[]{:S(2)}, u32[]{:S(2)}) %collective-permute-start.12) | collective-permute-done | bytes 524320 | tf_op jit(solution)/shard_map/ppermute | solution.py:638
  82.0 4.1 %collective-permute-start.16 = (bf16[256,1024]{1,0:T(8,128)(2,1)}, bf16[256,1024]{1,0:T(8,128)(2,1)}, u32[]{:S(2)}, u32[]{:S(2)}) collective-permute-start(bf16[256,1024]{1,0:T(8,128)(2,1)} %enter.12), channel_id=1, source_target_pairs={{0,1},{1,2},{2,3},{3,8},{8,9},{9,10},{10,11},{11,0},{4,5},{5,6},{6... | collective-permute-start | bytes 1572872 | tf_op jit(solution)/shard_map/ppermute | solution.py:638
  87.4 9.7 %collective-permute-done.8.part_hbm = bf16[256,1024]{1,0:T(8,128)(2,1)} collective-permute-done((bf16[256,1024]{1,0:T(8,128)(2,1)}, bf16[256,1024]{1,0:T(8,128)(2,1)}, u32[]{:S(2)}, u32[]{:S(2)}) %collective-permute-start.8) | collective-permute-done | bytes 524320 | tf_op jit(solution)/shard_map/ppermute | solution.py:638
  103.7 4.6 %collective-permute-done.16.part_hbm = bf16[256,1024]{1,0:T(8,128)(2,1)} collective-permute-done((bf16[256,1024]{1,0:T(8,128)(2,1)}, bf16[256,1024]{1,0:T(8,128)(2,1)}, u32[]{:S(2)}, u32[]{:S(2)}) %collective-permute-start.16) | collective-permute-done | bytes 524320 | tf_op jit(solution)/shard_map/ppermute | solution.py:638
  114.9 4.7 %collective-permute-done.9 = bf16[256,1024]{1,0:T(8,128)(2,1)} collective-permute-done((bf16[256,1024]{1,0:T(8,128)(2,1)}, bf16[256,1024]{1,0:T(8,128)(2,1)}, u32[]{:S(2)}, u32[]{:S(2)}) %collective-permute-start.9) | collective-permute-done | bytes 524320 | tf_op jit(solution)/shard_map/ppermute | solution.py:638
  122.3 7.3 %collective-permute-done.17 = bf16[256,1024]{1,0:T(8,128)(2,1)} collective-permute-done((bf16[256,1024]{1,0:T(8,128)(2,1)}, bf16[256,1024]{1,0:T(8,128)(2,1)}, u32[]{:S(2)}, u32[]{:S(2)}) %collective-permute-start.17) | collective-permute-done | bytes 524320 | tf_op jit(solution)/shard_map/ppermute | solution.py:638
  133.4 6.6 %collective-permute-done.10 = bf16[256,1024]{1,0:T(8,128)(2,1)} collective-permute-done((bf16[256,1024]{1,0:T(8,128)(2,1)}, bf16[256,1024]{1,0:T(8,128)(2,1)}, u32[]{:S(2)}, u32[]{:S(2)}) %collective-permute-start.10) | collective-permute-done | bytes 524320 | tf_op jit(solution)/shard_map/ppermute | solution.py:639
  140.0 3.5 %outer_share.2.refs_17_ = bf16[256,1024]{1,0:T(8,128)(2,1)} custom-call(s32[2]{0:T(128)} %pad_add_fusion.refs_0_.at_ref, s32[1024,64]{1,0:T(8,128)} %copy.19.refs_1_.mask_ref, bf16[2,256,512]{2,1,0:T(8,128)(2,1)} %copy-done.4, bf16[2,256,512]{2,1,0:T(8,128)(2,1)} %collective-permute-done.6.refs_3_, bf16[2,1024,512]{2,1,0:T(8,128)(2,1)} %bitcast.39, ...), custom_call_target="tpu_custom_call" | custom-call | flops 1 | bytes 1 | tf_op jit(solution)/shard_map/outer_share/pallas_call | solution.py:344
  143.6 9.7 %collective-permute-start.21 = (bf16[256,1024]{1,0:T(8,128)(2,1)}, bf16[256,1024]{1,0:T(8,128)(2,1)}, u32[]{:S(2)}, u32[]{:S(2)}) collective-permute-start(bf16[256,1024]{1,0:T(8,128)(2,1)} %outer_share.2.refs_17_), channel_id=1, source_target_pairs={{1,0},{9,8},{5,4},{13,12},{17,16},{25,24},{21,20},{29,28},{33,32},... | collective-permute-start | bytes 1572872 | tf_op jit(solution)/shard_map/ppermute | solution.py:656
  156.3 6.3 %collective-permute-done.21.refs_22_.end_ref.share_a = bf16[256,1024]{1,0:T(8,128)(2,1)} collective-permute-done((bf16[256,1024]{1,0:T(8,128)(2,1)}, bf16[256,1024]{1,0:T(8,128)(2,1)}, u32[]{:S(2)}, u32[]{:S(2)}) %collective-permute-start.21) | collective-permute-done | bytes 524320 | tf_op jit(solution)/shard_map/ppermute | solution.py:656
  164.0 6.5 %collective-permute-start.23 = (bf16[2,256,512]{2,1,0:T(8,128)(2,1)}, bf16[2,256,512]{2,1,0:T(8,128)(2,1)}, u32[]{:S(2)}, u32[]{:S(2)}) collective-permute-start(bf16[2,256,512]{2,1,0:T(8,128)(2,1)} %get-tuple-element.28), channel_id=1, source_target_pairs={{0,2},{8,10},{4,6},{12,14},{16,18},{24,26},{20,22},{28,30},{32,34}... | collective-permute-start | bytes 1572872 | tf_op jit(solution)/shard_map/ppermute | solution.py:663
  174.5 11.5 %pairs.1 = (bf16[2,512,2048]{2,1,0:T(8,128)(2,1)}, bf16[4,16,2,16,1024]{4,3,2,1,0:T(8,128)(2,1)}, bf16[4,16,2,16,1024]{4,3,2,1,0:T(8,128)(2,1)}) custom-call(s32[2]{0:T(128)} %pad_add_fusion.refs_0_.at_ref, bf16[16,16,1024]{2,1,0:T(8,128)(2,1)} %bitcast.45, bf16[16,16,1024]{2,1,0:T(8,128)(2,1)} %bitcast.48, ...), custom_call_target="tpu_custom_call" | custom-call | flops 1 | bytes 1 | tf_op jit(solution)/shard_map/pairs/pallas_call | solution.py:468
  186.1 10.4 %beams.1.formed_ref = f32[256,2048]{1,0:T(8,128)} custom-call(s32[2]{0:T(128)} %pad_add_fusion.refs_0_.at_ref, s32[1024,64]{1,0:T(8,128)} %copy.19.refs_1_.mask_ref, bf16[2,1024,512]{2,1,0:T(8,128)(2,1)} %bitcast.41, bf16[2,256,512]{2,1,0:T(8,128)(2,1)} %collective-permute-done.22.near_ref, bf16[2,256,512]{2,1,0:T(8,128)(2,1)} %collective-permute-done.23.far_ref, ...), custom_call_target="tpu_custom_call" | custom-call | flops 1 | bytes 1 | tf_op jit(solution)/shard_map/beams/pallas_call | solution.py:552
  199.7 3.9 %finish.1 = bf16[512,4,256]{2,1,0:T(4,128)(2,1)} custom-call(s32[2]{0:T(128)} %pad_add_fusion.refs_0_.at_ref, f32[256,2048]{1,0:T(8,128)} %beams.1.formed_ref, bf16[256,1024]{1,0:T(8,128)(2,1)} %collective-permute-done.21.refs_22_.end_ref.share_a, bf16[256,1024]{1,0:T(8,128)(2,1)} %collective-permute-done.24.share_b, bf16[2,512,2048]{2,1,0:T(8,128)(2,1)} %last_pairs.1.refs_0_), custom_call_target="tpu_custom_call" | custom-call | flops 1 | bytes 1 | tf_op jit(solution)/shard_map/finish/pallas_call | solution.py:594
  (62 shorter events, 47.0 us)
Async XLA Ops:
  8.8 38.6 %all-to-all-start = ((bf16[32,16,2048]{2,1,0:T(8,128)(2,1)}), bf16[32,16,2048]{2,1,0:T(8,128)(2,1)}, u32[]{:S(2)}, u32[]{:S(2)}) async-start(bf16[32,16,2048]{2,1,0:T(8,128)(2,1)} %channelize.1), calls=%async_computation | async-start | bytes 4194304 | tf_op jit(solution)/shard_map/all_to_all | solution.py:631
  17.7 28.9 %collective-permute-start = (bf16[2,256,512]{2,1,0:T(8,128)(2,1)}, bf16[2,256,512]{2,1,0:T(8,128)(2,1)S(1)}, u32[]{:S(2)}, u32[]{:S(2)}) collective-permute-start(bf16[2,256,512]{2,1,0:T(8,128)(2,1)} %get-tuple-element.35), channel_id=1, source_target_pairs={{1,2},{9,10},{5,6},{13,14},{17,18},{25,26},{21,22},{29,30},{33,34}... | collective-permute-start | bytes 1572872 | tf_op jit(solution)/shard_map/ppermute | solution.py:627
  25.0 21.6 %collective-permute-start.2 = (bf16[2,16,16,256]{3,2,1,0:T(8,128)(2,1)S(1)}, bf16[2,16,16,256]{3,2,1,0:T(8,128)(2,1)S(1)}, u32[]{:S(2)}, u32[]{:S(2)}) collective-permute-start(bf16[2,16,16,256]{3,2,1,0:T(8,128)(2,1)S(1)} %dynamic-slice_bitcast_fusion.2), channel_id=1, source_target_pairs={{2,0},{10,8},{6,4},{14,12},{18,16},{26,24},{22,20},{30,28},{34,32}... | collective-permute-start | bytes 786440 | tf_op jit(solution)/shard_map/ppermute | solution.py:622
  50.6 18.0 %collective-permute-start.3 = (bf16[256,1024]{1,0:T(8,128)(2,1)}, bf16[256,1024]{1,0:T(8,128)(2,1)}, u32[]{:S(2)}, u32[]{:S(2)}) collective-permute-start(bf16[256,1024]{1,0:T(8,128)(2,1)} %get-tuple-element.18), channel_id=1, source_target_pairs={{0,1},{1,2},{2,3},{3,8},{8,9},{9,10},{10,11},{11,0},{4,5},{5,6},{6... | collective-permute-start | bytes 1572872 | tf_op jit(solution)/shard_map/ppermute | solution.py:638
  50.7 20.1 %collective-permute-start.4 = (bf16[256,1024]{1,0:T(8,128)(2,1)}, bf16[256,1024]{1,0:T(8,128)(2,1)}, u32[]{:S(2)}, u32[]{:S(2)}) collective-permute-start(bf16[256,1024]{1,0:T(8,128)(2,1)} %get-tuple-element.20), channel_id=1, source_target_pairs={{0,11},{1,0},{2,1},{3,2},{8,3},{9,8},{10,9},{11,10},{4,15},{5,4},{... | collective-permute-start | bytes 1572872 | tf_op jit(solution)/shard_map/ppermute | solution.py:639
  58.8 21.0 %collective-permute-start.12 = (bf16[256,1024]{1,0:T(8,128)(2,1)}, bf16[256,1024]{1,0:T(8,128)(2,1)}, u32[]{:S(2)}, u32[]{:S(2)}) collective-permute-start(bf16[256,1024]{1,0:T(8,128)(2,1)} %get-tuple-element.23), channel_id=1, source_target_pairs={{0,1},{1,2},{2,3},{3,8},{8,9},{9,10},{10,11},{11,0},{4,5},{5,6},{6... | collective-permute-start | bytes 1572872 | tf_op jit(solution)/shard_map/ppermute | solution.py:638
  58.9 27.1 %collective-permute-start.13 = (bf16[256,1024]{1,0:T(8,128)(2,1)}, bf16[256,1024]{1,0:T(8,128)(2,1)}, u32[]{:S(2)}, u32[]{:S(2)}) collective-permute-start(bf16[256,1024]{1,0:T(8,128)(2,1)} %get-tuple-element.24), channel_id=1, source_target_pairs={{0,11},{1,0},{2,1},{3,2},{8,3},{9,8},{10,9},{11,10},{4,15},{5,4},{... | collective-permute-start | bytes 1572872 | tf_op jit(solution)/shard_map/ppermute | solution.py:639
  62.1 25.3 %collective-permute-start.6 = (bf16[2,256,512]{2,1,0:T(8,128)(2,1)}, bf16[2,256,512]{2,1,0:T(8,128)(2,1)}, u32[]{:S(2)}, u32[]{:S(2)}) collective-permute-start(bf16[2,256,512]{2,1,0:T(8,128)(2,1)} %get-tuple-element.35), channel_id=1, source_target_pairs={{0,2},{8,10},{4,6},{12,14},{16,18},{24,26},{20,22},{28,30},{32,34}... | collective-permute-start | bytes 1572872 | tf_op jit(solution)/shard_map/ppermute | solution.py:628
  70.7 26.4 %collective-permute-start.8 = (bf16[256,1024]{1,0:T(8,128)(2,1)}, bf16[256,1024]{1,0:T(8,128)(2,1)}, u32[]{:S(2)}, u32[]{:S(2)}) collective-permute-start(bf16[256,1024]{1,0:T(8,128)(2,1)} %enter.8), channel_id=1, source_target_pairs={{0,1},{1,2},{2,3},{3,8},{8,9},{9,10},{10,11},{11,0},{4,5},{5,6},{6... | collective-permute-start | bytes 1572872 | tf_op jit(solution)/shard_map/ppermute | solution.py:638
  70.9 31.5 %collective-permute-start.5 = (bf16[256,1024]{1,0:T(8,128)(2,1)}, bf16[256,1024]{1,0:T(8,128)(2,1)}, u32[]{:S(2)}, u32[]{:S(2)}) collective-permute-start(bf16[256,1024]{1,0:T(8,128)(2,1)} %enter.9), channel_id=1, source_target_pairs={{0,11},{1,0},{2,1},{3,2},{8,3},{9,8},{10,9},{11,10},{4,15},{5,4},{... | collective-permute-start | bytes 1572872 | tf_op jit(solution)/shard_map/ppermute | solution.py:639
  82.0 26.4 %collective-permute-start.16 = (bf16[256,1024]{1,0:T(8,128)(2,1)}, bf16[256,1024]{1,0:T(8,128)(2,1)}, u32[]{:S(2)}, u32[]{:S(2)}) collective-permute-start(bf16[256,1024]{1,0:T(8,128)(2,1)} %enter.12), channel_id=1, source_target_pairs={{0,1},{1,2},{2,3},{3,8},{8,9},{9,10},{10,11},{11,0},{4,5},{5,6},{6... | collective-permute-start | bytes 1572872 | tf_op jit(solution)/shard_map/ppermute | solution.py:638
  86.0 27.5 %collective-permute-start.14 = (bf16[256,1024]{1,0:T(8,128)(2,1)}, bf16[256,1024]{1,0:T(8,128)(2,1)}, u32[]{:S(2)}, u32[]{:S(2)}) collective-permute-start(bf16[256,1024]{1,0:T(8,128)(2,1)} %enter.13), channel_id=1, source_target_pairs={{0,11},{1,0},{2,1},{3,2},{8,3},{9,8},{10,9},{11,10},{4,15},{5,4},{... | collective-permute-start | bytes 1572872 | tf_op jit(solution)/shard_map/ppermute | solution.py:639
  99.2 20.3 %collective-permute-start.9 = (bf16[256,1024]{1,0:T(8,128)(2,1)}, bf16[256,1024]{1,0:T(8,128)(2,1)}, u32[]{:S(2)}, u32[]{:S(2)}) collective-permute-start(bf16[256,1024]{1,0:T(8,128)(2,1)} %enter.11), channel_id=1, source_target_pairs={{0,1},{1,2},{2,3},{8,9},{9,10},{10,11},{4,5},{5,6},{6,7},{12,13},{... | collective-permute-start | bytes 1572872 | tf_op jit(solution)/shard_map/ppermute | solution.py:638
  102.4 18.6 %collective-permute-start.7 = (bf16[256,1024]{1,0:T(8,128)(2,1)}, bf16[256,1024]{1,0:T(8,128)(2,1)}, u32[]{:S(2)}, u32[]{:S(2)}) collective-permute-start(bf16[256,1024]{1,0:T(8,128)(2,1)} %enter.10), channel_id=1, source_target_pairs={{1,0},{2,1},{3,2},{9,8},{10,9},{11,10},{5,4},{6,5},{7,6},{13,12},{... | collective-permute-start | bytes 1572872 | tf_op jit(solution)/shard_map/ppermute | solution.py:639
  110.5 19.2 %collective-permute-start.17 = (bf16[256,1024]{1,0:T(8,128)(2,1)}, bf16[256,1024]{1,0:T(8,128)(2,1)}, u32[]{:S(2)}, u32[]{:S(2)}) collective-permute-start(bf16[256,1024]{1,0:T(8,128)(2,1)} %enter.15), channel_id=1, source_target_pairs={{0,1},{1,2},{2,3},{8,9},{9,10},{10,11},{4,5},{5,6},{6,7},{12,13},{... | collective-permute-start | bytes 1572872 | tf_op jit(solution)/shard_map/ppermute | solution.py:638
  113.6 17.5 %collective-permute-start.15 = (bf16[256,1024]{1,0:T(8,128)(2,1)}, bf16[256,1024]{1,0:T(8,128)(2,1)}, u32[]{:S(2)}, u32[]{:S(2)}) collective-permute-start(bf16[256,1024]{1,0:T(8,128)(2,1)} %enter.14), channel_id=1, source_target_pairs={{1,0},{2,1},{3,2},{9,8},{10,9},{11,10},{5,4},{6,5},{7,6},{13,12},{... | collective-permute-start | bytes 1572872 | tf_op jit(solution)/shard_map/ppermute | solution.py:639
  121.0 19.0 %collective-permute-start.10 = (bf16[256,1024]{1,0:T(8,128)(2,1)}, bf16[256,1024]{1,0:T(8,128)(2,1)}, u32[]{:S(2)}, u32[]{:S(2)}) collective-permute-start(bf16[256,1024]{1,0:T(8,128)(2,1)} %collective-permute-done.7), channel_id=1, source_target_pairs={{1,0},{2,1},{9,8},{10,9},{5,4},{6,5},{13,12},{14,13},{17,16},{18,1... | collective-permute-start | bytes 1572872 | tf_op jit(solution)/shard_map/ppermute | solution.py:639
  129.7 23.6 %collective-permute-start.19 = (bf16[256,1024]{1,0:T(8,128)(2,1)}, bf16[256,1024]{1,0:T(8,128)(2,1)}, u32[]{:S(2)}, u32[]{:S(2)}) collective-permute-start(bf16[256,1024]{1,0:T(8,128)(2,1)} %collective-permute-done.17), channel_id=1, source_target_pairs={{1,2},{2,3},{9,10},{10,11},{5,6},{6,7},{13,14},{14,15},{17,18},{18... | collective-permute-start | bytes 1572872 | tf_op jit(solution)/shard_map/ppermute | solution.py:638
  131.1 22.2 %collective-permute-start.18 = (bf16[256,1024]{1,0:T(8,128)(2,1)}, bf16[256,1024]{1,0:T(8,128)(2,1)}, u32[]{:S(2)}, u32[]{:S(2)}) collective-permute-start(bf16[256,1024]{1,0:T(8,128)(2,1)} %collective-permute-done.15), channel_id=1, source_target_pairs={{1,0},{2,1},{9,8},{10,9},{5,4},{6,5},{13,12},{14,13},{17,16},{18,1... | collective-permute-start | bytes 1572872 | tf_op jit(solution)/shard_map/ppermute | solution.py:639
  143.6 19.0 %collective-permute-start.21 = (bf16[256,1024]{1,0:T(8,128)(2,1)}, bf16[256,1024]{1,0:T(8,128)(2,1)}, u32[]{:S(2)}, u32[]{:S(2)}) collective-permute-start(bf16[256,1024]{1,0:T(8,128)(2,1)} %outer_share.2.refs_17_), channel_id=1, source_target_pairs={{1,0},{9,8},{5,4},{13,12},{17,16},{25,24},{21,20},{29,28},{33,32},... | collective-permute-start | bytes 1572872 | tf_op jit(solution)/shard_map/ppermute | solution.py:656
  155.0 41.4 %collective-permute-start.20 = (bf16[2,512,512]{2,1,0:T(8,128)(2,1)}, bf16[2,512,512]{2,1,0:T(8,128)(2,1)}, u32[]{:S(2)}, u32[]{:S(2)}) collective-permute-start(bf16[2,512,512]{2,1,0:T(8,128)(2,1)} %edge.1.refs_21_), channel_id=1, source_target_pairs={{1,0},{9,8},{5,4},{13,12},{17,16},{25,24},{21,20},{29,28},{33,32},... | collective-permute-start | bytes 3145736 | tf_op jit(solution)/shard_map/ppermute | solution.py:654
  162.6 23.5 %collective-permute-start.22 = (bf16[2,256,512]{2,1,0:T(8,128)(2,1)}, bf16[2,256,512]{2,1,0:T(8,128)(2,1)}, u32[]{:S(2)}, u32[]{:S(2)}) collective-permute-start(bf16[2,256,512]{2,1,0:T(8,128)(2,1)} %get-tuple-element.28), channel_id=1, source_target_pairs={{1,2},{9,10},{5,6},{13,14},{17,18},{25,26},{21,22},{29,30},{33,34}... | collective-permute-start | bytes 1572872 | tf_op jit(solution)/shard_map/ppermute | solution.py:662
  164.0 22.0 %collective-permute-start.23 = (bf16[2,256,512]{2,1,0:T(8,128)(2,1)}, bf16[2,256,512]{2,1,0:T(8,128)(2,1)}, u32[]{:S(2)}, u32[]{:S(2)}) collective-permute-start(bf16[2,256,512]{2,1,0:T(8,128)(2,1)} %get-tuple-element.28), channel_id=1, source_target_pairs={{0,2},{8,10},{4,6},{12,14},{16,18},{24,26},{20,22},{28,30},{32,34}... | collective-permute-start | bytes 1572872 | tf_op jit(solution)/shard_map/ppermute | solution.py:663
  173.0 26.7 %collective-permute-start.24 = (bf16[256,1024]{1,0:T(8,128)(2,1)}, bf16[256,1024]{1,0:T(8,128)(2,1)}, u32[]{:S(2)}, u32[]{:S(2)}) collective-permute-start(bf16[256,1024]{1,0:T(8,128)(2,1)} %outer_share.3), channel_id=1, source_target_pairs={{1,0},{9,8},{5,4},{13,12},{17,16},{25,24},{21,20},{29,28},{33,32},... | collective-permute-start | bytes 1572872 | tf_op jit(solution)/shard_map/ppermute | solution.py:657
  (8 other events, 140.7 us)
